TPU v7x, 32 devices: a whole 2x2x4 slice. The times are simulated.
32 devices in a mesh: groups: 2 (over x), node: 8 (over z, y), outer: 2 (over core).
Axes of the slice: x: 2, y: 2, z: 4, core: 2. Of those that a mesh axis runs over, the one named last changes fastest.
Arguments:
- tokens: bfloat16 [16384, 8192], P(('groups', 'node', 'outer')), parts along dimension 0, may hold values from -6 to 6
- frozen_weight: bfloat16 [8192, 1024], P(('node', 'outer')), may hold values from -0.0625 to 0.0625
- down_adapter: bfloat16 [8192, 128], replicated, may hold values from -0.0625 to 0.0625
- second_adapter_weight: bfloat16 [1024, 128], replicated, may hold values from -0.75 to 0.75
- tenant_ids: int32 [128], P(('groups', 'node', 'outer')), parts along dimension 0, may hold values from 0 to 7
- block_counts: int32 [32], P(('groups', 'node', 'outer')), parts along dimension 0, may hold values from 1 to 4, as said below
- positions: int32 [16384], P(('groups', 'node', 'outer')), parts along dimension 0, may hold values from 0 to 4095, as said below
- cotangent: bfloat16 [16384, 1024], P(('groups', 'node', 'outer')), parts along dimension 0, may hold values from -6 to 6
Outputs:
- keys: bfloat16 [16384, 1024], P(('groups', 'node', 'outer')), parts along dimension 0
- down_adapter_gradient: float32 [16384, 128], P(('groups', 'node')), parts along dimension 0
- up_adapter_gradient: float32 [2048, 128], P(('groups', 'node')), parts along dimension 0
There are 2 independent parts, one for each index of `groups`. A program takes and returns all parts, laid end to end along the dimension named above; an argument that names none is the same for every part. Nothing has to cross between parts.
Inputs may be any that keep to these rules, and one draw needn't show every extreme that they name: `block_counts`: each device's live blocks come first among its 4 blocks; some device has all live. Each block of 128 tokens holds consecutive positions starting at a multiple of 128.
All inputs are finite; a program needn't handle non-finite values.
Results may differ from a plain program's by a relative error of at most 0.0051.
Values may be sent and summed in bfloat16 or wider, within the bound.
No kernel may reach another device: no remote copies, remote signals or barrier semaphores. Data moves between devices by JAX's collectives and lax.ppermute only.
A program may use at most 128 MiB of HBM per device.

v0:
```python
import jax
import jax.numpy as jnp
from jax import lax
from jax.sharding import PartitionSpec as P

HEAD = 128
R = 16


ROPE_BASE = 500000.0
ADAPTER_SCALE = 2.0


def rope_tables(positions):
    half_head = HEAD // 2
    frequency = ROPE_BASE ** (-2.0 * jnp.arange(half_head, dtype=jnp.float32) / HEAD)
    angle = positions.astype(jnp.float32)[:, None] * frequency[None, :]
    return (jnp.cos(angle), jnp.sin(angle))


def rotate(field, cosine, sine, orient):
    rows = field.shape[0]
    shaped = field.reshape(rows, -1, 2, HEAD // 2)
    first = shaped[:, :, 0]
    second = shaped[:, :, 1]
    cos_b = cosine[:, None, :]
    sin_b = orient * sine[:, None, :]
    out_first = first * cos_b - second * sin_b
    out_second = second * cos_b + first * sin_b
    return jnp.stack((out_first, out_second), axis=2).reshape(rows, -1)


def body(
    tokens,
    frozen_weight,
    down_adapter,
    second_adapter_weight,
    tenant_ids,
    block_counts,
    positions,
    cotangent,
):
    token_rows = tokens.shape[0]
    block_total = tenant_ids.shape[0]
    block_rows = token_rows // block_total
    width_cols = down_adapter.shape[1]
    live_blocks = (jnp.arange(block_total, dtype=jnp.int32) < block_counts[0]).astype(jnp.float32)
    live_rows = jnp.repeat(live_blocks, block_rows)[:, None]
    column_tenant = jnp.arange(width_cols, dtype=jnp.int32) // R
    select_blocks = (tenant_ids[:, None] == column_tenant[None, :]).astype(
        jnp.float32
    ) * live_blocks[:, None]
    select = jnp.repeat(select_blocks, block_rows, axis=0)
    lowrank_hidden = (
        jnp.dot(tokens, down_adapter, preferred_element_type=jnp.float32) * select
    ).astype(jnp.bfloat16)
    frozen_output = jnp.dot(
        tokens,
        lax.all_gather(frozen_weight, ("node", "outer"), axis=0, tiled=True),
        preferred_element_type=jnp.float32,
    )
    adapter_output = lax.dot_general(
        lowrank_hidden,
        second_adapter_weight,
        (((1,), (1,)), ((), ())),
        preferred_element_type=jnp.float32,
    )
    unrotated_keys = frozen_output + ADAPTER_SCALE * adapter_output
    cosine, sine = rope_tables(positions)
    keys = (live_rows * rotate(unrotated_keys, cosine, sine, 1.0)).astype(jnp.bfloat16)
    output_gradient = (
        live_rows * rotate(cotangent.astype(jnp.float32), cosine, sine, -1.0)
    ).astype(jnp.bfloat16)
    backward_gradient = (
        jnp.dot(output_gradient, second_adapter_weight, preferred_element_type=jnp.float32) * select
    ).astype(jnp.bfloat16)
    down_product = ADAPTER_SCALE * lax.dot_general(
        tokens, backward_gradient, (((0,), (0,)), ((), ())), preferred_element_type=jnp.float32
    )
    up_product = ADAPTER_SCALE * lax.dot_general(
        output_gradient,
        lowrank_hidden,
        (((0,), (0,)), ((), ())),
        preferred_element_type=jnp.float32,
    )
    shares = (
        lax.psum_scatter(down_product, "node", scatter_dimension=0, tiled=True),
        lax.psum_scatter(up_product, "node", scatter_dimension=0, tiled=True),
    )
    down_adapter_gradient, up_adapter_gradient = lax.psum((shares[0], shares[1]), "outer")
    return (keys, down_adapter_gradient, up_adapter_gradient)


def solution(mesh):
    placed = (
        P(("groups", "node", "outer"), None),
        P(("node", "outer"), None),
        P(),
        P(),
        P(("groups", "node", "outer")),
        P(("groups", "node", "outer")),
        P(("groups", "node", "outer")),
        P(("groups", "node", "outer"), None),
    )
    return jax.shard_map(
        body,
        mesh=mesh,
        in_specs=placed,
        out_specs=(
            P(("groups", "node", "outer"), None),
            P(("groups", "node"), None),
            P(("groups", "node"), None),
        ),
        check_vma=False,
    )
```

profile of v0, /device:TPU:0, one launch (start us, length us, event | category | flops | bytes accessed | tf_op | source)
XLA Modules:
  0.0 348.2 jit_solution(1092644011541346058)
XLA Ops:
  7.2 0.0 copy-start
  7.2 0.0 all-gather.2.cloned.1.call-start
  7.2 0.7 all-gather.2.cloned.1.call-update
  7.9 0.0 reduce-scatter.5.cloned.1.call-start
  8.6 0.7 convert_element_type.26
  9.3 1.5 copy.13
  10.8 0.0 copy-start.4
  10.8 1.6 convert.1
  12.5 0.1 broadcast_bitcast_fusion
  12.5 0.5 broadcast_multiply_fusion
  13.1 0.0 copy-start.2
  13.1 5.8 %fusion.3 = bf16[512,128]{1,0:T(8,128)(2,1)S(1)} fusion(f32[512,128]{1,0:T(8,128)S(1)} %bitcast.31, bf16[512,8192]{1,0:T(8,128)(2,1)} %param.8, bf16[8192,128]{1,0:T(8,128)(2,1)S(1)} %copy-done), kind=kOutput, calls=%fused_computation.12 | convolution fusion | flops 1073872896 | bytes 10878976 | tf_op jit(solution)/shard_map/dot_general | solution.py:55
  19.0 1.8 fusion.5
  20.7 119.1 %all-gather.2.cloned.1.call-done = bf16[8192,1024]{1,0:T(8,128)(2,1)} async-done(((bf16[512,1024]{1,0:T(8,128)(2,1)}), bf16[8192,1024]{1,0:T(8,128)(2,1)}) %all-gather.2.cloned.1.call-update) | async-done | bytes 16777232 | tf_op jit(solution)/shard_map/all_gather | solution.py:59
  139.8 16.1 %multiply_add_fusion = f32[512,1024]{1,0:T(8,128)} fusion(f32[512,1024]{1,0:T(8,128)} %fusion.5, bf16[512,8192]{1,0:T(8,128)(2,1)} %param.8, bf16[8192,1024]{1,0:T(8,128)(2,1)} %all-gather.2.cloned.1.call-done), kind=kOutput, calls=%fused_computation.8 | convolution fusion | flops 8590983168 | bytes 29360128 | tf_op jit(solution)/shard_map/dot_general | solution.py:57
  155.9 2.9 copy.12
  158.8 3.1 multiply_subtract_fusion
  161.9 0.7 pad_maximum_fusion
  162.6 1.5 fusion.1
  164.1 1.2 convolution_multiply_fusion.1
  165.4 0.0 reduce-scatter.5.cloned.1.call-update
  165.4 0.0 reduce-scatter.3.cloned.1.call-start
  165.4 7.7 %fusion = f32[8192,128]{0,1:T(8,128)} fusion(bf16[512,8192]{1,0:T(8,128)(2,1)} %param.8, f32[512,128]{1,0:T(8,128)} %bitcast.32, bf16[512,1024]{0,1:T(8,128)(2,1)S(1)} %get-tuple-element.20, bf16[1024,128]{1,0:T(8,128)(2,1)S(1)} %copy-done.2), kind=kOutput, calls=%fused_computation.1 | convolution fusion | flops 1209139200 | bytes 14155776 | tf_op jit(solution)/shard_map/dot_general | solution.py:77
  173.1 0.0 reduce-scatter.3.cloned.1.call-update
  173.1 0.0 all-reduce.3.cloned.1.call-start
  173.2 52.4 %reduce-scatter.5.cloned.1.call-done = f32[128,128]{1,0:T(8,128)} async-done(((f32[1024,128]{1,0:T(8,128)}), f32[128,128]{1,0:T(8,128)}) %reduce-scatter.5.cloned.1.call-update) | async-done | bytes 65552 | tf_op jit(solution)/shard_map/reduce_scatter | solution.py:88
  225.6 91.6 %reduce-scatter.3.cloned.1.call-done = f32[1024,128]{0,1:T(8,128)} async-done(((f32[8192,128]{0,1:T(8,128)}), f32[1024,128]{0,1:T(8,128)}) %reduce-scatter.3.cloned.1.call-update) | async-done | bytes 524304 | tf_op jit(solution)/shard_map/reduce_scatter | solution.py:87
  317.2 0.0 all-reduce.3.cloned.1.call-update
  317.2 1.3 copy.14
  318.5 19.6 %all-reduce.3.cloned.1.call-done = (f32[1024,128]{0,1:T(8,128)}, f32[128,128]{1,0:T(8,128)}) async-done(((f32[1024,128]{0,1:T(8,128)}, f32[128,128]{1,0:T(8,128)}), (f32[1024,128]{0,1:T(8,128)}, f32[128,128]{1,0:T(8,128)})) %all-reduce.3.cloned.1.call-update) | async-done | bytes 589840 | tf_op jit(solution)/shard_map/psum | solution.py:90
  338.1 2.0 copy.15
  340.2 1.5 copy.19
  (11 shorter events, 0.0 us)
Async XLA Ops:
  7.2 5.9 %copy-start = (bf16[8192,128]{1,0:T(8,128)(2,1)S(1)}, bf16[8192,128]{1,0:T(8,128)(2,1)}, u32[]{:S(2)}) copy-start(bf16[8192,128]{1,0:T(8,128)(2,1)} %param.10) | copy-start | bytes 6291460
  7.2 132.6 %all-gather.2.cloned.1.call-start = ((), (), s32[]{:S(2)}) async-start(), calls=%async_computation.2 | async-start | bytes 17825792 | tf_op jit(solution)/shard_map/all_gather | solution.py:59
  7.9 217.7 %reduce-scatter.5.cloned.1.call-start = ((), (), s32[]{:S(2)}) async-start(), calls=%async_computation.4 | async-start | bytes 589824 | tf_op jit(solution)/shard_map/reduce_scatter | solution.py:88
  10.8 1.7 copy-start.4
  13.1 5.8 %copy-start.3 = (f32[4,128,128]{2,1,0:T(8,128)}, f32[4,128,128]{2,1,0:T(8,128)S(1)}, u32[]{:S(2)}) copy-start(f32[4,128,128]{2,1,0:T(8,128)S(1)} %broadcast_in_dim.5) | copy-start | bytes 786436
  13.1 5.8 %copy-start.2 = (bf16[1024,128]{1,0:T(8,128)(2,1)S(1)}, bf16[1024,128]{1,0:T(8,128)(2,1)}, u32[]{:S(2)}) copy-start(bf16[1024,128]{1,0:T(8,128)(2,1)} %param.11) | copy-start | bytes 786436
  165.4 151.8 %reduce-scatter.3.cloned.1.call-start = ((), (), s32[]{:S(2)}) async-start(), calls=%async_computation.3 | async-start | bytes 4718592 | tf_op jit(solution)/shard_map/reduce_scatter | solution.py:87
  173.1 144.1 %copy-start.1 = (bf16[512,1024]{0,1:T(8,128)(2,1)S(1)}, bf16[512,1024]{0,1:T(8,128)(2,1)}, u32[]{:S(2)}) copy-start(bf16[512,1024]{0,1:T(8,128)(2,1)} %get-tuple-element.21) | copy-start | bytes 3145732
  173.1 165.0 %all-reduce.3.cloned.1.call-start = ((), (), s32[]{:S(2)}) async-start(), calls=%async_computation.5 | async-start | bytes 1179648 | tf_op jit(solution)/shard_map/psum | solution.py:90
Sparse Core Ops, SparseCore 0:
  10.2 129.5 all-gather.1
  165.5 60.0 reduce-scatter.4
  229.7 87.4 reduce-scatter.2
  319.4 18.6 all-reduce.2
where the time goes:
time: 348 us
  waiting for transfers between devices  283 us (81%)
  matrix products  32.5 us (9%)
  between operations  14.5 us (4%)
  local copies, waits for them, and re-layouts  9.27 us (3%)
  other arithmetic  8.23 us (2%)
    all_gather x1, waiting for transfers between devices, body(): lax.all_gather(frozen_weight, ('node', 'outer'), axis=0, tiled=True)  119 us
    reduce_scatter x1, waiting for transfers between devices, body(): lax.psum_scatter(down_product, 'node', scatter_dimension=0, tiled=True)  91.6 us
    reduce_scatter x1, waiting for transfers between devices, body(): lax.psum_scatter(up_product, 'node', scatter_dimension=0, tiled=True)  52.4 us
    psum x1, waiting for transfers between devices, body(): lax.psum((shares[0], shares[1]), 'outer')  19.6 us
    dot_general x1, matrix products, body(): jnp.dot(tokens, lax.all_gather(frozen_weight, ('node', 'outer'), axis=0,...  16.1 us
    dot_general x1, matrix products, body(): lax.dot_general(tokens, backward_gradient, (((0,), (0,)), ((), ())), pref...  7.65 us
  transfers between devices with their start and end apart: 4, of which 4 were waited for; matrix products, arithmetic and copies ran while one was open for 6% of the time, Pallas kernels for 0%

commit v1 on v0

--- a/solution.py
+++ b/solution.py
@@ -1,14 +1,463 @@
+import functools
+
 import jax
 import jax.numpy as jnp
+import numpy as np
 from jax import lax
+from jax.experimental import pallas as pl
+from jax.experimental.pallas import tpu as pltpu
 from jax.sharding import PartitionSpec as P
 
 HEAD = 128
 R = 16
-
-
+BLK = 128
+SEQ = 4096
 ROPE_BASE = 500000.0
 ADAPTER_SCALE = 2.0
+ALL = ("groups", "node", "outer")
+ANY = pl.BlockSpec(memory_space=pl.ANY)
+VMEM_LIMIT = 48 * 1024 * 1024
+
+
+def rope_constants():
+    half = HEAD // 2
+    frequency = ROPE_BASE ** (-2.0 * np.arange(half) / HEAD)
+    inside = np.arange(BLK)[:, None] * frequency[None, :]
+    starts = BLK * np.arange(SEQ // BLK)[:, None] * frequency[None, :]
+    both = lambda t: np.concatenate((t, t), axis=1)
+    return np.concatenate(
+        (both(np.cos(inside)), both(np.sin(inside)), both(np.cos(starts)), both(np.sin(starts)))
+    ).astype(np.float32)
+
+
+def block_tables(tab_ref, c_row, s_row):
+    c_in = tab_ref[0:BLK, :]
+    s_in = tab_ref[BLK : 2 * BLK, :]
+    cosine = c_in * c_row - s_in * s_row
+    sine = s_in * c_row + c_in * s_row
+    lane = lax.broadcasted_iota(jnp.int32, (1, HEAD), 1)
+    return cosine, jnp.where(lane < HEAD // 2, -sine, sine)
+
+
+def gradient_kernel(
+    sc, tids, count, pos, tok_ref, a_ref, b_ref, cot_ref, tab_ref,
+    low_ref, own_ref, sib_ref, grad, back, acc, piece,
+):
+    step = pl.program_id(0)
+    slots = pl.num_programs(0)
+    chunk = tok_ref.shape[1]
+    kv = cot_ref.shape[1]
+    blocks = tok_ref.shape[0] // BLK
+    up_rows = kv // slots
+    down_half, up_half = chunk // 2, up_rows // 2
+    outer = sc[8]
+    lane = lax.broadcasted_iota(jnp.int32, (1, HEAD), 1)
+
+    def select(b):
+        hit = jnp.logical_and(lane // R == tids[b], b < count[0])
+        return jnp.where(hit, 1.0, 0.0).astype(jnp.float32)
+
+    @pl.when(step == 0)
+    def _():
+        acc[...] = jnp.zeros_like(acc)
+        for b in range(blocks):
+            rows = slice(b * BLK, (b + 1) * BLK)
+            start = pos[b * BLK] // BLK
+            cosine, sine = block_tables(
+                tab_ref,
+                tab_ref[pl.ds(2 * BLK + start, 1), :],
+                tab_ref[pl.ds(2 * BLK + SEQ // BLK + start, 1), :],
+            )
+            live = jnp.where(b < count[0], 1.0, 0.0).astype(jnp.float32)
+            for h in range(kv // HEAD):
+                cols = slice(h * HEAD, (h + 1) * HEAD)
+                x = cot_ref[rows, cols].astype(jnp.float32)
+                g = x * cosine - pltpu.roll(x, HEAD // 2, 1) * sine
+                grad[rows, cols] = (live * g).astype(jnp.bfloat16)
+            back[rows, :] = (
+                jnp.dot(grad[rows, :], b_ref[...], preferred_element_type=jnp.float32) * select(b)
+            ).astype(jnp.bfloat16)
+
+    tok = tok_ref[...]
+    acc[...] += jnp.dot(tok, a_ref[...], preferred_element_type=jnp.float32)
+    piece[...] = ADAPTER_SCALE * lax.dot_general(
+        tok, back[...], (((0,), (0,)), ((), ())), preferred_element_type=jnp.float32
+    )
+    own_ref[step, 0:down_half, :] = piece[pl.ds(outer * down_half, down_half), :]
+    sib_ref[step, 0:down_half, :] = piece[
+        pl.ds((1 - outer) * down_half, down_half), :
+    ].astype(jnp.bfloat16)
+
+    @pl.when(step == slots - 1)
+    def _():
+        for b in range(blocks):
+            rows = slice(b * BLK, (b + 1) * BLK)
+            low_ref[rows, :] = (acc[rows, :] * select(b)).astype(jnp.bfloat16)
+        note = jnp.zeros((1, HEAD), jnp.int32)
+        for b in range(blocks):
+            note = jnp.where(lane == b, pos[b * BLK] // BLK, note)
+        note = jnp.where(lane == blocks, count[0], note)
+        low_ref[blocks * BLK :, :] = jnp.broadcast_to(
+            note.astype(jnp.float32), (16, HEAD)
+        ).astype(jnp.bfloat16)
+        piece[0:kv, :] = ADAPTER_SCALE * lax.dot_general(
+            grad[...], low_ref[0 : blocks * BLK, :], (((0,), (0,)), ((), ())),
+            preferred_element_type=jnp.float32,
+        )
+        for r in range(slots):
+            base = sc[r] * up_rows
+            own_ref[r, down_half:, :] = piece[pl.ds(base + outer * up_half, up_half), :]
+            sib_ref[r, down_half:, :] = piece[
+                pl.ds(base + (1 - outer) * up_half, up_half), :
+            ].astype(jnp.bfloat16)
+
+
+def first_kernel(spec, common, sc, w_ref, r_ref, out_ref, sems):
+    rows, half = r_ref.shape
+    plane, outer = sc[9], sc[8]
+    tail = spec + common - rows
+
+    def gather(p, o):
+        mine = w_ref.at[:, o * half : (o + 1) * half]
+        lower, upper = (mine, r_ref) if o == 0 else (r_ref, mine)
+        if p == 0:
+            moves = ((lower, 0, rows, 0), (upper, 0, tail, rows))
+        else:
+            moves = (
+                (upper, rows - spec, spec, 0),
+                (lower, spec, rows - spec, spec),
+                (upper, 0, tail, rows),
+            )
+        copies = [
+            pltpu.make_async_copy(
+                src.at[at : at + n, :], out_ref.at[to : to + n, :], sems.at[i]
+            )
+            for i, (src, at, n, to) in enumerate(moves)
+        ]
+        for c in copies:
+            c.start()
+        for c in copies:
+            c.wait()
+
+    for p in range(2):
+        for o in range(2):
+            pl.when(jnp.logical_and(plane == p, outer == o))(functools.partial(gather, p, o))
+
+
+def sources_of(kind, sc, chunk, spec, common, refs):
+    plane, outer = sc[9], sc[8]
+    mine, theirs = plane * (spec + common), (1 - plane) * (spec + common)
+    node = lambda i: sc[i] * chunk
+
+    def whole(i, held, crossed, at):
+        return (
+            node(i), chunk,
+            ((held, 0, spec, mine), (held, spec, common, spec), (crossed, at, spec, theirs)),
+        )
+
+    if kind == 0:
+        w_ref, r_ref, y0, x1, z1 = refs
+        rows = r_ref.shape[0]
+        half = r_ref.shape[1]
+        own = w_ref.at[:, pl.ds(pl.multiple_of(outer * half, half), half)]
+        return (
+            (node(10), chunk, ((own, 0, rows, outer * rows), (r_ref, 0, rows, (1 - outer) * rows))),
+            whole(14, y0, x1, 0),
+            whole(11, z1, x1, spec),
+        )
+    if kind == 1:
+        y1, x2, z2 = refs
+        return (whole(15, y1, x2, 0), whole(12, z2, x2, spec))
+    if kind == 2:
+        y2, x3, z3, y3 = refs
+        return (
+            whole(16, y2, x3, 0),
+            whole(13, z3, x3, spec),
+            (
+                node(17) + plane * spec, spec + common,
+                ((y3, 0, spec, plane * common), (y3, spec, common, (1 - plane) * spec)),
+            ),
+        )
+    (x4,) = refs
+    return ((node(17) + theirs, spec, ((x4, 0, spec, 0),)),)
+
+
+def load_sources(sources, toks, tv, wv, sems):
+    at, copies = 0, []
+    for first, width, pieces in sources:
+        first = pl.multiple_of(first, 128)
+        for i, t in enumerate(toks):
+            copies.append((t.at[:, pl.ds(first, width)], tv.at[i, :, at : at + width]))
+        for ref, row, n, to in pieces:
+            to = pl.multiple_of(at + to, 128)
+            copies.append((ref.at[row : row + n, :], wv.at[pl.ds(to, n), :]))
+        at += width
+    made = [pltpu.make_async_copy(s, d, sems.at[i]) for i, (s, d) in enumerate(copies)]
+    for c in made:
+        c.start()
+    return made
+
+
+def product_kernel(kind, spec, common, sc, *refs):
+    refs, (out_ref, tv, wv, sems, step_sems) = refs[:-5], refs[-5:]
+    toks, extra, pieces = refs[:2], refs[2:5] if kind == 0 else refs[2:3], refs[5:] if kind == 0 else refs[3:]
+    chunk = toks[0].shape[1] // 8
+    sources = sources_of(kind, sc, chunk, spec, common, pieces)
+    made = load_sources(sources, toks, tv, wv, sems)
+    if kind:
+        total = pltpu.make_async_copy(extra[0], out_ref, step_sems.at[0])
+        total.start()
+        total.wait()
+    for c in made:
+        c.wait()
+    tokens = out_ref.shape[1]
+    half = out_ref.shape[2]
+    block = 256
+
+    @pl.loop(0, 2 * (tokens // block))
+    def _(i):
+        core = i // (tokens // block)
+        rows = pl.ds(pl.multiple_of(lax.rem(i, tokens // block) * block, block), block)
+        if kind:
+            start = out_ref[core, rows, :]
+        else:
+            low, low_s, b_ref = extra
+            lows = jnp.where(core == 0, low[rows, :], low_s[rows, :])
+            start = ADAPTER_SCALE * lax.dot_general(
+                lows, b_ref[pl.ds(pl.multiple_of(sc[8] * half, half), half), :],
+                (((1,), (1,)), ((), ())), preferred_element_type=jnp.float32,
+            )
+        out_ref[core, rows, :] = start + jnp.dot(
+            tv[core, rows, :], wv[...], preferred_element_type=jnp.float32
+        )
+
+
+def finish_kernel(core, spec, common, sc, tok, total_ref, low_ref, tab_ref, x4, out_ref, tv, wv, tot, res, sems):
+    chunk = tok.shape[1] // 8
+    sources = sources_of(3, sc, chunk, spec, common, (x4,))
+    made = load_sources(sources, (tok,), tv, wv, sems)
+    total = pltpu.make_async_copy(total_ref.at[core], tot, sems.at[3])
+    total.start()
+    tokens, half = tot.shape
+    note = low_ref[tokens:, :].astype(jnp.float32)[0:1, :]
+    starts = SEQ // BLK
+    index = lax.broadcasted_iota(jnp.int32, (starts, HEAD), 0).astype(jnp.float32)
+    blocks = tokens // BLK
+    tables = []
+    for b in range(blocks):
+        hit = index == note[:, b : b + 1]
+        pick = lambda at: jnp.sum(
+            jnp.where(hit, tab_ref[at : at + starts, :], 0.0), axis=0, keepdims=True
+        )
+        tables.append(block_tables(tab_ref, pick(2 * BLK), pick(2 * BLK + starts)))
+    for c in made:
+        c.wait()
+    total.wait()
+    for b in range(blocks):
+        rows = slice(b * BLK, (b + 1) * BLK)
+        cosine, sine = tables[b]
+        live = jnp.where(note[:, blocks : blocks + 1] > b, 1.0, 0.0)
+        cosine, sine = cosine * live, sine * live
+        pre = tot[rows, :] + jnp.dot(tv[0, rows, :], wv[...], preferred_element_type=jnp.float32)
+        for h in range(half // HEAD):
+            cols = slice(h * HEAD, (h + 1) * HEAD)
+            x = pre[:, cols]
+            res[rows, cols] = (x * cosine + pltpu.roll(x, HEAD // 2, 1) * sine).astype(jnp.bfloat16)
+    if core:
+        dst = out_ref
+    else:
+        dst = out_ref.at[:, pl.ds(pl.multiple_of(sc[8] * half, half), half)]
+    save = pltpu.make_async_copy(res, dst, sems.at[3])
+    save.start()
+    save.wait()
+
+
+def merge_kernel(sc, given_ref, keys_ref, out_ref, sem):
+    half = given_ref.shape[1]
+    at = pl.multiple_of((1 - sc[8]) * half, half)
+    move = pltpu.make_async_copy(given_ref, out_ref.at[:, pl.ds(at, half)], sem)
+    move.start()
+    move.wait()
+
+
+class Routes:
+    def __init__(self, mesh):
+        self.groups, self.nodes, self.outers = (mesh.shape[a] for a in ALL)
+        self.z = self.nodes // 2
+        line = list(range(self.z))
+        ring = line[:1] + line[1::2] + line[2::2][::-1]
+        self.next = {ring[i]: ring[(i + 1) % self.z] for i in range(self.z)}
+        self.prev = {v: k for k, v in self.next.items()}
+
+    def pairs(self, f):
+        at = lambda g, z, y, o: (g * self.nodes + 2 * z + y) * self.outers + o
+        return [
+            (at(g, z, y, o), at(*f(g, z, y, o)))
+            for g in range(self.groups)
+            for z in range(self.z)
+            for y in range(2)
+            for o in range(self.outers)
+        ]
+
+    def table(self):
+        rows = []
+        for _, n, o, g in [
+            (0, n, o, g) for g in range(self.groups) for n in range(self.nodes) for o in range(self.outers)
+        ]:
+            z, y = divmod(n, 2)
+            slot = [n ^ (((r >> 2) & 1) | (((r >> 1) & 1) << 1) | ((r & 1) << 2)) for r in range(8)]
+            from_z = [z]
+            for _ in range(self.z - 1):
+                from_z.append(self.prev[from_z[-1]])
+            rows.append(
+                slot + [o, g] + [2 * k + y for k in from_z] + [2 * k + 1 - y for k in from_z]
+            )
+        return np.array(rows, np.int32)
+
+
+def call(kernel, name, shapes, in_specs, out_specs, scratch, args, grid=(), prefetch=1, flops=0, moved=0, aliases=None):
+    return pl.pallas_call(
+        kernel,
+        out_shape=shapes,
+        grid_spec=pltpu.PrefetchScalarGridSpec(
+            num_scalar_prefetch=prefetch, grid=grid, in_specs=in_specs, out_specs=out_specs,
+            scratch_shapes=scratch,
+        ),
+        compiler_params=pltpu.CompilerParams(vmem_limit_bytes=VMEM_LIMIT),
+        cost_estimate=pl.CostEstimate(flops=flops, bytes_accessed=moved, transcendentals=0),
+        input_output_aliases=aliases or {},
+        name=name,
+    )(*args)
+
+
+def fast_body(
+    routes, tokens, frozen_weight, down_adapter, second_adapter_weight, tenant_ids, block_counts, positions, cotangent
+):
+    bf16, f32 = jnp.bfloat16, jnp.float32
+    rows, width = tokens.shape
+    weight_rows, kv = frozen_weight.shape
+    half = kv // 2
+    nodes = routes.nodes
+    chunk = 2 * weight_rows
+    spec, common = 3 * chunk // 8, chunk // 4
+    held = spec + common
+    rank = down_adapter.shape[1]
+    outer = lax.axis_index("outer")
+    me = lax.axis_index(ALL)
+    table = routes.table()
+    sc = lax.dynamic_slice(jnp.asarray(table), (me, 0), (1, table.shape[1]))[0]
+    tab = jnp.asarray(rope_constants())
+
+    send = lambda x, f: lax.ppermute(x, ALL, routes.pairs(f))
+    to_core = lambda g, z, y, o: (g, z, y, 1 - o)
+    to_x = lambda g, z, y, o: (1 - g, z, y, o)
+    to_y = lambda g, z, y, o: (g, z, 1 - y, o)
+    to_z = lambda g, z, y, o: (g, routes.next[z], y, o)
+    to_z1 = lambda g, z, y, o: (g, z ^ 1, y, o)
+    to_z2 = lambda g, z, y, o: (g, z ^ 2, y, o)
+    vm = pl.BlockSpec(memory_space=pltpu.VMEM)
+    dma = pltpu.SemaphoreType.DMA
+    shape = jax.ShapeDtypeStruct
+
+    other = lax.dynamic_slice(frozen_weight, (0, (1 - outer) * half), (weight_rows, half))
+    r = send(other, to_core)
+    z0 = call(
+        functools.partial(first_kernel, spec, common), "first_rows", shape((held, half), bf16),
+        [ANY, ANY], vm, [dma((3,))], (sc, frozen_weight, r), moved=4 * held * half,
+    )
+    z1 = send(z0, to_z)
+    y0 = send(z0, to_y)
+    sib_tokens = send(tokens, to_core)
+
+    slot_rows = chunk // 2 + kv // nodes // 2
+    low, own, sib = call(
+        gradient_kernel, "adapter_gradients",
+        (
+            shape((rows + 16, rank), bf16),
+            shape((nodes, slot_rows, rank), f32),
+            shape((nodes, slot_rows, rank), bf16),
+        ),
+        [
+            pl.BlockSpec((rows, chunk), lambda i, sc, *_: (0, sc[i])),
+            pl.BlockSpec((chunk, rank), lambda i, sc, *_: (sc[i], 0)),
+            pl.BlockSpec((kv, rank), lambda i, *_: (0, 0)),
+            pl.BlockSpec((rows, kv), lambda i, *_: (0, 0)),
+            pl.BlockSpec(tab.shape, lambda i, *_: (0, 0)),
+        ],
+        (
+            pl.BlockSpec((rows + 16, rank), lambda i, *_: (0, 0)),
+            pl.BlockSpec((nodes, slot_rows, rank), lambda i, *_: (0, 0, 0)),
+            pl.BlockSpec((nodes, slot_rows, rank), lambda i, *_: (0, 0, 0)),
+        ),
+        [
+            pltpu.VMEM((rows, kv), bf16),
+            pltpu.VMEM((rows, rank), bf16),
+            pltpu.VMEM((rows, rank), f32),
+            pltpu.VMEM((max(chunk, kv), rank), f32),
+        ],
+        (sc, tenant_ids, block_counts, positions, tokens, down_adapter, second_adapter_weight, cotangent, tab),
+        grid=(nodes,), prefetch=4,
+        flops=2 * rows * rank * (2 * width + 2 * kv), moved=2 * rows * width + 2 * width * rank + 6 * nodes * slot_rows * rank,
+    )
+    low_s = send(low, to_core)
+    s = own + send(sib, to_core).astype(f32)
+    s = s[:4] + send(s[4:].astype(bf16), to_y).astype(f32)
+
+    crossed = lambda y, z: send(jnp.concatenate((y[:spec], z[:spec])), to_x)
+    z2 = send(z1, to_z)
+    y1 = send(z1, to_y)
+    x1 = crossed(y0, z1)
+    z3 = send(z2, to_z)
+    y2 = send(z2, to_y)
+    x2 = crossed(y1, z2)
+    y3 = send(z3, to_y)
+    x3 = crossed(y2, z3)
+    x4 = send(y3[:spec], to_x)
+
+    s = s[:2] + send(s[2:].astype(bf16), to_z1).astype(f32)
+    s = s[0] + send(s[1].astype(bf16), to_z2).astype(f32)
+    t = send(s, to_core)
+
+    def product(kind, depth, copies, extra, extra_specs, pieces):
+        return call(
+            functools.partial(product_kernel, kind, spec, common), "product_%d" % kind,
+            shape((2, rows, half), f32),
+            [ANY, ANY, *extra_specs, *[ANY] * len(pieces)], vm,
+            [pltpu.VMEM((2, rows, depth), bf16), pltpu.VMEM((depth, half), bf16), dma((copies,)), dma((1,))],
+            (sc, tokens, sib_tokens, *extra, *pieces),
+            flops=4 * rows * depth * half, moved=4 * rows * depth + 2 * depth * half + 16 * rows * half,
+        )
+
+    total = product(
+        0, 3 * chunk, 14, (low, low_s, second_adapter_weight), (vm, vm, vm), (frozen_weight, r, y0, x1, z1)
+    )
+    total = product(1, 2 * chunk, 10, (total,), (ANY,), (y1, x2, z2))
+    total = product(2, 2 * chunk + held, 14, (total,), (ANY,), (y2, x3, z3, y3))
+
+    def finish(core, out, tok, lows):
+        return call(
+            functools.partial(finish_kernel, core, spec, common), "finish_%d" % core, out,
+            [ANY, ANY, vm, vm, ANY], ANY,
+            [
+                pltpu.VMEM((1, rows, spec), bf16), pltpu.VMEM((spec, half), bf16),
+                pltpu.VMEM((rows, half), f32), pltpu.VMEM((rows, half), bf16), dma((4,)),
+            ],
+            (sc, tok, total, lows, tab, x4),
+            flops=2 * rows * spec * half, moved=6 * rows * half + 2 * rows * spec,
+        )
+
+    theirs = finish(1, shape((rows, half), bf16), sib_tokens, low_s)
+    given = send(theirs, to_core)
+    mine = finish(0, shape((rows, kv), bf16), tokens, low)
+    keys = call(
+        merge_kernel, "merge", shape((rows, kv), bf16), [ANY, ANY], ANY, [dma],
+        (sc, given, mine), aliases={2: 0}, moved=4 * rows * half,
+    )
+    down_rows = chunk // 2
+    lower, upper = jnp.where(outer == 0, s, t), jnp.where(outer == 0, t, s)
+    down = jnp.concatenate((lower[:down_rows], upper[:down_rows]))
+    up = jnp.concatenate((lower[down_rows:], upper[down_rows:]))
+    return keys, down, up
 
 
 def rope_tables(positions):
@@ -30,15 +479,8 @@
     return jnp.stack((out_first, out_second), axis=2).reshape(rows, -1)
 
 
-def body(
-    tokens,
-    frozen_weight,
-    down_adapter,
-    second_adapter_weight,
-    tenant_ids,
-    block_counts,
-    positions,
-    cotangent,
+def plain_body(
+    tokens, frozen_weight, down_adapter, second_adapter_weight, tenant_ids, block_counts, positions, cotangent
 ):
     token_rows = tokens.shape[0]
     block_total = tenant_ids.shape[0]
@@ -102,8 +544,9 @@
         P(("groups", "node", "outer")),
         P(("groups", "node", "outer"), None),
     )
+    routed = tuple(mesh.shape[a] for a in ALL) == (2, 8, 2)
     return jax.shard_map(
-        body,
+        functools.partial(fast_body, Routes(mesh)) if routed else plain_body,
         mesh=mesh,
         in_specs=placed,
         out_specs=(

time: 348 us -> 177 us (0.51)
  waiting for transfers between devices: 283 us -> 77.3 us
  Pallas kernels: 0 us -> 59.6 us
  matrix products: 32.5 us -> 0 us
  starting transfers between devices: 0.16 us -> 23 us
  between operations: 14.5 us -> 1.57 us
    reduce_scatter x2 -> x0, waiting for transfers between devices: 144 us -> none  [the longest x1 91.6 us: body(): lax.psum_scatter(down_product, 'node', scatter_dimension=0, tiled=True)]
    all_gather x1 -> x0, waiting for transfers between devices: 119 us -> none  [body(): lax.all_gather(frozen_weight, ('node', 'outer'), axis=0, tiled=True)]
    ppermute x0 -> x20, waiting for transfers between devices: none -> 77.3 us  [fast_body(): send = lambda x, f: lax.ppermute(x, ALL, routes.pairs(f))]
    pallas_call x0 -> x8, Pallas kernels: none -> 59.6 us  [call(): pl.pallas_call(kernel, out_shape=shapes, grid_spec=pltpu.PrefetchScalarGr...]
    dot_general x5 -> x0, matrix products: 32.5 us -> none  [the longest x1 16.1 us: body(): jnp.dot(tokens, lax.all_gather(frozen_weight, ('node', 'outer'), axis=0,...]
    ppermute x0 -> x20, starting transfers between devices: none -> 23 us  [fast_body(): send = lambda x, f: lax.ppermute(x, ALL, routes.pairs(f))]
    psum x1 -> x0, waiting for transfers between devices: 19.6 us -> none  [body(): lax.psum((shares[0], shares[1]), 'outer')]
  transfers between devices with their start and end apart: 4 -> 20, of which waited for: 4 -> 10; matrix products, arithmetic and copies ran while one was open for 6% -> 4% of each run, Pallas kernels for 0% -> 24%
where the time goes in v1:
time: 177 us; the launch traced here: 175 us
  waiting for transfers between devices  77.3 us (44%)
  Pallas kernels  59.6 us (34%)
  starting transfers between devices  23 us (13%)
  local copies, waits for them, and re-layouts  8.32 us (5%)
  other arithmetic  5.48 us (3%)
    ppermute x20, waiting for transfers between devices, fast_body(): send = lambda x, f: lax.ppermute(x, ALL, routes.pairs(f))  77.3 us
    pallas_call x8, Pallas kernels, call(): pl.pallas_call(kernel, out_shape=shapes, grid_spec=pltpu.PrefetchScalarGr...  59.6 us
    ppermute x20, starting transfers between devices, fast_body(): send = lambda x, f: lax.ppermute(x, ALL, routes.pairs(f))  23 us
    unnamed x20, local copies, waits for them, and re-layouts  6.17 us
  transfers between devices with their start and end apart: 20, of which 10 were waited for; matrix products, arithmetic and copies ran while one was open for 4% of the time, Pallas kernels for 24%

profile of v1, /device:TPU:0, one launch (start us, length us, event | category | flops | bytes accessed | tf_op | source)
XLA Modules:
  0.0 175.3 jit_solution(17977554896618453850)
XLA Ops:
  1.2 1.1 constant_dynamic-slice_fusion
  3.8 1.6 copy-done.2
  6.3 0.9 copy-done.5
  8.6 12.5 %adapter_gradients.1 = (bf16[528,128]{1,0:T(8,128)(2,1)S(1)}, f32[8,576,128]{2,1,0:T(8,128)}, bf16[8,576,128]{2,1,0:T(8,128)(2,1)S(1)}) custom-call(s32[18]{0:T(128)S(1)} %dynamic-slice_bitcast_fusion.sc, s32[4]{0:T(128)S(1)} %copy-done.9, s32[1]{0:T(128)S(6)} %copy.15.count, s32[512]{0:T(512)S(1)} %copy-done.8, bf16[512,8192]{1,0:T(8,128)(2,1)} %tok.1, ...), custom_call_target="tpu_custom_call" | custom-call | flops 2415919104 | bytes 14024704 | tf_op jit(solution)/shard_map/adapter_gradients/pallas_call | solution.py:319
  22.3 2.7 %collective-permute-start.4 = (bf16[640,512]{1,0:T(8,128)(2,1)S(1)}, bf16[640,512]{1,0:T(8,128)(2,1)S(1)}, u32[]{:S(2)}, u32[]{:S(2)}) collective-permute-start(bf16[640,512]{1,0:T(8,128)(2,1)S(1)} %first_rows.1), channel_id=1, source_target_pairs={{0,4},{1,5},{2,6},{3,7},{4,12},{5,13},{6,14},{7,15},{8,0},{9,1},{1... | collective-permute-start | bytes 1966088 | tf_op jit(solution)/shard_map/ppermute | solution.py:351
  25.0 16.1 %collective-permute-done.4.refs_9_ = bf16[640,512]{1,0:T(8,128)(2,1)S(1)} collective-permute-done((bf16[640,512]{1,0:T(8,128)(2,1)S(1)}, bf16[640,512]{1,0:T(8,128)(2,1)S(1)}, u32[]{:S(2)}, u32[]{:S(2)}) %collective-permute-start.4) | collective-permute-done | bytes 655392 | tf_op jit(solution)/shard_map/ppermute | solution.py:351
  42.0 1.9 %convert_add_fusion = f32[8,576,128]{2,1,0:T(8,128)S(1)} fusion(f32[8,576,128]{2,1,0:T(8,128)} %get-tuple-element.7, bf16[8,576,128]{2,1,0:T(8,128)(2,1)S(1)} %collective-permute-done.15), kind=kLoop, calls=%fused_computation | loop fusion | flops 1179648 | bytes 5898240 | tf_op jit(solution)/shard_map/add | solution.py:403
  43.9 1.6 collective-permute-start.16
  46.0 1.5 collective-permute-start.6
  47.5 10.9 %collective-permute-done.7.refs_5_ = bf16[640,512]{1,0:T(8,128)(2,1)S(1)} collective-permute-done((bf16[640,512]{1,0:T(8,128)(2,1)S(1)}, bf16[640,512]{1,0:T(8,128)(2,1)S(1)}, u32[]{:S(2)}, u32[]{:S(2)}) %collective-permute-start.7) | collective-permute-done | bytes 655392 | tf_op jit(solution)/shard_map/ppermute | solution.py:351
  58.9 1.4 collective-permute-done.16
  60.4 3.4 %collective-permute-start.17 = (bf16[2,576,128]{2,1,0:T(8,128)(2,1)S(1)}, bf16[2,576,128]{2,1,0:T(8,128)(2,1)S(1)}, u32[]{:S(2)}, u32[]{:S(2)}) collective-permute-start(bf16[2,576,128]{2,1,0:T(8,128)(2,1)S(1)} %slice.99), channel_id=1, source_target_pairs={{0,4},{1,5},{2,6},{3,7},{4,0},{5,1},{6,2},{7,3},{8,12},{9,13},{10,... | collective-permute-start | bytes 884744 | tf_op jit(solution)/shard_map/ppermute | solution.py:351
  63.9 10.4 %collective-permute-done.3.refs_7_ = bf16[640,512]{1,0:T(8,128)(2,1)S(1)} collective-permute-done((bf16[640,512]{1,0:T(8,128)(2,1)S(1)}, bf16[640,512]{1,0:T(8,128)(2,1)S(1)}, u32[]{:S(2)}, u32[]{:S(2)}) %collective-permute-start.3) | collective-permute-done | bytes 655392 | tf_op jit(solution)/shard_map/ppermute | solution.py:351
  74.3 1.6 collective-permute-start.9
  76.0 12.4 %collective-permute-done.6.refs_3_ = bf16[640,512]{1,0:T(8,128)(2,1)S(1)} collective-permute-done((bf16[640,512]{1,0:T(8,128)(2,1)S(1)}, bf16[640,512]{1,0:T(8,128)(2,1)S(1)}, u32[]{:S(2)}, u32[]{:S(2)}) %collective-permute-start.6) | collective-permute-done | bytes 655392 | tf_op jit(solution)/shard_map/ppermute | solution.py:351
  88.4 1.6 collective-permute-start.5
  90.6 1.5 collective-permute-start.12
  92.1 10.3 %collective-permute-done.9.refs_3_ = bf16[640,512]{1,0:T(8,128)(2,1)S(1)} collective-permute-done((bf16[640,512]{1,0:T(8,128)(2,1)S(1)}, bf16[640,512]{1,0:T(8,128)(2,1)S(1)}, u32[]{:S(2)}, u32[]{:S(2)}) %collective-permute-start.9) | collective-permute-done | bytes 655392 | tf_op jit(solution)/shard_map/ppermute | solution.py:351
  102.4 2.1 %collective-permute-start.18 = (bf16[576,128]{1,0:T(8,128)(2,1)S(1)}, bf16[576,128]{1,0:T(8,128)(2,1)S(1)}, u32[]{:S(2)}, u32[]{:S(2)}) collective-permute-start(bf16[576,128]{1,0:T(8,128)(2,1)S(1)} %fusion.1), channel_id=1, source_target_pairs={{0,8},{1,9},{2,10},{3,11},{4,12},{5,13},{6,14},{7,15},{8,0},{9,1},... | collective-permute-start | bytes 442376 | tf_op jit(solution)/shard_map/ppermute | solution.py:351
  104.6 3.8 %collective-permute-done.18 = bf16[576,128]{1,0:T(8,128)(2,1)S(1)} collective-permute-done((bf16[576,128]{1,0:T(8,128)(2,1)S(1)}, bf16[576,128]{1,0:T(8,128)(2,1)S(1)}, u32[]{:S(2)}, u32[]{:S(2)}) %collective-permute-start.18) | collective-permute-done | bytes 147488 | tf_op jit(solution)/shard_map/ppermute | solution.py:351
  108.4 1.6 collective-permute-start.11
  110.1 4.4 %collective-permute-done.12.refs_6_ = bf16[640,512]{1,0:T(8,128)(2,1)S(1)} collective-permute-done((bf16[640,512]{1,0:T(8,128)(2,1)S(1)}, bf16[640,512]{1,0:T(8,128)(2,1)S(1)}, u32[]{:S(2)}, u32[]{:S(2)}) %collective-permute-start.12) | collective-permute-done | bytes 655392 | tf_op jit(solution)/shard_map/ppermute | solution.py:351
  116.0 1.7 collective-permute-start.13
  117.8 9.2 %product_0.1.refs_2_ = f32[2,512,512]{2,1,0:T(8,128)} custom-call(s32[18]{0:T(128)S(1)} %dynamic-slice_bitcast_fusion.sc, bf16[512,8192]{1,0:T(8,128)(2,1)} %tok.1, bf16[512,8192]{1,0:T(8,128)(2,1)} %collective-permute-done.refs_1_.tok, bf16[528,128]{1,0:T(8,128)(2,1)S(1)} %get-tuple-element.6.refs_2_.low_ref, ...), custom_call_target="tpu_custom_call" | custom-call | flops 3221225472 | bytes 13631488 | tf_op jit(solution)/shard_map/product_0/pallas_call | solution.py:319
  127.0 6.5 %product_1.1.refs_2_ = f32[2,512,512]{2,1,0:T(8,128)S(1)} custom-call(s32[18]{0:T(128)S(1)} %dynamic-slice_bitcast_fusion.sc, bf16[512,8192]{1,0:T(8,128)(2,1)} %tok.1, bf16[512,8192]{1,0:T(8,128)(2,1)} %collective-permute-done.refs_1_.tok, f32[2,512,512]{2,1,0:T(8,128)} %product_0.1.refs_2_, bf16[640,512]{1,0:T(8,128)(2,1)S(1)} %collective-permute-done.6.refs_3_, ...), custom_call_target="tpu_custom_call" | custom-call | flops 2147483648 | bytes 10485760 | tf_op jit(solution)/shard_map/product_1/pallas_call | solution.py:319
  133.5 1.4 copy-done
  134.9 7.1 %collective-permute-done.11.refs_4_ = bf16[768,512]{1,0:T(8,128)(2,1)S(1)} collective-permute-done((bf16[768,512]{1,0:T(8,128)(2,1)S(1)}, bf16[768,512]{1,0:T(8,128)(2,1)S(1)}, u32[]{:S(2)}, u32[]{:S(2)}) %collective-permute-start.11) | collective-permute-done | bytes 786464 | tf_op jit(solution)/shard_map/ppermute | solution.py:351
  142.0 7.8 %product_2.1.total_ref = f32[2,512,512]{2,1,0:T(8,128)S(1)} custom-call(s32[18]{0:T(128)S(1)} %dynamic-slice_bitcast_fusion.sc, bf16[512,8192]{1,0:T(8,128)(2,1)} %tok.1, bf16[512,8192]{1,0:T(8,128)(2,1)} %collective-permute-done.refs_1_.tok, f32[2,512,512]{2,1,0:T(8,128)} %copy-done, bf16[640,512]{1,0:T(8,128)(2,1)S(1)} %collective-permute-done.9.refs_3_, ...), custom_call_target="tpu_custom_call" | custom-call | flops 2818572288 | bytes 12451840 | tf_op jit(solution)/shard_map/product_2/pallas_call | solution.py:319
  149.8 2.2 %finish_1.1 = bf16[512,512]{1,0:T(8,128)(2,1)S(1)} custom-call(s32[18]{0:T(128)S(1)} %dynamic-slice_bitcast_fusion.sc, bf16[512,8192]{1,0:T(8,128)(2,1)} %collective-permute-done.refs_1_.tok, f32[2,512,512]{2,1,0:T(8,128)S(1)} %product_2.1.total_ref, bf16[528,128]{1,0:T(8,128)(2,1)S(1)} %collective-permute-done.1.refs_3_.low_ref, f32[320,128]{1,0:T(8,128)S(1)} %copy-done.4, ...), custom_call_target="tpu_custom_call" | custom-call | flops 201326592 | bytes 1966080 | tf_op jit(solution)/shard_map/finish_1/pallas_call | solution.py:319
  152.2 1.1 broadcast_select_fusion.1
  154.8 2.9 %finish_0.1.keys_ref = bf16[512,1024]{1,0:T(8,128)(2,1)} custom-call(s32[18]{0:T(128)S(1)} %dynamic-slice_bitcast_fusion.sc, bf16[512,8192]{1,0:T(8,128)(2,1)} %tok.1, f32[2,512,512]{2,1,0:T(8,128)S(1)} %product_2.1.total_ref, bf16[528,128]{1,0:T(8,128)(2,1)S(1)} %get-tuple-element.6.refs_2_.low_ref, f32[320,128]{1,0:T(8,128)S(1)} %copy-done.4, ...), custom_call_target="tpu_custom_call" | custom-call | flops 201326592 | bytes 1966080 | tf_op jit(solution)/shard_map/finish_0/pallas_call | solution.py:319
  157.8 17.5 %merge.1 = bf16[512,1024]{1,0:T(8,128)(2,1)} custom-call(s32[18]{0:T(128)S(1)} %dynamic-slice_bitcast_fusion.sc, bf16[512,512]{1,0:T(8,128)(2,1)} %collective-permute-done.14.given_ref, bf16[512,1024]{1,0:T(8,128)(2,1)} %finish_0.1.keys_ref), custom_call_target="tpu_custom_call", output_to_operand_aliasing={{}: (2, {})} | custom-call | bytes 1048576 | tf_op jit(solution)/shard_map/merge/pallas_call | solution.py:319
  (62 shorter events, 10.9 us)
Async XLA Ops:
  0.6 3.1 %copy-start.7 = (bf16[512,1024]{1,0:T(8,128)(2,1)S(1)}, bf16[512,1024]{1,0:T(8,128)(2,1)}, u32[]{:S(2)}) copy-start(bf16[512,1024]{1,0:T(8,128)(2,1)} %cot_ref.1) | copy-start | bytes 3145732
  0.6 117.1 %collective-permute-start = (bf16[512,8192]{1,0:T(8,128)(2,1)}, bf16[512,8192]{1,0:T(8,128)(2,1)}, u32[]{:S(2)}, u32[]{:S(2)}) collective-permute-start(bf16[512,8192]{1,0:T(8,128)(2,1)} %tok.1), channel_id=1, source_target_pairs={{0,1},{1,0},{2,3},{3,2},{4,5},{5,4},{6,7},{7,6},{8,9},{9,8},{10,11... | collective-permute-start | bytes 25165832 | tf_op jit(solution)/shard_map/ppermute | solution.py:351
  2.2 19.2 %collective-permute-start.2 = (bf16[512,512]{1,0:T(8,128)(2,1)S(1)}, bf16[512,512]{1,0:T(8,128)(2,1)S(1)}, u32[]{:S(2)}, u32[]{:S(2)}) collective-permute-start(bf16[512,512]{1,0:T(8,128)(2,1)S(1)} %constant_dynamic-slice_fusion), channel_id=1, source_target_pairs={{0,1},{1,0},{2,3},{3,2},{4,5},{5,4},{6,7},{7,6},{8,9},{9,8},{10,11... | collective-permute-start | bytes 1572872 | tf_op jit(solution)/shard_map/ppermute | solution.py:351
  3.8 1.6 copy-start.2
  5.4 0.9 copy-start.3
  6.3 0.9 copy-start.5
  7.2 0.7 copy-start.8
  7.9 0.7 copy-start.9
  8.6 12.9 %copy-start.1 = (bf16[512,1024]{1,0:T(8,128)(2,1)S(1)}, bf16[512,1024]{1,0:T(8,128)(2,1)}, u32[]{:S(2)}) copy-start(bf16[512,1024]{1,0:T(8,128)(2,1)} %refs_5_.1) | copy-start | bytes 3145732
  21.0 20.9 %collective-permute-start.15 = (bf16[8,576,128]{2,1,0:T(8,128)(2,1)S(1)}, bf16[8,576,128]{2,1,0:T(8,128)(2,1)S(1)}, u32[]{:S(2)}, u32[]{:S(2)}) collective-permute-start(bf16[8,576,128]{2,1,0:T(8,128)(2,1)S(1)} %get-tuple-element.8), channel_id=1, source_target_pairs={{0,1},{1,0},{2,3},{3,2},{4,5},{5,4},{6,7},{7,6},{8,9},{9,8},{10,11... | collective-permute-start | bytes 3538952 | tf_op jit(solution)/shard_map/ppermute | solution.py:351
  22.3 18.9 %collective-permute-start.4 = (bf16[640,512]{1,0:T(8,128)(2,1)S(1)}, bf16[640,512]{1,0:T(8,128)(2,1)S(1)}, u32[]{:S(2)}, u32[]{:S(2)}) collective-permute-start(bf16[640,512]{1,0:T(8,128)(2,1)S(1)} %first_rows.1), channel_id=1, source_target_pairs={{0,4},{1,5},{2,6},{3,7},{4,12},{5,13},{6,14},{7,15},{8,0},{9,1},{1... | collective-permute-start | bytes 1966088 | tf_op jit(solution)/shard_map/ppermute | solution.py:351
  41.1 17.3 %collective-permute-start.7 = (bf16[640,512]{1,0:T(8,128)(2,1)S(1)}, bf16[640,512]{1,0:T(8,128)(2,1)S(1)}, u32[]{:S(2)}, u32[]{:S(2)}) collective-permute-start(bf16[640,512]{1,0:T(8,128)(2,1)S(1)} %collective-permute-done.4.refs_9_), channel_id=1, source_target_pairs={{0,4},{1,5},{2,6},{3,7},{4,12},{5,13},{6,14},{7,15},{8,0},{9,1},{1... | collective-permute-start | bytes 1966088 | tf_op jit(solution)/shard_map/ppermute | solution.py:351
  43.9 16.3 %collective-permute-start.16 = (bf16[4,576,128]{2,1,0:T(8,128)(2,1)S(1)}, bf16[4,576,128]{2,1,0:T(8,128)(2,1)S(1)}, u32[]{:S(2)}, u32[]{:S(2)}) collective-permute-start(bf16[4,576,128]{2,1,0:T(8,128)(2,1)S(1)} %slice.98), channel_id=1, source_target_pairs={{0,2},{1,3},{2,0},{3,1},{4,6},{5,7},{6,4},{7,5},{8,10},{9,11},{10,... | collective-permute-start | bytes 1769480 | tf_op jit(solution)/shard_map/ppermute | solution.py:351
  45.5 28.8 %collective-permute-start.3 = (bf16[640,512]{1,0:T(8,128)(2,1)S(1)}, bf16[640,512]{1,0:T(8,128)(2,1)S(1)}, u32[]{:S(2)}, u32[]{:S(2)}) collective-permute-start(bf16[640,512]{1,0:T(8,128)(2,1)S(1)} %first_rows.1), channel_id=1, source_target_pairs={{0,2},{1,3},{2,0},{3,1},{4,6},{5,7},{6,4},{7,5},{8,10},{9,11},{10,... | collective-permute-start | bytes 1966088 | tf_op jit(solution)/shard_map/ppermute | solution.py:351
  46.0 42.3 %collective-permute-start.6 = (bf16[640,512]{1,0:T(8,128)(2,1)S(1)}, bf16[640,512]{1,0:T(8,128)(2,1)S(1)}, u32[]{:S(2)}, u32[]{:S(2)}) collective-permute-start(bf16[640,512]{1,0:T(8,128)(2,1)S(1)} %collective-permute-done.4.refs_9_), channel_id=1, source_target_pairs={{0,2},{1,3},{2,0},{3,1},{4,6},{5,7},{6,4},{7,5},{8,10},{9,11},{10,... | collective-permute-start | bytes 1966088 | tf_op jit(solution)/shard_map/ppermute | solution.py:351
  58.4 32.1 %collective-permute-start.10 = (bf16[640,512]{1,0:T(8,128)(2,1)S(1)}, bf16[640,512]{1,0:T(8,128)(2,1)S(1)}, u32[]{:S(2)}, u32[]{:S(2)}) collective-permute-start(bf16[640,512]{1,0:T(8,128)(2,1)S(1)} %collective-permute-done.7.refs_5_), channel_id=1, source_target_pairs={{0,4},{1,5},{2,6},{3,7},{4,12},{5,13},{6,14},{7,15},{8,0},{9,1},{1... | collective-permute-start | bytes 1966088 | tf_op jit(solution)/shard_map/ppermute | solution.py:351
  60.4 29.7 %collective-permute-start.17 = (bf16[2,576,128]{2,1,0:T(8,128)(2,1)S(1)}, bf16[2,576,128]{2,1,0:T(8,128)(2,1)S(1)}, u32[]{:S(2)}, u32[]{:S(2)}) collective-permute-start(bf16[2,576,128]{2,1,0:T(8,128)(2,1)S(1)} %slice.99), channel_id=1, source_target_pairs={{0,4},{1,5},{2,6},{3,7},{4,0},{5,1},{6,2},{7,3},{8,12},{9,13},{10,... | collective-permute-start | bytes 884744 | tf_op jit(solution)/shard_map/ppermute | solution.py:351
  74.3 28.1 %collective-permute-start.9 = (bf16[640,512]{1,0:T(8,128)(2,1)S(1)}, bf16[640,512]{1,0:T(8,128)(2,1)S(1)}, u32[]{:S(2)}, u32[]{:S(2)}) collective-permute-start(bf16[640,512]{1,0:T(8,128)(2,1)S(1)} %collective-permute-done.7.refs_5_), channel_id=1, source_target_pairs={{0,2},{1,3},{2,0},{3,1},{4,6},{5,7},{6,4},{7,5},{8,10},{9,11},{10,... | collective-permute-start | bytes 1966088 | tf_op jit(solution)/shard_map/ppermute | solution.py:351
  88.4 27.7 %collective-permute-start.5 = (bf16[768,512]{1,0:T(8,128)(2,1)S(1)}, bf16[768,512]{1,0:T(8,128)(2,1)S(1)}, u32[]{:S(2)}, u32[]{:S(2)}) collective-permute-start(bf16[768,512]{1,0:T(8,128)(2,1)S(1)} %pad_maximum_fusion), channel_id=1, source_target_pairs={{0,16},{1,17},{2,18},{3,19},{4,20},{5,21},{6,22},{7,23},{8,24},{9,... | collective-permute-start | bytes 2359304 | tf_op jit(solution)/shard_map/ppermute | solution.py:351
  90.1 36.9 %collective-permute-start.8 = (bf16[768,512]{1,0:T(8,128)(2,1)S(1)}, bf16[768,512]{1,0:T(8,128)(2,1)S(1)}, u32[]{:S(2)}, u32[]{:S(2)}) collective-permute-start(bf16[768,512]{1,0:T(8,128)(2,1)S(1)} %pad_maximum_fusion.1), channel_id=1, source_target_pairs={{0,16},{1,17},{2,18},{3,19},{4,20},{5,21},{6,22},{7,23},{8,24},{9,... | collective-permute-start | bytes 2359304 | tf_op jit(solution)/shard_map/ppermute | solution.py:351
  90.6 24.0 %collective-permute-start.12 = (bf16[640,512]{1,0:T(8,128)(2,1)S(1)}, bf16[640,512]{1,0:T(8,128)(2,1)S(1)}, u32[]{:S(2)}, u32[]{:S(2)}) collective-permute-start(bf16[640,512]{1,0:T(8,128)(2,1)S(1)} %collective-permute-done.10.refs_5_), channel_id=1, source_target_pairs={{0,2},{1,3},{2,0},{3,1},{4,6},{5,7},{6,4},{7,5},{8,10},{9,11},{10,... | collective-permute-start | bytes 1966088 | tf_op jit(solution)/shard_map/ppermute | solution.py:351
  102.4 6.0 %collective-permute-start.18 = (bf16[576,128]{1,0:T(8,128)(2,1)S(1)}, bf16[576,128]{1,0:T(8,128)(2,1)S(1)}, u32[]{:S(2)}, u32[]{:S(2)}) collective-permute-start(bf16[576,128]{1,0:T(8,128)(2,1)S(1)} %fusion.1), channel_id=1, source_target_pairs={{0,8},{1,9},{2,10},{3,11},{4,12},{5,13},{6,14},{7,15},{8,0},{9,1},... | collective-permute-start | bytes 442376 | tf_op jit(solution)/shard_map/ppermute | solution.py:351
  104.6 13.2 %copy-start.6 = (bf16[1024,128]{1,0:T(8,128)(2,1)S(1)}, bf16[1024,128]{1,0:T(8,128)(2,1)}, u32[]{:S(2)}) copy-start(bf16[1024,128]{1,0:T(8,128)(2,1)} %refs_4_.1) | copy-start | bytes 786436
  108.4 33.5 %collective-permute-start.11 = (bf16[768,512]{1,0:T(8,128)(2,1)S(1)}, bf16[768,512]{1,0:T(8,128)(2,1)S(1)}, u32[]{:S(2)}, u32[]{:S(2)}) collective-permute-start(bf16[768,512]{1,0:T(8,128)(2,1)S(1)} %pad_maximum_fusion.2), channel_id=1, source_target_pairs={{0,16},{1,17},{2,18},{3,19},{4,20},{5,21},{6,22},{7,23},{8,24},{9,... | collective-permute-start | bytes 2359304 | tf_op jit(solution)/shard_map/ppermute | solution.py:351
  114.5 1.4 collective-permute-start.1
  115.9 36.3 %collective-permute-start.19 = (f32[576,128]{1,0:T(8,128)}, f32[576,128]{1,0:T(8,128)}, u32[]{:S(2)}, u32[]{:S(2)}) collective-permute-start(f32[576,128]{1,0:T(8,128)} %fusion), channel_id=1, source_target_pairs={{0,1},{1,0},{2,3},{3,2},{4,5},{5,4},{6,7},{7,6},{8,9},{9,8},{10,11... | collective-permute-start | bytes 884744 | tf_op jit(solution)/shard_map/ppermute | solution.py:351
  116.0 33.8 %collective-permute-start.13 = (bf16[384,512]{1,0:T(8,128)(2,1)S(1)}, bf16[384,512]{1,0:T(8,128)(2,1)S(1)}, u32[]{:S(2)}, u32[]{:S(2)}) collective-permute-start(bf16[384,512]{1,0:T(8,128)(2,1)S(1)} %slice.77), channel_id=1, source_target_pairs={{0,16},{1,17},{2,18},{3,19},{4,20},{5,21},{6,22},{7,23},{8,24},{9,... | collective-permute-start | bytes 1179656 | tf_op jit(solution)/shard_map/ppermute | solution.py:351
  133.5 1.4 copy-start
  134.9 14.9 %copy-start.4 = (f32[320,128]{1,0:T(8,128)S(1)}, f32[320,128]{1,0:T(8,128)}, u32[]{:S(2)}) copy-start(f32[320,128]{1,0:T(8,128)} %constant.31.clone.tab_ref) | copy-start | bytes 491524
  152.1 5.7 %collective-permute-start.14 = (bf16[512,512]{1,0:T(8,128)(2,1)S(1)}, bf16[512,512]{1,0:T(8,128)(2,1)}, u32[]{:S(2)}, u32[]{:S(2)}) collective-permute-start(bf16[512,512]{1,0:T(8,128)(2,1)S(1)} %finish_1.1), channel_id=1, source_target_pairs={{0,1},{1,0},{2,3},{3,2},{4,5},{5,4},{6,7},{7,6},{8,9},{9,8},{10,11... | collective-permute-start | bytes 1572872 | tf_op jit(solution)/shard_map/ppermute | solution.py:351

commit v2 on v1

v2 whole, which is shorter than its diff:
```python
import functools

import jax
import jax.numpy as jnp
import numpy as np
from jax import lax
from jax.experimental import pallas as pl
from jax.experimental.pallas import tpu as pltpu
from jax.sharding import PartitionSpec as P

HEAD = 128
R = 16
BLK = 128
SEQ = 4096
ROPE_BASE = 500000.0
ADAPTER_SCALE = 2.0
ALL = ("groups", "node", "outer")
ANY = pl.BlockSpec(memory_space=pltpu.HBM)
VMEM_LIMIT = 56 * 1024 * 1024


def rope_constants():
    half = HEAD // 2
    frequency = ROPE_BASE ** (-2.0 * np.arange(half) / HEAD)
    inside = np.arange(BLK)[:, None] * frequency[None, :]
    starts = BLK * np.arange(SEQ // BLK)[:, None] * frequency[None, :]
    both = lambda t: np.concatenate((t, t), axis=1)
    return np.concatenate(
        (both(np.cos(inside)), both(np.sin(inside)), both(np.cos(starts)), both(np.sin(starts)))
    ).astype(np.float32)


def block_tables(tab_ref, c_row, s_row):
    c_in = tab_ref[0:BLK, :]
    s_in = tab_ref[BLK : 2 * BLK, :]
    cosine = c_in * c_row - s_in * s_row
    sine = s_in * c_row + c_in * s_row
    lane = lax.broadcasted_iota(jnp.int32, (1, HEAD), 1)
    return cosine, jnp.where(lane < HEAD // 2, -sine, sine)


def gradient_kernel(
    sc, tids, count, pos, tok_ref, a_ref, b_ref, cot_ref, tab_ref,
    low_ref, own_ref, sib_ref, grad, back, acc, piece,
):
    step = pl.program_id(0)
    slots = pl.num_programs(0)
    chunk = tok_ref.shape[1]
    kv = cot_ref.shape[1]
    blocks = tok_ref.shape[0] // BLK
    up_rows = kv // slots
    down_half, up_half = chunk // 2, up_rows // 2
    outer = sc[8]
    lane = lax.broadcasted_iota(jnp.int32, (1, HEAD), 1)

    def select(b):
        hit = jnp.logical_and(lane // R == tids[b], b < count[0])
        return jnp.where(hit, 1.0, 0.0).astype(jnp.float32)

    @pl.when(step == 0)
    def _():
        acc[...] = jnp.zeros_like(acc)
        for b in range(blocks):
            rows = slice(b * BLK, (b + 1) * BLK)
            start = pos[b * BLK] // BLK
            cosine, sine = block_tables(
                tab_ref,
                tab_ref[pl.ds(2 * BLK + start, 1), :],
                tab_ref[pl.ds(2 * BLK + SEQ // BLK + start, 1), :],
            )
            live = jnp.where(b < count[0], 1.0, 0.0).astype(jnp.float32)
            for h in range(kv // HEAD):
                cols = slice(h * HEAD, (h + 1) * HEAD)
                x = cot_ref[rows, cols].astype(jnp.float32)
                g = x * cosine - pltpu.roll(x, HEAD // 2, 1) * sine
                grad[rows, cols] = (live * g).astype(jnp.bfloat16)
            back[rows, :] = (
                jnp.dot(grad[rows, :], b_ref[...], preferred_element_type=jnp.float32) * select(b)
            ).astype(jnp.bfloat16)

    tok = tok_ref[...]
    acc[...] += jnp.dot(tok, a_ref[...], preferred_element_type=jnp.float32)
    piece[...] = ADAPTER_SCALE * lax.dot_general(
        tok, back[...], (((0,), (0,)), ((), ())), preferred_element_type=jnp.float32
    )
    own_ref[step, 0:down_half, :] = piece[pl.ds(outer * down_half, down_half), :]
    sib_ref[step, 0:down_half, :] = piece[
        pl.ds((1 - outer) * down_half, down_half), :
    ].astype(jnp.bfloat16)

    @pl.when(step == slots - 1)
    def _():
        for b in range(blocks):
            rows = slice(b * BLK, (b + 1) * BLK)
            low_ref[rows, :] = (acc[rows, :] * select(b)).astype(jnp.bfloat16)
        piece[0:kv, :] = ADAPTER_SCALE * lax.dot_general(
            grad[...], low_ref[...], (((0,), (0,)), ((), ())),
            preferred_element_type=jnp.float32,
        )
        for r in range(slots):
            base = sc[r] * up_rows
            own_ref[r, down_half:, :] = piece[pl.ds(base + outer * up_half, up_half), :]
            sib_ref[r, down_half:, :] = piece[
                pl.ds(base + (1 - outer) * up_half, up_half), :
            ].astype(jnp.bfloat16)


def product_kernel(held_from, crossed_from, first, joined, sc, *refs):
    refs = list(refs)
    take = lambda n: [refs.pop(0) for _ in range(n)]
    toks = take(2)
    weights = (take(len(held_from)), take(len(crossed_from)))
    given = None if first else (take(2), take(2))
    low_ref, second_ref = take(2) if first else (None, None)
    outs = (take(2), take(1 if joined else 2))
    tvs, wvs, tots = (take(2) for _ in range(3))
    sems, out_sems = refs
    deep, half = weights[0][-1].shape
    outer, plane = sc[8], sc[9]
    made, saved = [], []
    first_column = lambda side: pl.multiple_of((1 - plane if side else plane) * half, half)

    def load(src, dst):
        c = pltpu.make_async_copy(src, dst, sems.at[len(made)])
        c.start()
        made.append(c)
        return c

    columns = lambda i: pl.ds(pl.multiple_of((2 * sc[i] + outer) * deep, deep), deep)
    need = {}
    for k in range(2):
        for side, sources in enumerate((held_from, crossed_from)):
            todo = need[k, side] = []
            for i, at in enumerate(sources):
                part = slice(i * deep, (i + 1) * deep)
                if k == 0:
                    w = weights[side][i]
                    if w.shape[1] != half:
                        w = w.at[:, pl.ds(first_column(side), half)]
                    todo.append(load(w, wvs[side].at[part, :]))
                todo.append(load(toks[k].at[:, columns(at)], tvs[side].at[k, :, part]))
            if not first:
                todo.append(load(given[k][side], tots[side].at[k]))

    def start(k, side):
        if not first:
            return tots[side][k]
        if k:
            return 0.0
        return ADAPTER_SCALE * lax.dot_general(
            low_ref[...], second_ref[pl.ds(first_column(side), half), :], (((1,), (1,)), ((), ())),
            preferred_element_type=jnp.float32,
        )

    for k in range(2):
        for side in range(2):
            for c in need[k, side]:
                c.wait()
            tots[side][k] = start(k, side) + jnp.dot(
                tvs[side][k], wvs[side][...], preferred_element_type=jnp.float32
            )
            if k and joined:
                dst = outs[1][0].at[:, side * half : (side + 1) * half]
            else:
                dst = outs[k][side]
            c = pltpu.make_async_copy(tots[side].at[k], dst, out_sems.at[2 * k + side])
            c.start()
            saved.append(c)
    for c in saved:
        c.wait()


def rope_blocks(pos, count, tab_ref, tokens, write):
    starts = SEQ // BLK
    for b in range(tokens // BLK):
        at = pos[b * BLK] // BLK
        cosine, sine = block_tables(
            tab_ref, tab_ref[pl.ds(2 * BLK + at, 1), :], tab_ref[pl.ds(2 * BLK + starts + at, 1), :]
        )
        live = jnp.where(b < count[0], 1.0, 0.0).astype(jnp.float32)
        write(slice(b * BLK, (b + 1) * BLK), cosine * live, sine * live)


def rotate_heads(pre, cosine, sine, res, rows):
    for h in range(pre.shape[1] // HEAD):
        cols = slice(h * HEAD, (h + 1) * HEAD)
        x = pre[:, cols]
        res[rows, cols] = (x * cosine + pltpu.roll(x, HEAD // 2, 1) * sine).astype(jnp.bfloat16)


def load_both(sc, tok_ref, nodes, pieces, tv, wv, sems):
    deep = pieces[0].shape[0]
    chunk = 2 * deep
    outer = sc[8]
    copies = []
    for i, node in enumerate(nodes):
        at = pl.multiple_of(sc[node] * chunk, chunk)
        copies.append((tok_ref.at[:, pl.ds(at, chunk)], tv.at[:, i * chunk : (i + 1) * chunk]))
        for core, piece in ((outer, pieces[2 * i]), (1 - outer, pieces[2 * i + 1])):
            copies.append((piece, wv.at[pl.ds(pl.multiple_of(i * chunk + core * deep, deep), deep), :]))
    made = [pltpu.make_async_copy(src, dst, sems.at[i]) for i, (src, dst) in enumerate(copies)]
    for c in made:
        c.start()
    return made


def held_keys_kernel(
    sc, count, pos, tok_ref, mine_h, mine_c, given_ref, y3, y3_other, a3, a3_other, tab_ref,
    keys_ref, total_ref, tv, wv, vh, vc, vg, res, sems,
):
    half = vh.shape[1]
    chunk = tv.shape[1] // 2
    made = load_both(sc, tok_ref, (17, 13), (y3, y3_other, a3, a3_other), tv, wv, sems)
    made += [
        pltpu.make_async_copy(mine_h, vh, sems.at[6]),
        pltpu.make_async_copy(given_ref, vg, sems.at[7]),
        pltpu.make_async_copy(mine_c, vc, sems.at[8]),
    ]
    for c in made[6:]:
        c.start()
    for c in made:
        c.wait()
    vc[...] = (vc[...] + vg[:, half:]) + jnp.dot(
        tv[:, chunk:], wv[chunk:, :], preferred_element_type=jnp.float32
    )
    last = pltpu.make_async_copy(vc, total_ref, sems.at[10])
    last.start()

    def write(at, cosine, sine):
        pre = jnp.dot(tv[at, 0:chunk], wv[0:chunk, :], preferred_element_type=jnp.float32)
        rotate_heads(pre + (vh[at, :] + vg[at, 0:half]), cosine, sine, res, at)

    rope_blocks(pos, count, tab_ref, vh.shape[0], write)
    save = pltpu.make_async_copy(
        res, keys_ref.at[:, pl.ds(pl.multiple_of(sc[9] * half, half), half)], sems.at[9]
    )
    save.start()
    save.wait()
    last.wait()


def more_kernel(sc, tok_ref, total_ref, e1, e1_other, e2, e2_other, out_ref, tv, wv, vc, sems):
    made = load_both(sc, tok_ref, (15, 16), (e1, e1_other, e2, e2_other), tv, wv, sems)
    total = pltpu.make_async_copy(total_ref, vc, sems.at[6])
    total.start()
    for c in made:
        c.wait()
    total.wait()
    vc[...] += jnp.dot(tv[...], wv[...], preferred_element_type=jnp.float32)
    save = pltpu.make_async_copy(vc, out_ref, sems.at[7])
    save.start()
    save.wait()


def crossed_keys_kernel(
    sc, count, pos, tok_ref, total_ref, e3, e3_other, e0, e0_other, tab_ref, keys_ref, out_ref,
    tv, wv, vc, res, sems,
):
    half = vc.shape[1]
    made = load_both(sc, tok_ref, (17, 14), (e3, e3_other, e0, e0_other), tv, wv, sems)
    total = pltpu.make_async_copy(total_ref, vc, sems.at[6])
    total.start()
    for c in made:
        c.wait()
    total.wait()

    def write(at, cosine, sine):
        pre = vc[at, :] + jnp.dot(tv[at, :], wv[...], preferred_element_type=jnp.float32)
        rotate_heads(pre, cosine, sine, res, at)

    rope_blocks(pos, count, tab_ref, vc.shape[0], write)
    save = pltpu.make_async_copy(
        res, out_ref.at[:, pl.ds(pl.multiple_of((1 - sc[9]) * half, half), half)], sems.at[7]
    )
    save.start()
    save.wait()


class Routes:
    def __init__(self, mesh):
        self.groups, self.nodes, self.outers = (mesh.shape[a] for a in ALL)
        self.z = self.nodes // 2
        line = list(range(self.z))
        ring = line[:1] + line[1::2] + line[2::2][::-1]
        self.next = {ring[i]: ring[(i + 1) % self.z] for i in range(self.z)}
        self.prev = {v: k for k, v in self.next.items()}

    def pairs(self, f):
        at = lambda g, z, y, o: (g * self.nodes + 2 * z + y) * self.outers + o
        return [
            (at(g, z, y, o), at(*f(g, z, y, o)))
            for g in range(self.groups)
            for z in range(self.z)
            for y in range(2)
            for o in range(self.outers)
        ]

    def table(self):
        rows = []
        for _, n, o, g in [
            (0, n, o, g) for g in range(self.groups) for n in range(self.nodes) for o in range(self.outers)
        ]:
            z, y = divmod(n, 2)
            slot = [n ^ (((r >> 2) & 1) << 1 | ((r >> 1) & 1) << 2 | (r & 1)) for r in range(8)]
            from_z = [z]
            for _ in range(self.z - 1):
                from_z.append(self.prev[from_z[-1]])
            rows.append(
                slot + [o, g] + [2 * k + y for k in from_z] + [2 * k + 1 - y for k in from_z]
            )
        return np.array(rows, np.int32)


def call(kernel, name, shapes, in_specs, out_specs, scratch, args, grid=(), prefetch=1, aliases=None):
    return pl.pallas_call(
        kernel,
        out_shape=shapes,
        grid_spec=pltpu.PrefetchScalarGridSpec(
            num_scalar_prefetch=prefetch, grid=grid, in_specs=in_specs, out_specs=out_specs,
            scratch_shapes=scratch,
        ),
        compiler_params=pltpu.CompilerParams(vmem_limit_bytes=VMEM_LIMIT),
        cost_estimate=pl.CostEstimate(flops=1000, bytes_accessed=1024, transcendentals=0),
        input_output_aliases=aliases or {},
        name=name,
    )(*args)


def fast_body(
    routes, tokens, frozen_weight, down_adapter, second_adapter_weight, tenant_ids, block_counts, positions, cotangent
):
    bf16, f32 = jnp.bfloat16, jnp.float32
    rows, width = tokens.shape
    deep, kv = frozen_weight.shape
    nodes = routes.nodes
    chunk = 2 * deep
    half = kv // 2
    rank = down_adapter.shape[1]
    plane = lax.axis_index("groups")
    outer = lax.axis_index("outer")
    tab = jnp.asarray(rope_constants())

    send = lambda x, f: lax.ppermute(x, ALL, routes.pairs(f))
    to_core = lambda g, z, y, o: (g, z, y, 1 - o)
    to_x = lambda g, z, y, o: (1 - g, z, y, o)
    to_y = lambda g, z, y, o: (g, z, 1 - y, o)
    to_z = lambda g, z, y, o: (g, routes.next[z], y, o)
    to_z1 = lambda g, z, y, o: (g, z ^ 1, y, o)
    to_z2 = lambda g, z, y, o: (g, z ^ 2, y, o)
    fence = lambda *x: lax.optimization_barrier(x)
    vm = pl.BlockSpec(memory_space=pltpu.VMEM)
    dma = pltpu.SemaphoreType.DMA
    shape = jax.ShapeDtypeStruct

    def product(held, crossed, given=(), adapters=(), joined=False):
        kh, kc = len(held) * deep, len(crossed) * deep
        outs = [shape((rows, half), f32)] * 2
        outs += [shape((rows, kv), f32)] if joined else outs
        return call(
            functools.partial(
                product_kernel, [i for _, i in held], [i for _, i in crossed], not given, joined
            ),
            "products", outs,
            [ANY] * (2 + len(held) + len(crossed) + len(given)) + [vm] * len(adapters), [ANY] * len(outs),
            [
                pltpu.VMEM((2, rows, kh), bf16), pltpu.VMEM((2, rows, kc), bf16),
                pltpu.VMEM((kh, half), bf16), pltpu.VMEM((kc, half), bf16),
                pltpu.VMEM((2, rows, half), f32), pltpu.VMEM((2, rows, half), f32),
                dma((3 * len(held) + 3 * len(crossed) + 4,)), dma((4,)),
            ],
            (sc, tokens, sib_tokens, *[w for w, _ in held], *[w for w, _ in crossed], *given, *adapters),
        )

    z0 = lax.dynamic_slice(frozen_weight, (0, plane * half), (deep, half))
    z0, own_tokens, table = fence(z0, tokens, jnp.asarray(routes.table()))
    sc = lax.dynamic_slice(table, (lax.axis_index(ALL), 0), (1, table.shape[1]))[0]
    z1 = send(z0, to_z)
    y0 = send(z0, to_y)
    sib_tokens = send(own_tokens, to_core)
    slot_rows = chunk // 2 + kv // nodes // 2
    low, own, sib = call(
        gradient_kernel, "adapter_gradients",
        (
            shape((rows, rank), bf16),
            shape((nodes, slot_rows, rank), f32),
            shape((nodes, slot_rows, rank), bf16),
        ),
        [
            pl.BlockSpec((rows, chunk), lambda i, sc, *_: (0, sc[i])),
            pl.BlockSpec((chunk, rank), lambda i, sc, *_: (sc[i], 0)),
            pl.BlockSpec((kv, rank), lambda i, *_: (0, 0)),
            pl.BlockSpec((rows, kv), lambda i, *_: (0, 0)),
            pl.BlockSpec(tab.shape, lambda i, *_: (0, 0)),
        ],
        (
            pl.BlockSpec((rows, rank), lambda i, *_: (0, 0)),
            pl.BlockSpec((nodes, slot_rows, rank), lambda i, *_: (0, 0, 0)),
            pl.BlockSpec((nodes, slot_rows, rank), lambda i, *_: (0, 0, 0)),
        ),
        [
            pltpu.VMEM((rows, kv), bf16),
            pltpu.VMEM((rows, rank), bf16),
            pltpu.VMEM((rows, rank), f32),
            pltpu.VMEM((max(chunk, kv), rank), f32),
        ],
        (sc, tenant_ids, block_counts, positions, tokens, down_adapter, second_adapter_weight, cotangent, tab),
        grid=(nodes,), prefetch=4,
    )
    z1, y0, low, own, sib, sib_tokens = fence(z1, y0, low, own, sib, sib_tokens)

    z2 = send(z1, to_z)
    y1 = send(z1, to_y)
    a1 = send(z1, to_x)
    other = send(sib, to_core)
    totals = product(
        ((frozen_weight, 10), (y0, 14), (z1, 11)), ((frozen_weight, 10),), adapters=(low, second_adapter_weight)
    )
    z2, y1, a1, other, *totals = fence(z2, y1, a1, other, *totals)

    z3 = send(z2, to_z)
    y2 = send(z2, to_y)
    a2 = send(z2, to_x)
    s = own + other.astype(f32)
    totals = product(((y1, 15), (z2, 12)), ((a1, 11),), given=totals)
    z3, y2, a2, s, *totals = fence(z3, y2, a2, s, *totals)

    y3 = send(z3, to_y)
    a3 = send(z3, to_x)
    got = send(s[4:].astype(bf16), to_z1)
    mine_h, mine_c, theirs = product(((y2, 16), (z3, 13)), ((a2, 12),), given=totals, joined=True)
    y3, a3, got, mine_h, mine_c, theirs = fence(y3, a3, got, mine_h, mine_c, theirs)

    given, y3_other, a3_other = send(theirs, to_core), send(y3, to_core), send(a3, to_core)
    e1 = send(y1, to_x)
    e2 = send(a2, to_y)
    s = s[:4] + got.astype(f32)
    got = send(s[2:].astype(bf16), to_z2)
    own_space = [
        pltpu.VMEM((rows, 2 * chunk), bf16), pltpu.VMEM((2 * chunk, half), bf16), pltpu.VMEM((rows, half), f32),
    ]
    keys, total = call(
        held_keys_kernel, "held_keys", [shape((rows, kv), bf16), shape((rows, half), f32)],
        [ANY] * 8 + [vm], [ANY, ANY],
        own_space + [
            pltpu.VMEM((rows, half), f32), pltpu.VMEM((rows, kv), f32), pltpu.VMEM((rows, half), bf16), dma((11,)),
        ],
        (sc, block_counts, positions, tokens, mine_h, mine_c, given, y3, y3_other, a3, a3_other, tab),
        prefetch=3,
    )
    y3, weight, total = fence(y3, frozen_weight, total)
    e3 = send(y3, to_x)
    e0 = send(lax.dynamic_slice(weight, (0, (1 - plane) * half), (deep, half)), to_y)
    e1, e2, got, total = fence(e1, e2, got, total)

    s = s[:2] + got.astype(f32)
    got = send(s[1].astype(bf16), to_y)
    total = call(
        more_kernel, "more_products", shape((rows, half), f32), [ANY] * 6, ANY, own_space + [dma((8,))],
        (sc, tokens, total, e1, send(e1, to_core), e2, send(e2, to_core)),
    )
    e3, e0, got, total = fence(e3, e0, got, total)

    s = s[0] + got.astype(f32)
    t = send(s, to_core)
    keys = call(
        crossed_keys_kernel, "crossed_keys", shape((rows, kv), bf16), [ANY] * 6 + [vm, ANY], ANY,
        own_space + [pltpu.VMEM((rows, half), bf16), dma((8,))],
        (sc, block_counts, positions, tokens, total, e3, send(e3, to_core), e0, send(e0, to_core), tab, keys),
        prefetch=3, aliases={10: 0},
    )
    down_rows = chunk // 2
    lower, upper = jnp.where(outer == 0, s, t), jnp.where(outer == 0, t, s)
    down = jnp.concatenate((lower[:down_rows], upper[:down_rows]))
    up = jnp.concatenate((lower[down_rows:], upper[down_rows:]))
    return keys, down, up


def rope_tables(positions):
    half_head = HEAD // 2
    frequency = ROPE_BASE ** (-2.0 * jnp.arange(half_head, dtype=jnp.float32) / HEAD)
    angle = positions.astype(jnp.float32)[:, None] * frequency[None, :]
    return (jnp.cos(angle), jnp.sin(angle))


def rotate(field, cosine, sine, orient):
    rows = field.shape[0]
    shaped = field.reshape(rows, -1, 2, HEAD // 2)
    first = shaped[:, :, 0]
    second = shaped[:, :, 1]
    cos_b = cosine[:, None, :]
    sin_b = orient * sine[:, None, :]
    out_first = first * cos_b - second * sin_b
    out_second = second * cos_b + first * sin_b
    return jnp.stack((out_first, out_second), axis=2).reshape(rows, -1)


def plain_body(
    tokens, frozen_weight, down_adapter, second_adapter_weight, tenant_ids, block_counts, positions, cotangent
):
    token_rows = tokens.shape[0]
    block_total = tenant_ids.shape[0]
    block_rows = token_rows // block_total
    width_cols = down_adapter.shape[1]
    live_blocks = (jnp.arange(block_total, dtype=jnp.int32) < block_counts[0]).astype(jnp.float32)
    live_rows = jnp.repeat(live_blocks, block_rows)[:, None]
    column_tenant = jnp.arange(width_cols, dtype=jnp.int32) // R
    select_blocks = (tenant_ids[:, None] == column_tenant[None, :]).astype(
        jnp.float32
    ) * live_blocks[:, None]
    select = jnp.repeat(select_blocks, block_rows, axis=0)
    lowrank_hidden = (
        jnp.dot(tokens, down_adapter, preferred_element_type=jnp.float32) * select
    ).astype(jnp.bfloat16)
    frozen_output = jnp.dot(
        tokens,
        lax.all_gather(frozen_weight, ("node", "outer"), axis=0, tiled=True),
        preferred_element_type=jnp.float32,
    )
    adapter_output = lax.dot_general(
        lowrank_hidden,
        second_adapter_weight,
        (((1,), (1,)), ((), ())),
        preferred_element_type=jnp.float32,
    )
    unrotated_keys = frozen_output + ADAPTER_SCALE * adapter_output
    cosine, sine = rope_tables(positions)
    keys = (live_rows * rotate(unrotated_keys, cosine, sine, 1.0)).astype(jnp.bfloat16)
    output_gradient = (
        live_rows * rotate(cotangent.astype(jnp.float32), cosine, sine, -1.0)
    ).astype(jnp.bfloat16)
    backward_gradient = (
        jnp.dot(output_gradient, second_adapter_weight, preferred_element_type=jnp.float32) * select
    ).astype(jnp.bfloat16)
    down_product = ADAPTER_SCALE * lax.dot_general(
        tokens, backward_gradient, (((0,), (0,)), ((), ())), preferred_element_type=jnp.float32
    )
    up_product = ADAPTER_SCALE * lax.dot_general(
        output_gradient,
        lowrank_hidden,
        (((0,), (0,)), ((), ())),
        preferred_element_type=jnp.float32,
    )
    shares = (
        lax.psum_scatter(down_product, "node", scatter_dimension=0, tiled=True),
        lax.psum_scatter(up_product, "node", scatter_dimension=0, tiled=True),
    )
    down_adapter_gradient, up_adapter_gradient = lax.psum((shares[0], shares[1]), "outer")
    return (keys, down_adapter_gradient, up_adapter_gradient)


def solution(mesh):
    placed = (
        P(("groups", "node", "outer"), None),
        P(("node", "outer"), None),
        P(),
        P(),
        P(("groups", "node", "outer")),
        P(("groups", "node", "outer")),
        P(("groups", "node", "outer")),
        P(("groups", "node", "outer"), None),
    )
    routed = tuple(mesh.shape[a] for a in ALL) == (2, 8, 2)
    return jax.shard_map(
        functools.partial(fast_body, Routes(mesh)) if routed else plain_body,
        mesh=mesh,
        in_specs=placed,
        out_specs=(
            P(("groups", "node", "outer"), None),
            P(("groups", "node"), None),
            P(("groups", "node"), None),
        ),
        check_vma=False,
    )
```

time: 177 us -> 119 us (0.67)
  waiting for transfers between devices: 77.3 us -> 26.6 us
  Pallas kernels: 59.6 us -> 52.8 us
  starting transfers between devices: 23 us -> 26.3 us
  other arithmetic: 5.48 us -> 2.84 us
    ppermute x20 -> x27, waiting for transfers between devices: 77.3 us -> 26.6 us  [fast_body(): send = lambda x, f: lax.ppermute(x, ALL, routes.pairs(f))]
    pallas_call x8 -> x7, Pallas kernels: 59.6 us -> 52.8 us  [call(): pl.pallas_call(kernel, out_shape=shapes, grid_spec=pltpu.PrefetchScalarGr...]
    ppermute x20 -> x27, starting transfers between devices: 23 us -> 26.3 us  [fast_body(): send = lambda x, f: lax.ppermute(x, ALL, routes.pairs(f))]
    unnamed x20 -> x38, local copies, waits for them, and re-layouts: 6.17 us -> 4.74 us
  transfers between devices with their start and end apart: 20 -> 27, of which waited for: 10 -> 11; matrix products, arithmetic and copies ran while one was open for 4% -> 4% of each run, Pallas kernels for 24% -> 39%
where the time goes in v2:
time: 119 us; the launch traced here: 118 us
  Pallas kernels  52.8 us (44%)
  waiting for transfers between devices  26.6 us (22%)
  starting transfers between devices  26.3 us (22%)
  local copies, waits for them, and re-layouts  8.01 us (7%)
  other arithmetic  2.84 us (2%)
  between operations  1.73 us (1%)
    pallas_call x7, Pallas kernels, call(): pl.pallas_call(kernel, out_shape=shapes, grid_spec=pltpu.PrefetchScalarGr...  52.8 us
    ppermute x27, waiting for transfers between devices, fast_body(): send = lambda x, f: lax.ppermute(x, ALL, routes.pairs(f))  26.6 us
    ppermute x27, starting transfers between devices, fast_body(): send = lambda x, f: lax.ppermute(x, ALL, routes.pairs(f))  26.3 us
    unnamed x38, local copies, waits for them, and re-layouts  4.74 us
  transfers between devices with their start and end apart: 27, of which 11 were waited for; matrix products, arithmetic and copies ran while one was open for 4% of the time, Pallas kernels for 39%

profile of v2, /device:TPU:0, one launch (start us, length us, event | category | flops | bytes accessed | tf_op | source)
XLA Modules:
  0.0 118.3 jit_solution(8594126882420584186)
XLA Ops:
  0.6 1.1 constant_dynamic-slice_fusion.2
  2.2 2.6 %collective-permute-start = (bf16[512,512]{1,0:T(8,128)(2,1)S(1)}, bf16[512,512]{1,0:T(8,128)(2,1)S(1)}, u32[]{:S(2)}, u32[]{:S(2)}) collective-permute-start(bf16[512,512]{1,0:T(8,128)(2,1)S(1)} %constant_dynamic-slice_fusion.2), channel_id=1, source_target_pairs={{0,4},{1,5},{2,6},{3,7},{4,12},{5,13},{6,14},{7,15},{8,0},{9,1},{1... | collective-permute-start | bytes 1572872 | tf_op jit(solution)/shard_map/ppermute | solution.py:343
  4.9 1.5 %collective-permute-start.1 = (bf16[512,512]{1,0:T(8,128)(2,1)S(1)}, bf16[512,512]{1,0:T(8,128)(2,1)S(1)}, u32[]{:S(2)}, u32[]{:S(2)}) collective-permute-start(bf16[512,512]{1,0:T(8,128)(2,1)S(1)} %constant_dynamic-slice_fusion.2), channel_id=1, source_target_pairs={{0,2},{1,3},{2,0},{3,1},{4,6},{5,7},{6,4},{7,5},{8,10},{9,11},{10,... | collective-permute-start | bytes 1572872 | tf_op jit(solution)/shard_map/ppermute | solution.py:343
  7.1 1.2 %fusion.2.sc = s32[18]{0:T(128)} fusion(s32[32,18]{1,0:T(8,128)} %constant.31.clone, s32[]{:T(128)S(6)} %select_n.22), kind=kLoop, calls=%fused_computation.16 | loop fusion | bytes 148 | tf_op jit(solution)/shard_map/squeeze | solution.py:376
  8.3 13.8 %adapter_gradients.1 = (bf16[512,128]{1,0:T(8,128)(2,1)}, f32[8,576,128]{2,1,0:T(8,128)}, bf16[8,576,128]{2,1,0:T(8,128)(2,1)}) custom-call(s32[18]{0:T(128)} %fusion.2.sc, s32[4]{0:T(128)} %tids.1, s32[1]{0:T(128)S(6)} %copy.15.count, s32[512]{0:T(512)} %pos.5, bf16[512,8192]{1,0:T(8,128)(2,1)} %tok_ref.7, bf16[8192,128]{1,0:T(8,128)(2,1)} %a_ref.1, ...), custom_call_target="tpu_custom_call" | custom-call | flops 1000 | bytes 1024 | tf_op jit(solution)/shard_map/adapter_gradients/pallas_call | solution.py:315
  22.2 2.6 %collective-permute-start.3 = (bf16[512,512]{1,0:T(8,128)(2,1)S(1)}, bf16[512,512]{1,0:T(8,128)(2,1)S(1)}, u32[]{:S(2)}, u32[]{:S(2)}) collective-permute-start(bf16[512,512]{1,0:T(8,128)(2,1)S(1)} %collective-permute-done.refs_4_), channel_id=1, source_target_pairs={{0,4},{1,5},{2,6},{3,7},{4,12},{5,13},{6,14},{7,15},{8,0},{9,1},{1... | collective-permute-start | bytes 1572872 | tf_op jit(solution)/shard_map/ppermute | solution.py:343
  25.3 1.5 %collective-permute-start.5 = (bf16[512,512]{1,0:T(8,128)(2,1)S(1)}, bf16[512,512]{1,0:T(8,128)(2,1)S(1)}, u32[]{:S(2)}, u32[]{:S(2)}) collective-permute-start(bf16[512,512]{1,0:T(8,128)(2,1)S(1)} %collective-permute-done.refs_4_), channel_id=1, source_target_pairs={{0,16},{1,17},{2,18},{3,19},{4,20},{5,21},{6,22},{7,23},{8,24},{9,... | collective-permute-start | bytes 1572872 | tf_op jit(solution)/shard_map/ppermute | solution.py:343
  26.8 7.8 %products.3 = (f32[512,512]{1,0:T(8,128)}, f32[512,512]{1,0:T(8,128)}, f32[512,512]{1,0:T(8,128)}, f32[512,512]{1,0:T(8,128)}) custom-call(s32[18]{0:T(128)} %fusion.2.sc, bf16[512,8192]{1,0:T(8,128)(2,1)} %tok_ref.7, bf16[512,8192]{1,0:T(8,128)(2,1)} %collective-permute-done.2.refs_1_, bf16[512,1024]{1,0:T(8,128)(2,1)} %refs_5_.1, ...), custom_call_target="tpu_custom_call" | custom-call | flops 1000 | bytes 1024 | tf_op jit(solution)/shard_map/products/pallas_call | solution.py:315
  34.6 2.8 %collective-permute-done.3.refs_3_ = bf16[512,512]{1,0:T(8,128)(2,1)S(1)} collective-permute-done((bf16[512,512]{1,0:T(8,128)(2,1)S(1)}, bf16[512,512]{1,0:T(8,128)(2,1)S(1)}, u32[]{:S(2)}, u32[]{:S(2)}) %collective-permute-start.3) | collective-permute-done | bytes 524320 | tf_op jit(solution)/shard_map/ppermute | solution.py:343
  37.4 1.5 %collective-permute-done.4.refs_2_ = bf16[512,512]{1,0:T(8,128)(2,1)} collective-permute-done((bf16[512,512]{1,0:T(8,128)(2,1)S(1)}, bf16[512,512]{1,0:T(8,128)(2,1)}, u32[]{:S(2)}, u32[]{:S(2)}) %collective-permute-start.4) | collective-permute-done | bytes 524320 | tf_op jit(solution)/shard_map/ppermute | solution.py:343
  39.7 1.5 %collective-permute-start.8 = (bf16[512,512]{1,0:T(8,128)(2,1)S(1)}, bf16[512,512]{1,0:T(8,128)(2,1)S(1)}, u32[]{:S(2)}, u32[]{:S(2)}) collective-permute-start(bf16[512,512]{1,0:T(8,128)(2,1)S(1)} %collective-permute-done.3.refs_3_), channel_id=1, source_target_pairs={{0,2},{1,3},{2,0},{3,1},{4,6},{5,7},{6,4},{7,5},{8,10},{9,11},{10,... | collective-permute-start | bytes 1572872 | tf_op jit(solution)/shard_map/ppermute | solution.py:343
  41.2 1.5 %collective-permute-start.9 = (bf16[512,512]{1,0:T(8,128)(2,1)S(1)}, bf16[512,512]{1,0:T(8,128)(2,1)S(1)}, u32[]{:S(2)}, u32[]{:S(2)}) collective-permute-start(bf16[512,512]{1,0:T(8,128)(2,1)S(1)} %collective-permute-done.3.refs_3_), channel_id=1, source_target_pairs={{0,16},{1,17},{2,18},{3,19},{4,20},{5,21},{6,22},{7,23},{8,24},{9,... | collective-permute-start | bytes 1572872 | tf_op jit(solution)/shard_map/ppermute | solution.py:343
  42.7 6.1 %products.4 = (f32[512,512]{1,0:T(8,128)}, f32[512,512]{1,0:T(8,128)}, f32[512,512]{1,0:T(8,128)}, f32[512,512]{1,0:T(8,128)}) custom-call(s32[18]{0:T(128)} %fusion.2.sc, bf16[512,8192]{1,0:T(8,128)(2,1)} %tok_ref.7, bf16[512,8192]{1,0:T(8,128)(2,1)} %collective-permute-done.2.refs_1_, bf16[512,512]{1,0:T(8,128)(2,1)} %collective-permute-done.4.refs_2_, ...), custom_call_target="tpu_custom_call" | custom-call | flops 1000 | bytes 1024 | tf_op jit(solution)/shard_map/products/pallas_call | solution.py:315
  49.0 4.2 %collective-permute-done.7.refs_3_ = bf16[512,512]{1,0:T(8,128)(2,1)S(1)} collective-permute-done((bf16[512,512]{1,0:T(8,128)(2,1)S(1)}, bf16[512,512]{1,0:T(8,128)(2,1)S(1)}, u32[]{:S(2)}, u32[]{:S(2)}) %collective-permute-start.7) | collective-permute-done | bytes 524320 | tf_op jit(solution)/shard_map/ppermute | solution.py:343
  54.3 1.5 %collective-permute-start.10 = (bf16[512,512]{1,0:T(8,128)(2,1)S(1)}, bf16[512,512]{1,0:T(8,128)(2,1)S(1)}, u32[]{:S(2)}, u32[]{:S(2)}) collective-permute-start(bf16[512,512]{1,0:T(8,128)(2,1)S(1)} %collective-permute-done.7.refs_3_), channel_id=1, source_target_pairs={{0,2},{1,3},{2,0},{3,1},{4,6},{5,7},{6,4},{7,5},{8,10},{9,11},{10,... | collective-permute-start | bytes 1572872 | tf_op jit(solution)/shard_map/ppermute | solution.py:343
  55.8 1.5 %collective-permute-start.11 = (bf16[512,512]{1,0:T(8,128)(2,1)S(1)}, bf16[512,512]{1,0:T(8,128)(2,1)}, u32[]{:S(2)}, u32[]{:S(2)}) collective-permute-start(bf16[512,512]{1,0:T(8,128)(2,1)S(1)} %collective-permute-done.7.refs_3_), channel_id=1, source_target_pairs={{0,16},{1,17},{2,18},{3,19},{4,20},{5,21},{6,22},{7,23},{8,24},{9,... | collective-permute-start | bytes 1572872 | tf_op jit(solution)/shard_map/ppermute | solution.py:343
  57.3 6.1 %products.5 = (f32[512,512]{1,0:T(8,128)}, f32[512,512]{1,0:T(8,128)}, f32[512,1024]{1,0:T(8,128)}) custom-call(s32[18]{0:T(128)} %fusion.2.sc, bf16[512,8192]{1,0:T(8,128)(2,1)} %tok_ref.7, bf16[512,8192]{1,0:T(8,128)(2,1)} %collective-permute-done.2.refs_1_, bf16[512,512]{1,0:T(8,128)(2,1)} %copy-done.13, bf16[512,512]{1,0:T(8,128)(2,1)} %copy-done.11, ...), custom_call_target="tpu_custom_call" | custom-call | flops 1000 | bytes 1024 | tf_op jit(solution)/shard_map/products/pallas_call | solution.py:315
  63.4 2.7 %collective-permute-done.10.y3 = bf16[512,512]{1,0:T(8,128)(2,1)S(1)} collective-permute-done((bf16[512,512]{1,0:T(8,128)(2,1)S(1)}, bf16[512,512]{1,0:T(8,128)(2,1)S(1)}, u32[]{:S(2)}, u32[]{:S(2)}) %collective-permute-start.10) | collective-permute-done | bytes 524320 | tf_op jit(solution)/shard_map/ppermute | solution.py:343
  66.1 1.3 %collective-permute-done.11.a3 = bf16[512,512]{1,0:T(8,128)(2,1)} collective-permute-done((bf16[512,512]{1,0:T(8,128)(2,1)S(1)}, bf16[512,512]{1,0:T(8,128)(2,1)}, u32[]{:S(2)}, u32[]{:S(2)}) %collective-permute-start.11) | collective-permute-done | bytes 524320 | tf_op jit(solution)/shard_map/ppermute | solution.py:343
  67.9 1.5 %collective-permute-start.18 = (bf16[512,512]{1,0:T(8,128)(2,1)}, bf16[512,512]{1,0:T(8,128)(2,1)}, u32[]{:S(2)}, u32[]{:S(2)}) collective-permute-start(bf16[512,512]{1,0:T(8,128)(2,1)} %collective-permute-done.4.refs_2_), channel_id=1, source_target_pairs={{0,16},{1,17},{2,18},{3,19},{4,20},{5,21},{6,22},{7,23},{8,24},{9,... | collective-permute-start | bytes 1572872 | tf_op jit(solution)/shard_map/ppermute | solution.py:343
  70.9 1.7 %collective-permute-done.14.y3_other = bf16[512,512]{1,0:T(8,128)(2,1)S(1)} collective-permute-done((bf16[512,512]{1,0:T(8,128)(2,1)S(1)}, bf16[512,512]{1,0:T(8,128)(2,1)S(1)}, u32[]{:S(2)}, u32[]{:S(2)}) %collective-permute-start.14) | collective-permute-done | bytes 524320 | tf_op jit(solution)/shard_map/ppermute | solution.py:343
  73.5 1.6 %collective-permute-start.20 = (bf16[2,576,128]{2,1,0:T(8,128)(2,1)}, bf16[2,576,128]{2,1,0:T(8,128)(2,1)}, u32[]{:S(2)}, u32[]{:S(2)}) collective-permute-start(bf16[2,576,128]{2,1,0:T(8,128)(2,1)} %slice.63), channel_id=1, source_target_pairs={{0,8},{1,9},{2,10},{3,11},{4,12},{5,13},{6,14},{7,15},{8,0},{9,1},... | collective-permute-start | bytes 884744 | tf_op jit(solution)/shard_map/ppermute | solution.py:343
  75.1 1.3 %copy-done.2 = f32[512,1024]{1,0:T(8,128)} copy-done((f32[512,1024]{1,0:T(8,128)}, f32[512,1024]{1,0:T(8,128)S(1)}, u32[]{:S(2)}) %copy-start.2) | copy-done | bytes 2097176
  76.4 7.3 %held_keys.1 = (bf16[512,1024]{1,0:T(8,128)(2,1)}, f32[512,512]{1,0:T(8,128)}) custom-call(s32[18]{0:T(128)} %fusion.2.sc, s32[1]{0:T(128)S(6)} %copy.15.count, s32[512]{0:T(512)} %pos.5, bf16[512,8192]{1,0:T(8,128)(2,1)} %tok_ref.7, f32[512,512]{1,0:T(8,128)} %get-tuple-element.101.mine_h, f32[512,512]{1,0:T(8,128)} %get-tuple-element.102.mine_c, ...), custom_call_target="tpu_custom_call" | custom-call | flops 1000 | bytes 1024 | tf_op jit(solution)/shard_map/held_keys/pallas_call | solution.py:315
  83.7 6.1 %collective-permute-done.20 = bf16[2,576,128]{2,1,0:T(8,128)(2,1)} collective-permute-done((bf16[2,576,128]{2,1,0:T(8,128)(2,1)}, bf16[2,576,128]{2,1,0:T(8,128)(2,1)}, u32[]{:S(2)}, u32[]{:S(2)}) %collective-permute-start.20) | collective-permute-done | bytes 294944 | tf_op jit(solution)/shard_map/ppermute | solution.py:343
  90.8 2.2 %collective-permute-start.16 = (bf16[512,512]{1,0:T(8,128)(2,1)S(1)}, bf16[512,512]{1,0:T(8,128)(2,1)S(1)}, u32[]{:S(2)}, u32[]{:S(2)}) collective-permute-start(bf16[512,512]{1,0:T(8,128)(2,1)S(1)} %copy-done.4), channel_id=1, source_target_pairs={{0,16},{1,17},{2,18},{3,19},{4,20},{5,21},{6,22},{7,23},{8,24},{9,... | collective-permute-start | bytes 1572872 | tf_op jit(solution)/shard_map/ppermute | solution.py:343
  93.1 1.0 slice_add_fusion
  94.1 1.4 %collective-permute-start.21 = (bf16[576,128]{1,0:T(8,128)(2,1)S(1)}, bf16[576,128]{1,0:T(8,128)(2,1)S(1)}, u32[]{:S(2)}, u32[]{:S(2)}) collective-permute-start(bf16[576,128]{1,0:T(8,128)(2,1)S(1)} %fusion.1), channel_id=1, source_target_pairs={{0,2},{1,3},{2,0},{3,1},{4,6},{5,7},{6,4},{7,5},{8,10},{9,11},{10,... | collective-permute-start | bytes 442376 | tf_op jit(solution)/shard_map/ppermute | solution.py:343
  97.1 5.5 %more_products.1.total_ref = f32[512,512]{1,0:T(8,128)} custom-call(s32[18]{0:T(128)} %fusion.2.sc, bf16[512,8192]{1,0:T(8,128)(2,1)} %tok_ref.7, f32[512,512]{1,0:T(8,128)} %get-tuple-element.111.total_ref, bf16[512,512]{1,0:T(8,128)(2,1)} %collective-permute-done.18.e1, bf16[512,512]{1,0:T(8,128)(2,1)} %copy-done.17, ...), custom_call_target="tpu_custom_call" | custom-call | flops 1000 | bytes 1024 | tf_op jit(solution)/shard_map/more_products/pallas_call | solution.py:315
  102.6 4.9 %collective-permute-done.21 = bf16[576,128]{1,0:T(8,128)(2,1)S(1)} collective-permute-done((bf16[576,128]{1,0:T(8,128)(2,1)S(1)}, bf16[576,128]{1,0:T(8,128)(2,1)S(1)}, u32[]{:S(2)}, u32[]{:S(2)}) %collective-permute-start.21) | collective-permute-done | bytes 147488 | tf_op jit(solution)/shard_map/ppermute | solution.py:343
  108.2 1.0 collective-permute-done.26
  111.8 6.3 %crossed_keys.1 = bf16[512,1024]{1,0:T(8,128)(2,1)} custom-call(s32[18]{0:T(128)} %fusion.2.sc, s32[1]{0:T(128)S(6)} %copy.15.count, s32[512]{0:T(512)} %pos.5, bf16[512,8192]{1,0:T(8,128)(2,1)} %tok_ref.7, f32[512,512]{1,0:T(8,128)} %more_products.1.total_ref, bf16[512,512]{1,0:T(8,128)(2,1)} %copy-done.7, ...), custom_call_target="tpu_custom_call", output_to_operand_aliasing={{}: (10, {})} | custom-call | flops 1000 | bytes 1024 | tf_op jit(solution)/shard_map/crossed_keys/pallas_call | solution.py:315
  (84 shorter events, 11.9 us)
Async XLA Ops:
  1.7 20.4 %collective-permute-start.2 = (bf16[512,8192]{1,0:T(8,128)(2,1)}, bf16[512,8192]{1,0:T(8,128)(2,1)}, u32[]{:S(2)}, u32[]{:S(2)}) collective-permute-start(bf16[512,8192]{1,0:T(8,128)(2,1)} %tok_ref.7), channel_id=1, source_target_pairs={{0,1},{1,0},{2,3},{3,2},{4,5},{5,4},{6,7},{7,6},{8,9},{9,8},{10,11... | collective-permute-start | bytes 25165832 | tf_op jit(solution)/shard_map/ppermute | solution.py:343
  2.2 19.8 %collective-permute-start = (bf16[512,512]{1,0:T(8,128)(2,1)S(1)}, bf16[512,512]{1,0:T(8,128)(2,1)S(1)}, u32[]{:S(2)}, u32[]{:S(2)}) collective-permute-start(bf16[512,512]{1,0:T(8,128)(2,1)S(1)} %constant_dynamic-slice_fusion.2), channel_id=1, source_target_pairs={{0,4},{1,5},{2,6},{3,7},{4,12},{5,13},{6,14},{7,15},{8,0},{9,1},{1... | collective-permute-start | bytes 1572872 | tf_op jit(solution)/shard_map/ppermute | solution.py:343
  4.9 17.2 %collective-permute-start.1 = (bf16[512,512]{1,0:T(8,128)(2,1)S(1)}, bf16[512,512]{1,0:T(8,128)(2,1)S(1)}, u32[]{:S(2)}, u32[]{:S(2)}) collective-permute-start(bf16[512,512]{1,0:T(8,128)(2,1)S(1)} %constant_dynamic-slice_fusion.2), channel_id=1, source_target_pairs={{0,2},{1,3},{2,0},{3,1},{4,6},{5,7},{6,4},{7,5},{8,10},{9,11},{10,... | collective-permute-start | bytes 1572872 | tf_op jit(solution)/shard_map/ppermute | solution.py:343
  22.0 4.8 %copy-start.8 = (bf16[512,512]{1,0:T(8,128)(2,1)}, bf16[512,512]{1,0:T(8,128)(2,1)S(1)}, u32[]{:S(2)}) copy-start(bf16[512,512]{1,0:T(8,128)(2,1)S(1)} %collective-permute-done.refs_4_) | copy-start | bytes 1572868
  22.1 16.9 %collective-permute-start.6 = (bf16[8,576,128]{2,1,0:T(8,128)(2,1)}, bf16[8,576,128]{2,1,0:T(8,128)(2,1)S(1)}, u32[]{:S(2)}, u32[]{:S(2)}) collective-permute-start(bf16[8,576,128]{2,1,0:T(8,128)(2,1)} %get-tuple-element.68), channel_id=1, source_target_pairs={{0,1},{1,0},{2,3},{3,2},{4,5},{5,4},{6,7},{7,6},{8,9},{9,8},{10,11... | collective-permute-start | bytes 3538952 | tf_op jit(solution)/shard_map/ppermute | solution.py:343
  22.2 15.2 %collective-permute-start.3 = (bf16[512,512]{1,0:T(8,128)(2,1)S(1)}, bf16[512,512]{1,0:T(8,128)(2,1)S(1)}, u32[]{:S(2)}, u32[]{:S(2)}) collective-permute-start(bf16[512,512]{1,0:T(8,128)(2,1)S(1)} %collective-permute-done.refs_4_), channel_id=1, source_target_pairs={{0,4},{1,5},{2,6},{3,7},{4,12},{5,13},{6,14},{7,15},{8,0},{9,1},{1... | collective-permute-start | bytes 1572872 | tf_op jit(solution)/shard_map/ppermute | solution.py:343
  24.8 14.1 %collective-permute-start.4 = (bf16[512,512]{1,0:T(8,128)(2,1)S(1)}, bf16[512,512]{1,0:T(8,128)(2,1)}, u32[]{:S(2)}, u32[]{:S(2)}) collective-permute-start(bf16[512,512]{1,0:T(8,128)(2,1)S(1)} %collective-permute-done.refs_4_), channel_id=1, source_target_pairs={{0,2},{1,3},{2,0},{3,1},{4,6},{5,7},{6,4},{7,5},{8,10},{9,11},{10,... | collective-permute-start | bytes 1572872 | tf_op jit(solution)/shard_map/ppermute | solution.py:343
  25.3 13.7 %collective-permute-start.5 = (bf16[512,512]{1,0:T(8,128)(2,1)S(1)}, bf16[512,512]{1,0:T(8,128)(2,1)S(1)}, u32[]{:S(2)}, u32[]{:S(2)}) collective-permute-start(bf16[512,512]{1,0:T(8,128)(2,1)S(1)} %collective-permute-done.refs_4_), channel_id=1, source_target_pairs={{0,16},{1,17},{2,18},{3,19},{4,20},{5,21},{6,22},{7,23},{8,24},{9,... | collective-permute-start | bytes 1572872 | tf_op jit(solution)/shard_map/ppermute | solution.py:343
  37.4 5.3 %copy-start.10 = (bf16[512,512]{1,0:T(8,128)(2,1)}, bf16[512,512]{1,0:T(8,128)(2,1)S(1)}, u32[]{:S(2)}) copy-start(bf16[512,512]{1,0:T(8,128)(2,1)S(1)} %collective-permute-done.3.refs_3_) | copy-start | bytes 1572868
  39.0 9.8 %copy-start.1 = (f32[8,576,128]{2,1,0:T(8,128)S(1)}, f32[8,576,128]{2,1,0:T(8,128)}, u32[]{:S(2)}) copy-start(f32[8,576,128]{2,1,0:T(8,128)} %get-tuple-element.77) | copy-start | bytes 7077892
  39.0 14.2 %collective-permute-start.7 = (bf16[512,512]{1,0:T(8,128)(2,1)S(1)}, bf16[512,512]{1,0:T(8,128)(2,1)S(1)}, u32[]{:S(2)}, u32[]{:S(2)}) collective-permute-start(bf16[512,512]{1,0:T(8,128)(2,1)S(1)} %collective-permute-done.3.refs_3_), channel_id=1, source_target_pairs={{0,4},{1,5},{2,6},{3,7},{4,12},{5,13},{6,14},{7,15},{8,0},{9,1},{1... | collective-permute-start | bytes 1572872 | tf_op jit(solution)/shard_map/ppermute | solution.py:343
  39.7 13.5 %collective-permute-start.8 = (bf16[512,512]{1,0:T(8,128)(2,1)S(1)}, bf16[512,512]{1,0:T(8,128)(2,1)S(1)}, u32[]{:S(2)}, u32[]{:S(2)}) collective-permute-start(bf16[512,512]{1,0:T(8,128)(2,1)S(1)} %collective-permute-done.3.refs_3_), channel_id=1, source_target_pairs={{0,2},{1,3},{2,0},{3,1},{4,6},{5,7},{6,4},{7,5},{8,10},{9,11},{10,... | collective-permute-start | bytes 1572872 | tf_op jit(solution)/shard_map/ppermute | solution.py:343
  41.2 12.3 %collective-permute-start.9 = (bf16[512,512]{1,0:T(8,128)(2,1)S(1)}, bf16[512,512]{1,0:T(8,128)(2,1)S(1)}, u32[]{:S(2)}, u32[]{:S(2)}) collective-permute-start(bf16[512,512]{1,0:T(8,128)(2,1)S(1)} %collective-permute-done.3.refs_3_), channel_id=1, source_target_pairs={{0,16},{1,17},{2,18},{3,19},{4,20},{5,21},{6,22},{7,23},{8,24},{9,... | collective-permute-start | bytes 1572872 | tf_op jit(solution)/shard_map/ppermute | solution.py:343
  53.6 13.8 %collective-permute-start.12 = (bf16[4,576,128]{2,1,0:T(8,128)(2,1)S(1)}, bf16[4,576,128]{2,1,0:T(8,128)(2,1)S(1)}, u32[]{:S(2)}, u32[]{:S(2)}) collective-permute-start(bf16[4,576,128]{2,1,0:T(8,128)(2,1)S(1)} %slice.62), channel_id=1, source_target_pairs={{0,4},{1,5},{2,6},{3,7},{4,0},{5,1},{6,2},{7,3},{8,12},{9,13},{10,... | collective-permute-start | bytes 1769480 | tf_op jit(solution)/shard_map/ppermute | solution.py:343
  54.3 11.8 %collective-permute-start.10 = (bf16[512,512]{1,0:T(8,128)(2,1)S(1)}, bf16[512,512]{1,0:T(8,128)(2,1)S(1)}, u32[]{:S(2)}, u32[]{:S(2)}) collective-permute-start(bf16[512,512]{1,0:T(8,128)(2,1)S(1)} %collective-permute-done.7.refs_3_), channel_id=1, source_target_pairs={{0,2},{1,3},{2,0},{3,1},{4,6},{5,7},{6,4},{7,5},{8,10},{9,11},{10,... | collective-permute-start | bytes 1572872 | tf_op jit(solution)/shard_map/ppermute | solution.py:343
  55.8 11.6 %collective-permute-start.11 = (bf16[512,512]{1,0:T(8,128)(2,1)S(1)}, bf16[512,512]{1,0:T(8,128)(2,1)}, u32[]{:S(2)}, u32[]{:S(2)}) collective-permute-start(bf16[512,512]{1,0:T(8,128)(2,1)S(1)} %collective-permute-done.7.refs_3_), channel_id=1, source_target_pairs={{0,16},{1,17},{2,18},{3,19},{4,20},{5,21},{6,22},{7,23},{8,24},{9,... | collective-permute-start | bytes 1572872 | tf_op jit(solution)/shard_map/ppermute | solution.py:343
  67.4 7.7 %collective-permute-start.13 = (f32[512,1024]{1,0:T(8,128)}, f32[512,1024]{1,0:T(8,128)S(1)}, u32[]{:S(2)}, u32[]{:S(2)}) collective-permute-start(f32[512,1024]{1,0:T(8,128)} %get-tuple-element.103), channel_id=1, source_target_pairs={{0,1},{1,0},{2,3},{3,2},{4,5},{5,4},{6,7},{7,6},{8,9},{9,8},{10,11... | collective-permute-start | bytes 6291464 | tf_op jit(solution)/shard_map/ppermute | solution.py:343
  67.4 5.3 %collective-permute-start.14 = (bf16[512,512]{1,0:T(8,128)(2,1)S(1)}, bf16[512,512]{1,0:T(8,128)(2,1)S(1)}, u32[]{:S(2)}, u32[]{:S(2)}) collective-permute-start(bf16[512,512]{1,0:T(8,128)(2,1)S(1)} %collective-permute-done.10.y3), channel_id=1, source_target_pairs={{0,1},{1,0},{2,3},{3,2},{4,5},{5,4},{6,7},{7,6},{8,9},{9,8},{10,11... | collective-permute-start | bytes 1572872 | tf_op jit(solution)/shard_map/ppermute | solution.py:343
  67.9 15.8 %collective-permute-start.18 = (bf16[512,512]{1,0:T(8,128)(2,1)}, bf16[512,512]{1,0:T(8,128)(2,1)}, u32[]{:S(2)}, u32[]{:S(2)}) collective-permute-start(bf16[512,512]{1,0:T(8,128)(2,1)} %collective-permute-done.4.refs_2_), channel_id=1, source_target_pairs={{0,16},{1,17},{2,18},{3,19},{4,20},{5,21},{6,22},{7,23},{8,24},{9,... | collective-permute-start | bytes 1572872 | tf_op jit(solution)/shard_map/ppermute | solution.py:343
  69.4 14.3 %collective-permute-start.19 = (bf16[512,512]{1,0:T(8,128)(2,1)}, bf16[512,512]{1,0:T(8,128)(2,1)}, u32[]{:S(2)}, u32[]{:S(2)}) collective-permute-start(bf16[512,512]{1,0:T(8,128)(2,1)} %copy-done.5), channel_id=1, source_target_pairs={{0,2},{1,3},{2,0},{3,1},{4,6},{5,7},{6,4},{7,5},{8,10},{9,11},{10,... | collective-permute-start | bytes 1572872 | tf_op jit(solution)/shard_map/ppermute | solution.py:343
  70.0 5.0 %collective-permute-start.15 = (bf16[512,512]{1,0:T(8,128)(2,1)}, bf16[512,512]{1,0:T(8,128)(2,1)}, u32[]{:S(2)}, u32[]{:S(2)}) collective-permute-start(bf16[512,512]{1,0:T(8,128)(2,1)} %collective-permute-done.11.a3), channel_id=1, source_target_pairs={{0,1},{1,0},{2,3},{3,2},{4,5},{5,4},{6,7},{7,6},{8,9},{9,8},{10,11... | collective-permute-start | bytes 1572872 | tf_op jit(solution)/shard_map/ppermute | solution.py:343
  73.5 16.4 %collective-permute-start.20 = (bf16[2,576,128]{2,1,0:T(8,128)(2,1)}, bf16[2,576,128]{2,1,0:T(8,128)(2,1)}, u32[]{:S(2)}, u32[]{:S(2)}) collective-permute-start(bf16[2,576,128]{2,1,0:T(8,128)(2,1)} %slice.63), channel_id=1, source_target_pairs={{0,8},{1,9},{2,10},{3,11},{4,12},{5,13},{6,14},{7,15},{8,0},{9,1},... | collective-permute-start | bytes 884744 | tf_op jit(solution)/shard_map/ppermute | solution.py:343
  75.0 15.3 %copy-start = (bf16[512,1024]{1,0:T(8,128)(2,1)S(1)}, bf16[512,1024]{1,0:T(8,128)(2,1)}, u32[]{:S(2)}) copy-start(bf16[512,1024]{1,0:T(8,128)(2,1)} %refs_5_.1) | copy-start | bytes 3145732
  75.0 15.8 %copy-start.4 = (bf16[512,512]{1,0:T(8,128)(2,1)S(1)}, bf16[512,512]{1,0:T(8,128)(2,1)}, u32[]{:S(2)}) copy-start(bf16[512,512]{1,0:T(8,128)(2,1)} %copy-done.3) | copy-start | bytes 1572868
  89.8 5.7 %collective-permute-start.22 = (bf16[512,512]{1,0:T(8,128)(2,1)}, bf16[512,512]{1,0:T(8,128)(2,1)S(1)}, u32[]{:S(2)}, u32[]{:S(2)}) collective-permute-start(bf16[512,512]{1,0:T(8,128)(2,1)} %collective-permute-done.18.e1), channel_id=1, source_target_pairs={{0,1},{1,0},{2,3},{3,2},{4,5},{5,4},{6,7},{7,6},{8,9},{9,8},{10,11... | collective-permute-start | bytes 1572872 | tf_op jit(solution)/shard_map/ppermute | solution.py:343
  89.9 5.7 %collective-permute-start.23 = (bf16[512,512]{1,0:T(8,128)(2,1)}, bf16[512,512]{1,0:T(8,128)(2,1)S(1)}, u32[]{:S(2)}, u32[]{:S(2)}) collective-permute-start(bf16[512,512]{1,0:T(8,128)(2,1)} %collective-permute-done.19.e2), channel_id=1, source_target_pairs={{0,1},{1,0},{2,3},{3,2},{4,5},{5,4},{6,7},{7,6},{8,9},{9,8},{10,11... | collective-permute-start | bytes 1572872 | tf_op jit(solution)/shard_map/ppermute | solution.py:343
  90.4 17.1 %collective-permute-start.17 = (bf16[512,512]{1,0:T(8,128)(2,1)S(1)}, bf16[512,512]{1,0:T(8,128)(2,1)S(1)}, u32[]{:S(2)}, u32[]{:S(2)}) collective-permute-start(bf16[512,512]{1,0:T(8,128)(2,1)S(1)} %constant_dynamic-slice_fusion), channel_id=1, source_target_pairs={{0,2},{1,3},{2,0},{3,1},{4,6},{5,7},{6,4},{7,5},{8,10},{9,11},{10,... | collective-permute-start | bytes 1572872 | tf_op jit(solution)/shard_map/ppermute | solution.py:343
  90.8 16.7 %collective-permute-start.16 = (bf16[512,512]{1,0:T(8,128)(2,1)S(1)}, bf16[512,512]{1,0:T(8,128)(2,1)S(1)}, u32[]{:S(2)}, u32[]{:S(2)}) collective-permute-start(bf16[512,512]{1,0:T(8,128)(2,1)S(1)} %copy-done.4), channel_id=1, source_target_pairs={{0,16},{1,17},{2,18},{3,19},{4,20},{5,21},{6,22},{7,23},{8,24},{9,... | collective-permute-start | bytes 1572872 | tf_op jit(solution)/shard_map/ppermute | solution.py:343
  94.1 13.4 %collective-permute-start.21 = (bf16[576,128]{1,0:T(8,128)(2,1)S(1)}, bf16[576,128]{1,0:T(8,128)(2,1)S(1)}, u32[]{:S(2)}, u32[]{:S(2)}) collective-permute-start(bf16[576,128]{1,0:T(8,128)(2,1)S(1)} %fusion.1), channel_id=1, source_target_pairs={{0,2},{1,3},{2,0},{3,1},{4,6},{5,7},{6,4},{7,5},{8,10},{9,11},{10,... | collective-permute-start | bytes 442376 | tf_op jit(solution)/shard_map/ppermute | solution.py:343
  107.5 1.6 %collective-permute-start.26 = (f32[576,128]{1,0:T(8,128)S(1)}, f32[576,128]{1,0:T(8,128)S(1)}, u32[]{:S(2)}, u32[]{:S(2)}) collective-permute-start(f32[576,128]{1,0:T(8,128)S(1)} %fusion), channel_id=1, source_target_pairs={{0,1},{1,0},{2,3},{3,2},{4,5},{5,4},{6,7},{7,6},{8,9},{9,8},{10,11... | collective-permute-start | bytes 884744 | tf_op jit(solution)/shard_map/ppermute | solution.py:343
  107.6 3.2 %collective-permute-start.24 = (bf16[512,512]{1,0:T(8,128)(2,1)S(1)}, bf16[512,512]{1,0:T(8,128)(2,1)S(1)}, u32[]{:S(2)}, u32[]{:S(2)}) collective-permute-start(bf16[512,512]{1,0:T(8,128)(2,1)S(1)} %collective-permute-done.16.e3), channel_id=1, source_target_pairs={{0,1},{1,0},{2,3},{3,2},{4,5},{5,4},{6,7},{7,6},{8,9},{9,8},{10,11... | collective-permute-start | bytes 1572872 | tf_op jit(solution)/shard_map/ppermute | solution.py:343
  108.1 2.7 %collective-permute-start.25 = (bf16[512,512]{1,0:T(8,128)(2,1)S(1)}, bf16[512,512]{1,0:T(8,128)(2,1)S(1)}, u32[]{:S(2)}, u32[]{:S(2)}) collective-permute-start(bf16[512,512]{1,0:T(8,128)(2,1)S(1)} %collective-permute-done.17.e0), channel_id=1, source_target_pairs={{0,1},{1,0},{2,3},{3,2},{4,5},{5,4},{6,7},{7,6},{8,9},{9,8},{10,11... | collective-permute-start | bytes 1572872 | tf_op jit(solution)/shard_map/ppermute | solution.py:343
  (14 other events, 36.6 us)

commit v3 on v2

v3 whole, which is shorter than its diff:
```python
import functools

import jax
import jax.numpy as jnp
import numpy as np
from jax import lax
from jax.experimental import pallas as pl
from jax.experimental.pallas import tpu as pltpu
from jax.sharding import PartitionSpec as P

HEAD = 128
R = 16
BLK = 128
SEQ = 4096
ROPE_BASE = 500000.0
ADAPTER_SCALE = 2.0
ALL = ("groups", "node", "outer")
HBM = pl.BlockSpec(memory_space=pltpu.HBM)
ANY = pl.BlockSpec(memory_space=pl.ANY)
MIB = 1024 * 1024


def rope_constants():
    half = HEAD // 2
    frequency = ROPE_BASE ** (-2.0 * np.arange(half) / HEAD)
    inside = np.arange(BLK)[:, None] * frequency[None, :]
    starts = BLK * np.arange(SEQ // BLK)[:, None] * frequency[None, :]
    both = lambda t: np.concatenate((t, t), axis=1)
    return np.concatenate(
        (both(np.cos(inside)), both(np.sin(inside)), both(np.cos(starts)), both(np.sin(starts)))
    ).astype(np.float32)


def block_tables(tab_ref, c_row, s_row):
    c_in = tab_ref[0:BLK, :]
    s_in = tab_ref[BLK : 2 * BLK, :]
    cosine = c_in * c_row - s_in * s_row
    sine = s_in * c_row + c_in * s_row
    lane = lax.broadcasted_iota(jnp.int32, (1, HEAD), 1)
    return cosine, jnp.where(lane < HEAD // 2, -sine, sine)


def gradient_kernel(
    sc, tids, count, pos, tok_ref, a_ref, b_ref, cot_ref, tab_ref, low_ref, own_ref, sib_ref,
    tv, av, bv, cv, tab, cosines, sines, grad, low, back, piece, sems,
):
    slots, rows, chunk = tv.shape
    down_half, up_half = chunk // 2, HEAD // 2
    outer = sc[8]
    lane = lax.broadcasted_iota(jnp.int32, (1, HEAD), 1)

    def chunk_copies(i):
        columns = pl.ds(pl.multiple_of(sc[i] * chunk, chunk), chunk)
        heads = pl.ds(pl.multiple_of(i * HEAD, HEAD), HEAD)
        return (
            pltpu.make_async_copy(cot_ref.at[:, heads], cv.at[i], sems.at[0, i]),
            pltpu.make_async_copy(a_ref.at[columns, :], av.at[i], sems.at[1, i]),
            pltpu.make_async_copy(tok_ref.at[:, columns], tv.at[i], sems.at[2, i]),
        )

    small = (
        pltpu.make_async_copy(tab_ref, tab, sems.at[3, 0]), pltpu.make_async_copy(b_ref, bv, sems.at[3, 1]),
    )
    for c in small:
        c.start()
    for i in range(slots):
        for c in chunk_copies(i):
            c.start()
    for c in small:
        c.wait()

    def keep_tables(at, cosine, sine):
        cosines[at, :] = cosine
        sines[at, :] = sine

    rope_blocks(pos, count, tab, rows, keep_tables)
    low[...] = jnp.zeros_like(low)
    back[...] = jnp.zeros_like(back)

    @pl.loop(0, slots)
    def _(i):
        for c in chunk_copies(i):
            c.wait()
        low[...] += jnp.dot(tv[i], av[i], preferred_element_type=jnp.float32)
        x = cv[i].astype(jnp.float32)
        g = (x * cosines[...] - pltpu.roll(x, HEAD // 2, 1) * sines[...]).astype(jnp.bfloat16)
        grad[i] = g
        second = bv[pl.ds(pl.multiple_of(i * HEAD, HEAD), HEAD), :]
        back[...] += jnp.dot(g, second, preferred_element_type=jnp.float32)

    for b in range(rows // BLK):
        at = slice(b * BLK, (b + 1) * BLK)
        hit = jnp.logical_and(lane // R == tids[b], b < count[0])
        select = jnp.where(hit, 1.0, 0.0).astype(jnp.float32)
        low_ref[at, :] = (low[at, :] * select).astype(jnp.bfloat16)
        back[at, :] = ADAPTER_SCALE * (back[at, :] * select).astype(jnp.bfloat16).astype(jnp.float32)
    turned = back[...].astype(jnp.bfloat16)
    contract = (((0,), (0,)), ((), ()))

    @pl.loop(0, slots)
    def _(i):
        for core, out in ((outer, own_ref), (1 - outer, sib_ref)):
            columns = pl.ds(pl.multiple_of(core * down_half, down_half), down_half)
            down = lax.dot_general(turned, tv[i, :, columns], contract, preferred_element_type=jnp.float32)
            out[i, 0:down_half, :] = down.T.astype(out.dtype)
        piece[...] = ADAPTER_SCALE * lax.dot_general(
            grad[sc[i]], low_ref[...], contract, preferred_element_type=jnp.float32
        )
        for core, out in ((outer, own_ref), (1 - outer, sib_ref)):
            at = pl.multiple_of(core * up_half, up_half)
            out[i, down_half:, :] = piece[pl.ds(at, up_half), :].astype(out.dtype)


def product_kernel(held_from, crossed_from, first, joined, sc, *refs):
    refs = list(refs)
    take = lambda n: [refs.pop(0) for _ in range(n)]
    toks = take(2)
    weights = (take(len(held_from)), take(len(crossed_from)))
    given = None if first else (take(2), take(2))
    low_ref, second_ref = take(2) if first else (None, None)
    outs = (take(2), take(1 if joined else 2))
    spare = take(1) if first else []
    tvs, wvs, tots = (take(2) for _ in range(3))
    sems, out_sems = refs
    deep, half = weights[0][-1].shape
    outer, plane = sc[8], sc[9]
    made, saved = [], []
    first_column = lambda side: pl.multiple_of((1 - plane if side else plane) * half, half)

    def load(src, dst):
        c = pltpu.make_async_copy(src, dst, sems.at[len(made)])
        c.start()
        made.append(c)
        return c

    columns = lambda i: pl.ds(pl.multiple_of((2 * sc[i] + outer) * deep, deep), deep)
    need = {}
    for k in range(2):
        for side, sources in enumerate((held_from, crossed_from)):
            todo = need[k, side] = []
            for i, at in enumerate(sources):
                part = slice(i * deep, (i + 1) * deep)
                if k == 0:
                    w = weights[side][i]
                    if w.shape[1] != half:
                        w = w.at[:, pl.ds(first_column(side), half)]
                    todo.append(load(w, wvs[side].at[part, :]))
                todo.append(load(toks[k].at[:, columns(at)], tvs[side].at[k, :, part]))
            if not first:
                todo.append(load(given[k][side], tots[side].at[k]))

    def start(k, side):
        if not first:
            return tots[side][k]
        if k:
            return 0.0
        return ADAPTER_SCALE * lax.dot_general(
            low_ref[...], second_ref[pl.ds(first_column(side), half), :], (((1,), (1,)), ((), ())),
            preferred_element_type=jnp.float32,
        )

    for k in range(2):
        for side in range(2):
            for c in need[k, side]:
                c.wait()
            if first and k == 0 and side:
                c = pltpu.make_async_copy(wvs[1].at[0:deep, :], spare[0], out_sems.at[4])
                c.start()
                saved.append(c)
            tots[side][k] = start(k, side) + jnp.dot(
                tvs[side][k], wvs[side][...], preferred_element_type=jnp.float32
            )
            if k and joined:
                dst = outs[1][0].at[:, side * half : (side + 1) * half]
            else:
                dst = outs[k][side]
            c = pltpu.make_async_copy(tots[side].at[k], dst, out_sems.at[2 * k + side])
            c.start()
            saved.append(c)
    for c in saved:
        c.wait()


def rope_blocks(pos, count, tab_ref, tokens, write):
    starts = SEQ // BLK
    for b in range(tokens // BLK):
        at = pos[b * BLK] // BLK
        cosine, sine = block_tables(
            tab_ref, tab_ref[pl.ds(2 * BLK + at, 1), :], tab_ref[pl.ds(2 * BLK + starts + at, 1), :]
        )
        live = jnp.where(b < count[0], 1.0, 0.0).astype(jnp.float32)
        write(slice(b * BLK, (b + 1) * BLK), cosine * live, sine * live)


def rotate_heads(pre, cosine, sine, res, rows):
    for h in range(pre.shape[1] // HEAD):
        cols = slice(h * HEAD, (h + 1) * HEAD)
        x = pre[:, cols]
        res[rows, cols] = (x * cosine + pltpu.roll(x, HEAD // 2, 1) * sine).astype(jnp.bfloat16)


def load_tokens(sc, tok_ref, nodes, pieces, tv, wv, sems):
    deep = pieces[0].shape[0]
    outer, copies = sc[8], []
    for core in range(2):
        for i, node in enumerate(nodes):
            at = pl.multiple_of((2 * sc[node] + (1 - outer if core else outer)) * deep, deep)
            to = (core * len(nodes) + i) * deep
            copies.append((tok_ref.at[:, pl.ds(at, deep)], tv.at[:, to : to + deep]))
            if not core:
                copies.append((pieces[i], wv.at[i * deep : (i + 1) * deep, :]))
    made = [pltpu.make_async_copy(src, dst, sems.at[i]) for i, (src, dst) in enumerate(copies)]
    for c in made:
        c.start()
    return made


def dots(tok, columns, weights):
    total = None
    for at, w in zip(columns, weights):
        part = jnp.dot(tok[:, at : at + w.shape[0]], w[...], preferred_element_type=jnp.float32)
        total = part if total is None else total + part
    return total


def held_keys_kernel(
    sc, count, pos, tok_ref, mine_h, mine_c, y3, a3, given, y3_other, a3_other, tab_ref,
    keys_ref, total_ref, tv, wv, vh, vc, res, sems,
):
    deep, half = y3.shape
    made = load_tokens(sc, tok_ref, (17, 13), (y3, a3), tv, wv, sems)
    made += [pltpu.make_async_copy(mine_h, vh, sems.at[6]), pltpu.make_async_copy(mine_c, vc, sems.at[7])]
    for c in made[6:]:
        c.start()
    for c in made:
        c.wait()
    vc[...] = (vc[...] + given[:, half:]) + dots(tv, (deep, 3 * deep), (wv.at[deep : 2 * deep, :], a3_other))
    last = pltpu.make_async_copy(vc, total_ref, sems.at[8])
    last.start()

    def write(at, cosine, sine):
        pre = dots(tv.at[at, :], (0, 2 * deep), (wv.at[0:deep, :], y3_other))
        rotate_heads(pre + (vh[at, :] + given[at, 0:half]), cosine, sine, res, at)

    rope_blocks(pos, count, tab_ref, vh.shape[0], write)
    save = pltpu.make_async_copy(
        res, keys_ref.at[:, pl.ds(pl.multiple_of(sc[9] * half, half), half)], sems.at[9]
    )
    save.start()
    save.wait()
    last.wait()


def crossed_kernel(sc, tok_ref, sib_ref, total_ref, e1, e2, mine_ref, theirs_ref, tv, wv, vc, sems, out_sems):
    deep = e1.shape[0]
    outer, copies = sc[8], []
    for i, (node, piece) in enumerate(((15, e1), (16, e2))):
        part = slice(i * deep, (i + 1) * deep)
        at = pl.multiple_of((2 * sc[node] + outer) * deep, deep)
        copies.append((piece, wv.at[part, :]))
        for k, tok in enumerate((tok_ref, sib_ref)):
            copies.append((tok.at[:, pl.ds(at, deep)], tv.at[k, :, part]))
    copies.append((total_ref, vc.at[0]))
    made = [pltpu.make_async_copy(src, dst, sems.at[i]) for i, (src, dst) in enumerate(copies)]
    for c in made:
        c.start()
    for c in made:
        c.wait()
    saves = []
    for k, dst in enumerate((mine_ref, theirs_ref)):
        part = jnp.dot(tv[k], wv[...], preferred_element_type=jnp.float32)
        vc[k] = part if k else vc[0] + part
        saves.append(pltpu.make_async_copy(vc.at[k], dst, out_sems.at[k]))
        saves[-1].start()
    for c in saves:
        c.wait()


def fold_kernel(keep_ref, got_ref, next_ref, *send_refs):
    at = next_ref.shape[0]
    next_ref[...] = keep_ref[0:at] + got_ref[0:at].astype(jnp.float32)
    for ref in send_refs:
        n = ref.shape[0]
        ref[...] = (keep_ref[at : at + n] + got_ref[at : at + n].astype(jnp.float32)).astype(ref.dtype)
        at += n


def sum_kernel(keep_ref, *refs):
    total = keep_ref[...]
    for ref in refs[:-1]:
        total = total + ref[...].astype(jnp.float32)
    refs[-1][...] = total


def crossed_keys_kernel(
    sc, count, pos, tok_ref, total_ref, e3, e0, e3_other, e0_other, given, share, share_other, tab_ref,
    keys_ref, out_ref, down_ref, up_ref, tv, wv, vc, res, sems,
):
    deep, half = e3.shape
    outer = sc[8]
    down_rows = down_ref.shape[0] // 2
    up_rows = up_ref.shape[0] // 2
    made = load_tokens(sc, tok_ref, (17, 14), (e3, e0), tv, wv, sems)
    total = pltpu.make_async_copy(total_ref, vc, sems.at[6])
    total.start()
    saves = []
    for i, (core, sums) in enumerate(((outer, share), (1 - outer, share_other))):
        down_at = pl.multiple_of(core * down_rows, down_rows)
        up_at = pl.multiple_of(core * up_rows, up_rows)
        saves += [
            pltpu.make_async_copy(
                sums.at[0, 0:down_rows, :], down_ref.at[pl.ds(down_at, down_rows), :], sems.at[7 + 2 * i]
            ),
            pltpu.make_async_copy(
                sums.at[0, down_rows:, :], up_ref.at[pl.ds(up_at, up_rows), :], sems.at[8 + 2 * i]
            ),
        ]
    for c in saves:
        c.start()
    for c in made:
        c.wait()
    total.wait()

    def write(at, cosine, sine):
        pre = vc[at, :] + given[at, :] + dots(tv.at[at, :], (0, 2 * deep, 3 * deep), (wv, e3_other, e0_other))
        rotate_heads(pre, cosine, sine, res, at)

    rope_blocks(pos, count, tab_ref, vc.shape[0], write)
    saves.append(
        pltpu.make_async_copy(
            res, out_ref.at[:, pl.ds(pl.multiple_of((1 - sc[9]) * half, half), half)], sems.at[11]
        )
    )
    saves[-1].start()
    for c in saves:
        c.wait()


class Routes:
    def __init__(self, mesh):
        self.groups, self.nodes, self.outers = (mesh.shape[a] for a in ALL)
        self.z = self.nodes // 2
        line = list(range(self.z))
        ring = line[:1] + line[1::2] + line[2::2][::-1]
        self.next = {ring[i]: ring[(i + 1) % self.z] for i in range(self.z)}
        self.prev = {v: k for k, v in self.next.items()}

    def pairs(self, f):
        at = lambda g, z, y, o: (g * self.nodes + 2 * z + y) * self.outers + o
        return [
            (at(g, z, y, o), at(*f(g, z, y, o)))
            for g in range(self.groups)
            for z in range(self.z)
            for y in range(2)
            for o in range(self.outers)
        ]

    def table(self):
        rows = []
        for _, n, o, g in [
            (0, n, o, g) for g in range(self.groups) for n in range(self.nodes) for o in range(self.outers)
        ]:
            z, y = divmod(n, 2)
            slot = [n ^ ((r >> 2) & 1 | ((r >> 1) & 1) << 1 | (r & 1) << 2) for r in range(8)]
            from_z = [z]
            for _ in range(self.z - 1):
                from_z.append(self.prev[from_z[-1]])
            rows.append(
                slot + [o, g] + [2 * k + y for k in from_z] + [2 * k + 1 - y for k in from_z]
            )
        return np.array(rows, np.int32)


def call(kernel, name, shapes, in_specs, out_specs, scratch, args, grid=(), prefetch=1, aliases=None, vmem=16):
    specs = [None] * prefetch + in_specs
    return pl.pallas_call(
        kernel,
        out_shape=shapes,
        grid_spec=pltpu.PrefetchScalarGridSpec(
            num_scalar_prefetch=prefetch, grid=grid, in_specs=in_specs, out_specs=out_specs,
            scratch_shapes=scratch,
        ),
        compiler_params=pltpu.CompilerParams(vmem_limit_bytes=vmem * MIB),
        cost_estimate=pl.CostEstimate(flops=1000, bytes_accessed=1024, transcendentals=0),
        input_output_aliases=aliases or {},
        name=name,
    )(*[pltpu.with_memory_space_constraint(x, pltpu.HBM) if spec is HBM else x for x, spec in zip(args, specs)])


def fast_body(
    routes, tokens, frozen_weight, down_adapter, second_adapter_weight, tenant_ids, block_counts, positions, cotangent
):
    bf16, f32 = jnp.bfloat16, jnp.float32
    rows, width = tokens.shape
    deep, kv = frozen_weight.shape
    nodes = routes.nodes
    chunk = 2 * deep
    half = kv // 2
    rank = down_adapter.shape[1]
    plane = lax.axis_index("groups")
    outer = lax.axis_index("outer")
    tab = jnp.asarray(rope_constants())

    send = lambda x, f: lax.ppermute(x, ALL, routes.pairs(f))
    to_core = lambda g, z, y, o: (g, z, y, 1 - o)
    to_x = lambda g, z, y, o: (1 - g, z, y, o)
    to_y = lambda g, z, y, o: (g, z, 1 - y, o)
    to_z = lambda g, z, y, o: (g, routes.next[z], y, o)
    to_z1 = lambda g, z, y, o: (g, z ^ 1, y, o)
    to_z2 = lambda g, z, y, o: (g, z ^ 2, y, o)
    to_z3 = lambda g, z, y, o: (g, z ^ 3, y, o)
    fence = lambda *x: lax.optimization_barrier(x)
    vm = pl.BlockSpec(memory_space=pltpu.VMEM)
    dma = pltpu.SemaphoreType.DMA
    shape = jax.ShapeDtypeStruct

    def fold(keep, got, stay, *go):
        slots = lambda n, dtype: pltpu.VMEM((n, *keep.shape[1:]), dtype)
        return call(
            fold_kernel, "fold", [slots(stay, f32), *[slots(n, bf16) for n in go]],
            [vm, vm], [vm] * (1 + len(go)), [], (keep, got), prefetch=0,
        )

    def product(held, crossed, given=(), adapters=(), joined=False):
        kh, kc = len(held) * deep, len(crossed) * deep
        outs = [pltpu.VMEM((rows, half), f32)] * 2
        outs += [pltpu.VMEM((rows, kv), f32)] if joined else outs
        outs += [] if given else [shape((deep, half), bf16)]
        return call(
            functools.partial(
                product_kernel, [i for _, i in held], [i for _, i in crossed], not given, joined
            ),
            "products", outs,
            [HBM] * 2 + [HBM if w is frozen_weight else ANY for w, _ in held + crossed] + [ANY] * len(given)
            + [vm] * len(adapters), [ANY] * len(outs),
            [
                pltpu.VMEM((2, rows, kh), bf16), pltpu.VMEM((2, rows, kc), bf16),
                pltpu.VMEM((kh, half), bf16), pltpu.VMEM((kc, half), bf16),
                pltpu.VMEM((2, rows, half), f32), pltpu.VMEM((2, rows, half), f32),
                dma((3 * len(held) + 3 * len(crossed) + 4,)), dma((5,)),
            ],
            (sc, tokens, sib_tokens, *[w for w, _ in held], *[w for w, _ in crossed], *given, *adapters),
        )

    z0 = lax.dynamic_slice(frozen_weight, (0, plane * half), (deep, half))
    z0, own_tokens, table = fence(z0, tokens, jnp.asarray(routes.table()))
    sc = lax.dynamic_slice(table, (lax.axis_index(ALL), 0), (1, table.shape[1]))[0]
    z1 = send(z0, to_z)
    y0 = send(z0, to_y)
    sib_tokens = send(own_tokens, to_core)
    slot_rows = chunk // 2 + kv // nodes // 2
    low, own, sib = call(
        gradient_kernel, "adapter_gradients",
        [
            pltpu.VMEM((rows, rank), bf16), pltpu.VMEM((nodes, slot_rows, rank), f32),
            pltpu.VMEM((nodes, slot_rows, rank), bf16),
        ],
        [HBM] * 5, [vm] * 3,
        [
            pltpu.VMEM((nodes, rows, chunk), bf16), pltpu.VMEM((nodes, chunk, rank), bf16),
            pltpu.VMEM((kv, rank), bf16), pltpu.VMEM((nodes, rows, HEAD), bf16), pltpu.VMEM(tab.shape, f32),
            pltpu.VMEM((rows, HEAD), f32), pltpu.VMEM((rows, HEAD), f32), pltpu.VMEM((nodes, rows, HEAD), bf16),
            pltpu.VMEM((rows, rank), f32), pltpu.VMEM((rows, rank), f32), pltpu.VMEM((HEAD, rank), f32),
            dma((4, nodes)),
        ],
        (sc, tenant_ids, block_counts, positions, tokens, down_adapter, second_adapter_weight, cotangent, tab),
        prefetch=4, vmem=52,
    )
    z1, y0, low, own, sib, sib_tokens = fence(z1, y0, low, own, sib, sib_tokens)

    z2 = send(z1, to_z)
    y1 = send(z1, to_y)
    a1 = send(z1, to_x)
    other = send(sib, to_core)
    *totals, c0 = product(
        ((frozen_weight, 10), (y0, 14), (z1, 11)), ((frozen_weight, 10),), adapters=(low, second_adapter_weight)
    )
    z2, y1, a1, other, *totals = fence(z2, y1, a1, other, *totals)

    z3 = send(z2, to_z)
    y2 = send(z2, to_y)
    a2 = send(z2, to_x)
    keep, out = fold(own, other, 4, 4)
    totals = product(((y1, 15), (z2, 12)), ((a1, 11),), given=totals)
    z3, y2, a2, keep, out, *totals = fence(z3, y2, a2, keep, out, *totals)

    y3 = send(y2, to_z)
    a3 = send(z3, to_x)
    got = send(out, to_y)
    mine_h, mine_c, theirs = product(((y2, 16), (z3, 13)), ((a2, 12),), given=totals, joined=True)
    y3, a3, got, mine_h, mine_c, theirs = fence(y3, a3, got, mine_h, mine_c, theirs)

    given, y3_other, a3_other = send(theirs, to_core), send(y3, to_core), send(a3, to_core)
    e1 = send(y1, to_x)
    e2 = send(a2, to_y)
    keep, *out = fold(keep, got, 1, 1, 1, 1)
    got = [send(x, f) for x, f in zip(out, (to_z2, to_z1, to_z3))]
    own_space = [
        pltpu.VMEM((rows, 2 * chunk), bf16), pltpu.VMEM((chunk, half), bf16), pltpu.VMEM((rows, half), f32),
    ]
    keys, total = call(
        held_keys_kernel, "held_keys", [shape((rows, kv), bf16), pltpu.VMEM((rows, half), f32)],
        [HBM] + [ANY] * 4 + [vm] * 4, [ANY, ANY],
        own_space + [pltpu.VMEM((rows, half), f32), pltpu.VMEM((rows, half), bf16), dma((10,))],
        (sc, block_counts, positions, tokens, mine_h, mine_c, y3, a3, given, y3_other, a3_other, tab),
        prefetch=3,
    )
    y3, c0, total = fence(y3, c0, total)
    e3 = send(y3, to_x)
    e0 = send(c0, to_y)
    e1, e2, total = fence(e1, e2, total)
    mine, theirs = call(
        crossed_kernel, "crossed_products", [pltpu.VMEM((rows, half), f32)] * 2,
        [HBM] * 2 + [ANY] * 3, [ANY, ANY],
        [
            pltpu.VMEM((2, rows, chunk), bf16), pltpu.VMEM((chunk, half), bf16),
            pltpu.VMEM((2, rows, half), f32), dma((7,)), dma((2,)),
        ],
        (sc, tokens, sib_tokens, total, e1, e2),
    )
    e3, e0, mine, theirs, *got = fence(e3, e0, mine, theirs, *got)

    share = call(
        sum_kernel, "share", pltpu.VMEM(keep.shape, f32), [vm] * 4, vm, [], (keep, *got), prefetch=0,
    )
    keys, down, up = call(
        crossed_keys_kernel, "crossed_keys",
        [shape((rows, kv), bf16), shape((chunk, rank), f32), shape((kv // nodes, rank), f32)],
        [HBM] + [ANY] * 3 + [vm] * 6 + [ANY], [ANY] * 3,
        own_space + [pltpu.VMEM((rows, half), bf16), dma((12,))],
        (
            sc, block_counts, positions, tokens, mine, e3, e0, send(e3, to_core), send(e0, to_core),
            send(theirs, to_core), share, send(share, to_core), tab, keys,
        ),
        prefetch=3, aliases={13: 0},
    )
    return keys, down, up


def rope_tables(positions):
    half_head = HEAD // 2
    frequency = ROPE_BASE ** (-2.0 * jnp.arange(half_head, dtype=jnp.float32) / HEAD)
    angle = positions.astype(jnp.float32)[:, None] * frequency[None, :]
    return (jnp.cos(angle), jnp.sin(angle))


def rotate(field, cosine, sine, orient):
    rows = field.shape[0]
    shaped = field.reshape(rows, -1, 2, HEAD // 2)
    first = shaped[:, :, 0]
    second = shaped[:, :, 1]
    cos_b = cosine[:, None, :]
    sin_b = orient * sine[:, None, :]
    out_first = first * cos_b - second * sin_b
    out_second = second * cos_b + first * sin_b
    return jnp.stack((out_first, out_second), axis=2).reshape(rows, -1)


def plain_body(
    tokens, frozen_weight, down_adapter, second_adapter_weight, tenant_ids, block_counts, positions, cotangent
):
    token_rows = tokens.shape[0]
    block_total = tenant_ids.shape[0]
    block_rows = token_rows // block_total
    width_cols = down_adapter.shape[1]
    live_blocks = (jnp.arange(block_total, dtype=jnp.int32) < block_counts[0]).astype(jnp.float32)
    live_rows = jnp.repeat(live_blocks, block_rows)[:, None]
    column_tenant = jnp.arange(width_cols, dtype=jnp.int32) // R
    select_blocks = (tenant_ids[:, None] == column_tenant[None, :]).astype(
        jnp.float32
    ) * live_blocks[:, None]
    select = jnp.repeat(select_blocks, block_rows, axis=0)
    lowrank_hidden = (
        jnp.dot(tokens, down_adapter, preferred_element_type=jnp.float32) * select
    ).astype(jnp.bfloat16)
    frozen_output = jnp.dot(
        tokens,
        lax.all_gather(frozen_weight, ("node", "outer"), axis=0, tiled=True),
        preferred_element_type=jnp.float32,
    )
    adapter_output = lax.dot_general(
        lowrank_hidden,
        second_adapter_weight,
        (((1,), (1,)), ((), ())),
        preferred_element_type=jnp.float32,
    )
    unrotated_keys = frozen_output + ADAPTER_SCALE * adapter_output
    cosine, sine = rope_tables(positions)
    keys = (live_rows * rotate(unrotated_keys, cosine, sine, 1.0)).astype(jnp.bfloat16)
    output_gradient = (
        live_rows * rotate(cotangent.astype(jnp.float32), cosine, sine, -1.0)
    ).astype(jnp.bfloat16)
    backward_gradient = (
        jnp.dot(output_gradient, second_adapter_weight, preferred_element_type=jnp.float32) * select
    ).astype(jnp.bfloat16)
    down_product = ADAPTER_SCALE * lax.dot_general(
        tokens, backward_gradient, (((0,), (0,)), ((), ())), preferred_element_type=jnp.float32
    )
    up_product = ADAPTER_SCALE * lax.dot_general(
        output_gradient,
        lowrank_hidden,
        (((0,), (0,)), ((), ())),
        preferred_element_type=jnp.float32,
    )
    shares = (
        lax.psum_scatter(down_product, "node", scatter_dimension=0, tiled=True),
        lax.psum_scatter(up_product, "node", scatter_dimension=0, tiled=True),
    )
    down_adapter_gradient, up_adapter_gradient = lax.psum((shares[0], shares[1]), "outer")
    return (keys, down_adapter_gradient, up_adapter_gradient)


def solution(mesh):
    placed = (
        P(("groups", "node", "outer"), None),
        P(("node", "outer"), None),
        P(),
        P(),
        P(("groups", "node", "outer")),
        P(("groups", "node", "outer")),
        P(("groups", "node", "outer")),
        P(("groups", "node", "outer"), None),
    )
    routed = tuple(mesh.shape[a] for a in ALL) == (2, 8, 2)
    return jax.shard_map(
        functools.partial(fast_body, Routes(mesh)) if routed else plain_body,
        mesh=mesh,
        in_specs=placed,
        out_specs=(
            P(("groups", "node", "outer"), None),
            P(("groups", "node"), None),
            P(("groups", "node"), None),
        ),
        check_vma=False,
    )
```

time: 119 us -> 102 us (0.86)
  Pallas kernels: 52.8 us -> 38.6 us
  local copies, waits for them, and re-layouts: 8.01 us -> 2.3 us
  starting transfers between devices: 26.3 us -> 29.4 us
  other arithmetic: 2.84 us -> 0 us
  waiting for transfers between devices: 26.6 us -> 29.4 us
    pallas_call x7 -> x10, Pallas kernels: 52.8 us -> 38.6 us  [call(): pl.pallas_call(kernel, out_shape=shapes, grid_spec=pltpu.PrefetchScalarGr...]
    unnamed x38 -> x8, local copies, waits for them, and re-layouts: 4.74 us -> 0.01 us
    ppermute x27, starting transfers between devices: 26.3 us -> 29.4 us  [fast_body(): send = lambda x, f: lax.ppermute(x, ALL, routes.pairs(f))]
    ppermute x27, waiting for transfers between devices: 26.6 us -> 29.4 us  [fast_body(): send = lambda x, f: lax.ppermute(x, ALL, routes.pairs(f))]
    concatenate x2 -> x0, other arithmetic: 1.46 us -> none  [the longest x1 0.83 us: fast_body(): down = jnp.concatenate((lower[:down_rows], upper[:down_rows]))]
    add x4 -> x0, other arithmetic: 1.34 us -> none  [the longest x1 1.01 us: fast_body(): s = s[:2] + got.astype(f32)]
  transfers between devices with their start and end apart: 27 -> 27, of which waited for: 11 -> 16; matrix products, arithmetic and copies ran while one was open for 4% -> 1% of each run, Pallas kernels for 39% -> 33%
where the time goes in v3:
time: 102 us; the launch traced here: 101 us
  Pallas kernels  38.6 us (38%)
  starting transfers between devices  29.4 us (29%)
  waiting for transfers between devices  29.4 us (29%)
  local copies, waits for them, and re-layouts  2.3 us (2%)
  between operations  1.55 us (2%)
    pallas_call x10, Pallas kernels, call(): pl.pallas_call(kernel, out_shape=shapes, grid_spec=pltpu.PrefetchScalarGr...  38.6 us
    ppermute x27, starting transfers between devices, fast_body(): send = lambda x, f: lax.ppermute(x, ALL, routes.pairs(f))  29.4 us
    ppermute x27, waiting for transfers between devices, fast_body(): send = lambda x, f: lax.ppermute(x, ALL, routes.pairs(f))  29.4 us
  transfers between devices with their start and end apart: 27, of which 16 were waited for; matrix products, arithmetic and copies ran while one was open for 1% of the time, Pallas kernels for 33%

profile of v3, /device:TPU:0, one launch (start us, length us, event | category | flops | bytes accessed | tf_op | source)
XLA Modules:
  0.0 101.3 jit_solution(1248334265526668782)
XLA Ops:
  2.2 2.6 %collective-permute-start = (bf16[512,512]{1,0:T(8,128)(2,1)S(1)}, bf16[512,512]{1,0:T(8,128)(2,1)S(1)}, u32[]{:S(2)}, u32[]{:S(2)}) collective-permute-start(bf16[512,512]{1,0:T(8,128)(2,1)S(1)} %constant_dynamic-slice_fusion), channel_id=1, source_target_pairs={{0,4},{1,5},{2,6},{3,7},{4,12},{5,13},{6,14},{7,15},{8,0},{9,1},{1... | collective-permute-start | bytes 1572872 | tf_op jit(solution)/shard_map/ppermute | solution.py:404
  4.9 1.5 %collective-permute-start.1 = (bf16[512,512]{1,0:T(8,128)(2,1)S(1)}, bf16[512,512]{1,0:T(8,128)(2,1)S(1)}, u32[]{:S(2)}, u32[]{:S(2)}) collective-permute-start(bf16[512,512]{1,0:T(8,128)(2,1)S(1)} %constant_dynamic-slice_fusion), channel_id=1, source_target_pairs={{0,2},{1,3},{2,0},{3,1},{4,6},{5,7},{6,4},{7,5},{8,10},{9,11},{10,... | collective-permute-start | bytes 1572872 | tf_op jit(solution)/shard_map/ppermute | solution.py:404
  7.1 1.2 %dynamic-slice_bitcast_fusion.sc = s32[18]{0:T(128)} fusion(s32[32,18]{1,0:T(8,128)} %constant.29.clone, s32[]{:T(128)S(6)} %select_n.7), kind=kLoop, calls=%fused_computation | loop fusion | bytes 148 | tf_op jit(solution)/shard_map/squeeze | solution.py:447
  8.3 10.0 %adapter_gradients.1 = (bf16[512,128]{1,0:T(8,128)(2,1)S(1)}, f32[8,576,128]{2,1,0:T(8,128)S(1)}, bf16[8,576,128]{2,1,0:T(8,128)(2,1)S(1)}) custom-call(s32[18]{0:T(128)} %dynamic-slice_bitcast_fusion.sc, s32[4]{0:T(128)} %tids.1, s32[1]{0:T(128)S(6)} %copy.15.count, s32[512]{0:T(512)} %pos.5, bf16[512,8192]{1,0:T(8,128)(2,1)} %tok_ref.7, ...), custom_call_target="tpu_custom_call" | custom-call | flops 1000 | bytes 1024 | tf_op jit(solution)/shard_map/adapter_gradients/pallas_call | solution.py:376
  18.9 2.6 %collective-permute-start.3 = (bf16[512,512]{1,0:T(8,128)(2,1)S(1)}, bf16[512,512]{1,0:T(8,128)(2,1)S(1)}, u32[]{:S(2)}, u32[]{:S(2)}) collective-permute-start(bf16[512,512]{1,0:T(8,128)(2,1)S(1)} %collective-permute-done.refs_4_), channel_id=1, source_target_pairs={{0,4},{1,5},{2,6},{3,7},{4,12},{5,13},{6,14},{7,15},{8,0},{9,1},{1... | collective-permute-start | bytes 1572872 | tf_op jit(solution)/shard_map/ppermute | solution.py:404
  21.5 1.5 %collective-permute-start.4 = (bf16[512,512]{1,0:T(8,128)(2,1)S(1)}, bf16[512,512]{1,0:T(8,128)(2,1)S(1)}, u32[]{:S(2)}, u32[]{:S(2)}) collective-permute-start(bf16[512,512]{1,0:T(8,128)(2,1)S(1)} %collective-permute-done.refs_4_), channel_id=1, source_target_pairs={{0,2},{1,3},{2,0},{3,1},{4,6},{5,7},{6,4},{7,5},{8,10},{9,11},{10,... | collective-permute-start | bytes 1572872 | tf_op jit(solution)/shard_map/ppermute | solution.py:404
  23.0 1.5 %collective-permute-start.5 = (bf16[512,512]{1,0:T(8,128)(2,1)S(1)}, bf16[512,512]{1,0:T(8,128)(2,1)S(1)}, u32[]{:S(2)}, u32[]{:S(2)}) collective-permute-start(bf16[512,512]{1,0:T(8,128)(2,1)S(1)} %collective-permute-done.refs_4_), channel_id=1, source_target_pairs={{0,16},{1,17},{2,18},{3,19},{4,20},{5,21},{6,22},{7,23},{8,24},{9,... | collective-permute-start | bytes 1572872 | tf_op jit(solution)/shard_map/ppermute | solution.py:404
  24.5 5.8 %products.3 = (f32[512,512]{1,0:T(8,128)S(1)}, f32[512,512]{1,0:T(8,128)S(1)}, f32[512,512]{1,0:T(8,128)S(1)}, f32[512,512]{1,0:T(8,128)S(1)}, bf16[512,512]{1,0:T(8,128)(2,1)S(1)}) custom-call(s32[18]{0:T(128)S(1)} %copy-done.2, bf16[512,8192]{1,0:T(8,128)(2,1)} %tok_ref.7, bf16[512,8192]{1,0:T(8,128)(2,1)} %collective-permute-done.2.refs_1_.sib_ref, ...), custom_call_target="tpu_custom_call" | custom-call | flops 1000 | bytes 1024 | tf_op jit(solution)/shard_map/products/pallas_call | solution.py:376
  30.2 3.9 %collective-permute-done.3.refs_3_ = bf16[512,512]{1,0:T(8,128)(2,1)S(1)} collective-permute-done((bf16[512,512]{1,0:T(8,128)(2,1)S(1)}, bf16[512,512]{1,0:T(8,128)(2,1)S(1)}, u32[]{:S(2)}, u32[]{:S(2)}) %collective-permute-start.3) | collective-permute-done | bytes 524320 | tf_op jit(solution)/shard_map/ppermute | solution.py:404
  34.1 1.4 %collective-permute-done.4.refs_2_ = bf16[512,512]{1,0:T(8,128)(2,1)S(1)} collective-permute-done((bf16[512,512]{1,0:T(8,128)(2,1)S(1)}, bf16[512,512]{1,0:T(8,128)(2,1)S(1)}, u32[]{:S(2)}, u32[]{:S(2)}) %collective-permute-start.4) | collective-permute-done | bytes 524320 | tf_op jit(solution)/shard_map/ppermute | solution.py:404
  35.5 1.2 %collective-permute-done.5.refs_4_ = bf16[512,512]{1,0:T(8,128)(2,1)S(1)} collective-permute-done((bf16[512,512]{1,0:T(8,128)(2,1)S(1)}, bf16[512,512]{1,0:T(8,128)(2,1)S(1)}, u32[]{:S(2)}, u32[]{:S(2)}) %collective-permute-start.5) | collective-permute-done | bytes 524320 | tf_op jit(solution)/shard_map/ppermute | solution.py:404
  36.8 1.2 %collective-permute-start.7 = (bf16[512,512]{1,0:T(8,128)(2,1)S(1)}, bf16[512,512]{1,0:T(8,128)(2,1)S(1)}, u32[]{:S(2)}, u32[]{:S(2)}) collective-permute-start(bf16[512,512]{1,0:T(8,128)(2,1)S(1)} %collective-permute-done.3.refs_3_), channel_id=1, source_target_pairs={{0,4},{1,5},{2,6},{3,7},{4,12},{5,13},{6,14},{7,15},{8,0},{9,1},{1... | collective-permute-start | bytes 1572872 | tf_op jit(solution)/shard_map/ppermute | solution.py:404
  38.5 1.5 %collective-permute-start.9 = (bf16[512,512]{1,0:T(8,128)(2,1)S(1)}, bf16[512,512]{1,0:T(8,128)(2,1)S(1)}, u32[]{:S(2)}, u32[]{:S(2)}) collective-permute-start(bf16[512,512]{1,0:T(8,128)(2,1)S(1)} %collective-permute-done.3.refs_3_), channel_id=1, source_target_pairs={{0,16},{1,17},{2,18},{3,19},{4,20},{5,21},{6,22},{7,23},{8,24},{9,... | collective-permute-start | bytes 1572872 | tf_op jit(solution)/shard_map/ppermute | solution.py:404
  40.1 4.6 %products.4 = (f32[512,512]{1,0:T(8,128)S(1)}, f32[512,512]{1,0:T(8,128)S(1)}, f32[512,512]{1,0:T(8,128)S(1)}, f32[512,512]{1,0:T(8,128)S(1)}) custom-call(s32[18]{0:T(128)S(1)} %copy-done.2, bf16[512,8192]{1,0:T(8,128)(2,1)} %tok_ref.7, bf16[512,8192]{1,0:T(8,128)(2,1)} %collective-permute-done.2.refs_1_.sib_ref, ...), custom_call_target="tpu_custom_call" | custom-call | flops 1000 | bytes 1024 | tf_op jit(solution)/shard_map/products/pallas_call | solution.py:376
  44.7 5.9 %collective-permute-done.7.refs_3_ = bf16[512,512]{1,0:T(8,128)(2,1)S(1)} collective-permute-done((bf16[512,512]{1,0:T(8,128)(2,1)S(1)}, bf16[512,512]{1,0:T(8,128)(2,1)S(1)}, u32[]{:S(2)}, u32[]{:S(2)}) %collective-permute-start.7) | collective-permute-done | bytes 524320 | tf_op jit(solution)/shard_map/ppermute | solution.py:404
  50.9 1.4 %collective-permute-start.12 = (bf16[4,576,128]{2,1,0:T(8,128)(2,1)S(1)}, bf16[4,576,128]{2,1,0:T(8,128)(2,1)S(1)}, u32[]{:S(2)}, u32[]{:S(2)}) collective-permute-start(bf16[4,576,128]{2,1,0:T(8,128)(2,1)S(1)} %get-tuple-element.105), channel_id=1, source_target_pairs={{0,2},{1,3},{2,0},{3,1},{4,6},{5,7},{6,4},{7,5},{8,10},{9,11},{10,... | collective-permute-start | bytes 1769480 | tf_op jit(solution)/shard_map/ppermute | solution.py:404
  52.9 1.5 %collective-permute-start.11 = (bf16[512,512]{1,0:T(8,128)(2,1)S(1)}, bf16[512,512]{1,0:T(8,128)(2,1)S(1)}, u32[]{:S(2)}, u32[]{:S(2)}) collective-permute-start(bf16[512,512]{1,0:T(8,128)(2,1)S(1)} %collective-permute-done.7.refs_3_), channel_id=1, source_target_pairs={{0,16},{1,17},{2,18},{3,19},{4,20},{5,21},{6,22},{7,23},{8,24},{9,... | collective-permute-start | bytes 1572872 | tf_op jit(solution)/shard_map/ppermute | solution.py:404
  54.4 4.7 %products.5 = (f32[512,512]{1,0:T(8,128)S(1)}, f32[512,512]{1,0:T(8,128)S(1)}, f32[512,1024]{1,0:T(8,128)S(1)}) custom-call(s32[18]{0:T(128)S(1)} %copy-done.2, bf16[512,8192]{1,0:T(8,128)(2,1)} %tok_ref.7, bf16[512,8192]{1,0:T(8,128)(2,1)} %collective-permute-done.2.refs_1_.sib_ref, bf16[512,512]{1,0:T(8,128)(2,1)S(1)} %collective-permute-done.8.refs_2_, ...), custom_call_target="tpu_custom_call" | custom-call | flops 1000 | bytes 1024 | tf_op jit(solution)/shard_map/products/pallas_call | solution.py:376
  59.1 5.1 %collective-permute-done.10.y3 = bf16[512,512]{1,0:T(8,128)(2,1)S(1)} collective-permute-done((bf16[512,512]{1,0:T(8,128)(2,1)S(1)}, bf16[512,512]{1,0:T(8,128)(2,1)S(1)}, u32[]{:S(2)}, u32[]{:S(2)}) %collective-permute-start.10) | collective-permute-done | bytes 524320 | tf_op jit(solution)/shard_map/ppermute | solution.py:404
  65.0 1.5 %collective-permute-start.18 = (bf16[512,512]{1,0:T(8,128)(2,1)S(1)}, bf16[512,512]{1,0:T(8,128)(2,1)S(1)}, u32[]{:S(2)}, u32[]{:S(2)}) collective-permute-start(bf16[512,512]{1,0:T(8,128)(2,1)S(1)} %collective-permute-done.4.refs_2_), channel_id=1, source_target_pairs={{0,16},{1,17},{2,18},{3,19},{4,20},{5,21},{6,22},{7,23},{8,24},{9,... | collective-permute-start | bytes 1572872 | tf_op jit(solution)/shard_map/ppermute | solution.py:404
  66.5 1.4 %collective-permute-start.19 = (bf16[512,512]{1,0:T(8,128)(2,1)S(1)}, bf16[512,512]{1,0:T(8,128)(2,1)S(1)}, u32[]{:S(2)}, u32[]{:S(2)}) collective-permute-start(bf16[512,512]{1,0:T(8,128)(2,1)S(1)} %collective-permute-done.9.refs_4_), channel_id=1, source_target_pairs={{0,2},{1,3},{2,0},{3,1},{4,6},{5,7},{6,4},{7,5},{8,10},{9,11},{10,... | collective-permute-start | bytes 1572872 | tf_op jit(solution)/shard_map/ppermute | solution.py:404
  67.9 1.5 %collective-permute-done.14.y3_other = bf16[512,512]{1,0:T(8,128)(2,1)S(1)} collective-permute-done((bf16[512,512]{1,0:T(8,128)(2,1)S(1)}, bf16[512,512]{1,0:T(8,128)(2,1)S(1)}, u32[]{:S(2)}, u32[]{:S(2)}) %collective-permute-start.14) | collective-permute-done | bytes 524320 | tf_op jit(solution)/shard_map/ppermute | solution.py:404
  70.2 4.7 %held_keys.1 = (bf16[512,1024]{1,0:T(8,128)(2,1)}, f32[512,512]{1,0:T(8,128)S(1)}) custom-call(s32[18]{0:T(128)S(1)} %copy-done.2, s32[1]{0:T(128)S(6)} %copy.15.count, s32[512]{0:T(512)S(1)} %copy-done.3, bf16[512,8192]{1,0:T(8,128)(2,1)} %tok_ref.7, f32[512,512]{1,0:T(8,128)S(1)} %get-tuple-element.116.mine_h, f32[512,512]{1,0:T(8,128)S(1)} %get-tuple-element.117.mine_c, ...), custom_call_target="tpu_custom_call" | custom-call | flops 1000 | bytes 1024 | tf_op jit(solution)/shard_map/held_keys/pallas_call | solution.py:376
  74.9 1.6 %collective-permute-start.16 = (bf16[512,512]{1,0:T(8,128)(2,1)S(1)}, bf16[512,512]{1,0:T(8,128)(2,1)S(1)}, u32[]{:S(2)}, u32[]{:S(2)}) collective-permute-start(bf16[512,512]{1,0:T(8,128)(2,1)S(1)} %collective-permute-done.10.y3), channel_id=1, source_target_pairs={{0,16},{1,17},{2,18},{3,19},{4,20},{5,21},{6,22},{7,23},{8,24},{9,... | collective-permute-start | bytes 1572872 | tf_op jit(solution)/shard_map/ppermute | solution.py:404
  76.4 1.4 %collective-permute-start.17 = (bf16[512,512]{1,0:T(8,128)(2,1)S(1)}, bf16[512,512]{1,0:T(8,128)(2,1)S(1)}, u32[]{:S(2)}, u32[]{:S(2)}) collective-permute-start(bf16[512,512]{1,0:T(8,128)(2,1)S(1)} %get-tuple-element.122), channel_id=1, source_target_pairs={{0,2},{1,3},{2,0},{3,1},{4,6},{5,7},{6,4},{7,5},{8,10},{9,11},{10,... | collective-permute-start | bytes 1572872 | tf_op jit(solution)/shard_map/ppermute | solution.py:404
  77.9 1.2 %collective-permute-start.20 = (bf16[1,576,128]{2,1,0:T(8,128)(2,1)S(1)}, bf16[1,576,128]{2,1,0:T(8,128)(2,1)S(1)}, u32[]{:S(2)}, u32[]{:S(2)}) collective-permute-start(bf16[1,576,128]{2,1,0:T(8,128)(2,1)S(1)} %get-tuple-element.131), channel_id=1, source_target_pairs={{0,8},{1,9},{2,10},{3,11},{4,12},{5,13},{6,14},{7,15},{8,0},{9,1},... | collective-permute-start | bytes 442376 | tf_op jit(solution)/shard_map/ppermute | solution.py:404
  79.7 1.5 %collective-permute-start.21 = (bf16[1,576,128]{2,1,0:T(8,128)(2,1)S(1)}, bf16[1,576,128]{2,1,0:T(8,128)(2,1)S(1)}, u32[]{:S(2)}, u32[]{:S(2)}) collective-permute-start(bf16[1,576,128]{2,1,0:T(8,128)(2,1)S(1)} %get-tuple-element.132), channel_id=1, source_target_pairs={{0,4},{1,5},{2,6},{3,7},{4,0},{5,1},{6,2},{7,3},{8,12},{9,13},{10,... | collective-permute-start | bytes 442376 | tf_op jit(solution)/shard_map/ppermute | solution.py:404
  81.3 2.2 %collective-permute-start.22 = (bf16[1,576,128]{2,1,0:T(8,128)(2,1)S(1)}, bf16[1,576,128]{2,1,0:T(8,128)(2,1)S(1)}, u32[]{:S(2)}, u32[]{:S(2)}) collective-permute-start(bf16[1,576,128]{2,1,0:T(8,128)(2,1)S(1)} %get-tuple-element.133), channel_id=1, source_target_pairs={{0,12},{1,13},{2,14},{3,15},{4,8},{5,9},{6,10},{7,11},{8,4},{9,5},... | collective-permute-start | bytes 442376 | tf_op jit(solution)/shard_map/ppermute | solution.py:404
  83.5 3.8 %crossed_products.1 = (f32[512,512]{1,0:T(8,128)S(1)}, f32[512,512]{1,0:T(8,128)S(1)}) custom-call(s32[18]{0:T(128)S(1)} %copy-done.2, bf16[512,8192]{1,0:T(8,128)(2,1)} %tok_ref.7, bf16[512,8192]{1,0:T(8,128)(2,1)} %collective-permute-done.2.refs_1_.sib_ref, f32[512,512]{1,0:T(8,128)S(1)} %get-tuple-element.124.total_ref, ...), custom_call_target="tpu_custom_call" | custom-call | flops 1000 | bytes 1024 | tf_op jit(solution)/shard_map/crossed_products/pallas_call | solution.py:376
  87.2 3.5 %collective-permute-done.20.refs_0_ = bf16[1,576,128]{2,1,0:T(8,128)(2,1)S(1)} collective-permute-done((bf16[1,576,128]{2,1,0:T(8,128)(2,1)S(1)}, bf16[1,576,128]{2,1,0:T(8,128)(2,1)S(1)}, u32[]{:S(2)}, u32[]{:S(2)}) %collective-permute-start.20) | collective-permute-done | bytes 147488 | tf_op jit(solution)/shard_map/ppermute | solution.py:404
  92.9 3.4 %collective-permute-done.26.share_other = f32[1,576,128]{2,1,0:T(8,128)S(1)} collective-permute-done((f32[1,576,128]{2,1,0:T(8,128)S(1)}, f32[1,576,128]{2,1,0:T(8,128)S(1)}, u32[]{:S(2)}, u32[]{:S(2)}) %collective-permute-start.26) | collective-permute-done | bytes 294944 | tf_op jit(solution)/shard_map/ppermute | solution.py:404
  96.4 4.7 %crossed_keys.1 = (bf16[512,1024]{1,0:T(8,128)(2,1)}, f32[1024,128]{1,0:T(8,128)}, f32[128,128]{1,0:T(8,128)}) custom-call(s32[18]{0:T(128)S(1)} %copy-done.2, s32[1]{0:T(128)S(6)} %copy.15.count, s32[512]{0:T(512)S(1)} %copy-done.3, bf16[512,8192]{1,0:T(8,128)(2,1)} %tok_ref.7, ...), custom_call_target="tpu_custom_call", output_to_operand_aliasing={{0}: (13, {})} | custom-call | flops 1000 | bytes 1024 | tf_op jit(solution)/shard_map/crossed_keys/pallas_call | solution.py:376
  (42 shorter events, 8.1 us)
Async XLA Ops:
  1.7 17.2 %collective-permute-start.2 = (bf16[512,8192]{1,0:T(8,128)(2,1)}, bf16[512,8192]{1,0:T(8,128)(2,1)}, u32[]{:S(2)}, u32[]{:S(2)}) collective-permute-start(bf16[512,8192]{1,0:T(8,128)(2,1)} %tok_ref.7), channel_id=1, source_target_pairs={{0,1},{1,0},{2,3},{3,2},{4,5},{5,4},{6,7},{7,6},{8,9},{9,8},{10,11... | collective-permute-start | bytes 25165832 | tf_op jit(solution)/shard_map/ppermute | solution.py:404
  2.2 16.2 %collective-permute-start = (bf16[512,512]{1,0:T(8,128)(2,1)S(1)}, bf16[512,512]{1,0:T(8,128)(2,1)S(1)}, u32[]{:S(2)}, u32[]{:S(2)}) collective-permute-start(bf16[512,512]{1,0:T(8,128)(2,1)S(1)} %constant_dynamic-slice_fusion), channel_id=1, source_target_pairs={{0,4},{1,5},{2,6},{3,7},{4,12},{5,13},{6,14},{7,15},{8,0},{9,1},{1... | collective-permute-start | bytes 1572872 | tf_op jit(solution)/shard_map/ppermute | solution.py:404
  4.9 14.0 %collective-permute-start.1 = (bf16[512,512]{1,0:T(8,128)(2,1)S(1)}, bf16[512,512]{1,0:T(8,128)(2,1)S(1)}, u32[]{:S(2)}, u32[]{:S(2)}) collective-permute-start(bf16[512,512]{1,0:T(8,128)(2,1)S(1)} %constant_dynamic-slice_fusion), channel_id=1, source_target_pairs={{0,2},{1,3},{2,0},{3,1},{4,6},{5,7},{6,4},{7,5},{8,10},{9,11},{10,... | collective-permute-start | bytes 1572872 | tf_op jit(solution)/shard_map/ppermute | solution.py:404
  8.3 16.2 %copy-start.1 = (bf16[1024,128]{1,0:T(8,128)(2,1)S(1)}, bf16[1024,128]{1,0:T(8,128)(2,1)}, u32[]{:S(2)}) copy-start(bf16[1024,128]{1,0:T(8,128)(2,1)} %refs_7_.1) | copy-start | bytes 786436
  8.3 16.2 %copy-start.2 = (s32[18]{0:T(128)S(1)}, s32[18]{0:T(128)}, u32[]{:S(2)}) copy-start(s32[18]{0:T(128)} %dynamic-slice_bitcast_fusion.sc) | copy-start | bytes 220
  18.9 17.9 %collective-permute-start.6 = (bf16[8,576,128]{2,1,0:T(8,128)(2,1)S(1)}, bf16[8,576,128]{2,1,0:T(8,128)(2,1)S(1)}, u32[]{:S(2)}, u32[]{:S(2)}) collective-permute-start(bf16[8,576,128]{2,1,0:T(8,128)(2,1)S(1)} %get-tuple-element.80), channel_id=1, source_target_pairs={{0,1},{1,0},{2,3},{3,2},{4,5},{5,4},{6,7},{7,6},{8,9},{9,8},{10,11... | collective-permute-start | bytes 3538952 | tf_op jit(solution)/shard_map/ppermute | solution.py:404
  18.9 15.2 %collective-permute-start.3 = (bf16[512,512]{1,0:T(8,128)(2,1)S(1)}, bf16[512,512]{1,0:T(8,128)(2,1)S(1)}, u32[]{:S(2)}, u32[]{:S(2)}) collective-permute-start(bf16[512,512]{1,0:T(8,128)(2,1)S(1)} %collective-permute-done.refs_4_), channel_id=1, source_target_pairs={{0,4},{1,5},{2,6},{3,7},{4,12},{5,13},{6,14},{7,15},{8,0},{9,1},{1... | collective-permute-start | bytes 1572872 | tf_op jit(solution)/shard_map/ppermute | solution.py:404
  21.5 14.1 %collective-permute-start.4 = (bf16[512,512]{1,0:T(8,128)(2,1)S(1)}, bf16[512,512]{1,0:T(8,128)(2,1)S(1)}, u32[]{:S(2)}, u32[]{:S(2)}) collective-permute-start(bf16[512,512]{1,0:T(8,128)(2,1)S(1)} %collective-permute-done.refs_4_), channel_id=1, source_target_pairs={{0,2},{1,3},{2,0},{3,1},{4,6},{5,7},{6,4},{7,5},{8,10},{9,11},{10,... | collective-permute-start | bytes 1572872 | tf_op jit(solution)/shard_map/ppermute | solution.py:404
  23.0 13.8 %collective-permute-start.5 = (bf16[512,512]{1,0:T(8,128)(2,1)S(1)}, bf16[512,512]{1,0:T(8,128)(2,1)S(1)}, u32[]{:S(2)}, u32[]{:S(2)}) collective-permute-start(bf16[512,512]{1,0:T(8,128)(2,1)S(1)} %collective-permute-done.refs_4_), channel_id=1, source_target_pairs={{0,16},{1,17},{2,18},{3,19},{4,20},{5,21},{6,22},{7,23},{8,24},{9,... | collective-permute-start | bytes 1572872 | tf_op jit(solution)/shard_map/ppermute | solution.py:404
  36.8 13.8 %collective-permute-start.7 = (bf16[512,512]{1,0:T(8,128)(2,1)S(1)}, bf16[512,512]{1,0:T(8,128)(2,1)S(1)}, u32[]{:S(2)}, u32[]{:S(2)}) collective-permute-start(bf16[512,512]{1,0:T(8,128)(2,1)S(1)} %collective-permute-done.3.refs_3_), channel_id=1, source_target_pairs={{0,4},{1,5},{2,6},{3,7},{4,12},{5,13},{6,14},{7,15},{8,0},{9,1},{1... | collective-permute-start | bytes 1572872 | tf_op jit(solution)/shard_map/ppermute | solution.py:404
  38.0 12.6 %collective-permute-start.8 = (bf16[512,512]{1,0:T(8,128)(2,1)S(1)}, bf16[512,512]{1,0:T(8,128)(2,1)S(1)}, u32[]{:S(2)}, u32[]{:S(2)}) collective-permute-start(bf16[512,512]{1,0:T(8,128)(2,1)S(1)} %collective-permute-done.3.refs_3_), channel_id=1, source_target_pairs={{0,2},{1,3},{2,0},{3,1},{4,6},{5,7},{6,4},{7,5},{8,10},{9,11},{10,... | collective-permute-start | bytes 1572872 | tf_op jit(solution)/shard_map/ppermute | solution.py:404
  38.5 12.4 %collective-permute-start.9 = (bf16[512,512]{1,0:T(8,128)(2,1)S(1)}, bf16[512,512]{1,0:T(8,128)(2,1)S(1)}, u32[]{:S(2)}, u32[]{:S(2)}) collective-permute-start(bf16[512,512]{1,0:T(8,128)(2,1)S(1)} %collective-permute-done.3.refs_3_), channel_id=1, source_target_pairs={{0,16},{1,17},{2,18},{3,19},{4,20},{5,21},{6,22},{7,23},{8,24},{9,... | collective-permute-start | bytes 1572872 | tf_op jit(solution)/shard_map/ppermute | solution.py:404
  50.9 19.3 %copy-start = (f32[320,128]{1,0:T(8,128)S(1)}, f32[320,128]{1,0:T(8,128)}, u32[]{:S(2)}) copy-start(f32[320,128]{1,0:T(8,128)} %constant.28.clone.tab_ref) | copy-start | bytes 491524
  50.9 19.3 %copy-start.3 = (s32[512]{0:T(512)S(1)}, s32[512]{0:T(512)}, u32[]{:S(2)}) copy-start(s32[512]{0:T(512)} %pos.5) | copy-start | bytes 6148
  50.9 13.6 %collective-permute-start.12 = (bf16[4,576,128]{2,1,0:T(8,128)(2,1)S(1)}, bf16[4,576,128]{2,1,0:T(8,128)(2,1)S(1)}, u32[]{:S(2)}, u32[]{:S(2)}) collective-permute-start(bf16[4,576,128]{2,1,0:T(8,128)(2,1)S(1)} %get-tuple-element.105), channel_id=1, source_target_pairs={{0,2},{1,3},{2,0},{3,1},{4,6},{5,7},{6,4},{7,5},{8,10},{9,11},{10,... | collective-permute-start | bytes 1769480 | tf_op jit(solution)/shard_map/ppermute | solution.py:404
  52.3 12.0 %collective-permute-start.10 = (bf16[512,512]{1,0:T(8,128)(2,1)S(1)}, bf16[512,512]{1,0:T(8,128)(2,1)S(1)}, u32[]{:S(2)}, u32[]{:S(2)}) collective-permute-start(bf16[512,512]{1,0:T(8,128)(2,1)S(1)} %collective-permute-done.8.refs_2_), channel_id=1, source_target_pairs={{0,4},{1,5},{2,6},{3,7},{4,12},{5,13},{6,14},{7,15},{8,0},{9,1},{1... | collective-permute-start | bytes 1572872 | tf_op jit(solution)/shard_map/ppermute | solution.py:404
  52.9 11.6 %collective-permute-start.11 = (bf16[512,512]{1,0:T(8,128)(2,1)S(1)}, bf16[512,512]{1,0:T(8,128)(2,1)S(1)}, u32[]{:S(2)}, u32[]{:S(2)}) collective-permute-start(bf16[512,512]{1,0:T(8,128)(2,1)S(1)} %collective-permute-done.7.refs_3_), channel_id=1, source_target_pairs={{0,16},{1,17},{2,18},{3,19},{4,20},{5,21},{6,22},{7,23},{8,24},{9,... | collective-permute-start | bytes 1572872 | tf_op jit(solution)/shard_map/ppermute | solution.py:404
  64.5 5.7 %collective-permute-start.13 = (f32[512,1024]{1,0:T(8,128)S(1)}, f32[512,1024]{1,0:T(8,128)S(1)}, u32[]{:S(2)}, u32[]{:S(2)}) collective-permute-start(f32[512,1024]{1,0:T(8,128)S(1)} %get-tuple-element.119), channel_id=1, source_target_pairs={{0,1},{1,0},{2,3},{3,2},{4,5},{5,4},{6,7},{7,6},{8,9},{9,8},{10,11... | collective-permute-start | bytes 6291464 | tf_op jit(solution)/shard_map/ppermute | solution.py:404
  64.5 4.9 %collective-permute-start.14 = (bf16[512,512]{1,0:T(8,128)(2,1)S(1)}, bf16[512,512]{1,0:T(8,128)(2,1)S(1)}, u32[]{:S(2)}, u32[]{:S(2)}) collective-permute-start(bf16[512,512]{1,0:T(8,128)(2,1)S(1)} %collective-permute-done.10.y3), channel_id=1, source_target_pairs={{0,1},{1,0},{2,3},{3,2},{4,5},{5,4},{6,7},{7,6},{8,9},{9,8},{10,11... | collective-permute-start | bytes 1572872 | tf_op jit(solution)/shard_map/ppermute | solution.py:404
  65.0 5.1 %collective-permute-start.15 = (bf16[512,512]{1,0:T(8,128)(2,1)S(1)}, bf16[512,512]{1,0:T(8,128)(2,1)S(1)}, u32[]{:S(2)}, u32[]{:S(2)}) collective-permute-start(bf16[512,512]{1,0:T(8,128)(2,1)S(1)} %collective-permute-done.11.a3), channel_id=1, source_target_pairs={{0,1},{1,0},{2,3},{3,2},{4,5},{5,4},{6,7},{7,6},{8,9},{9,8},{10,11... | collective-permute-start | bytes 1572872 | tf_op jit(solution)/shard_map/ppermute | solution.py:404
  65.0 14.7 %collective-permute-start.18 = (bf16[512,512]{1,0:T(8,128)(2,1)S(1)}, bf16[512,512]{1,0:T(8,128)(2,1)S(1)}, u32[]{:S(2)}, u32[]{:S(2)}) collective-permute-start(bf16[512,512]{1,0:T(8,128)(2,1)S(1)} %collective-permute-done.4.refs_2_), channel_id=1, source_target_pairs={{0,16},{1,17},{2,18},{3,19},{4,20},{5,21},{6,22},{7,23},{8,24},{9,... | collective-permute-start | bytes 1572872 | tf_op jit(solution)/shard_map/ppermute | solution.py:404
  66.5 14.8 %collective-permute-start.19 = (bf16[512,512]{1,0:T(8,128)(2,1)S(1)}, bf16[512,512]{1,0:T(8,128)(2,1)S(1)}, u32[]{:S(2)}, u32[]{:S(2)}) collective-permute-start(bf16[512,512]{1,0:T(8,128)(2,1)S(1)} %collective-permute-done.9.refs_4_), channel_id=1, source_target_pairs={{0,2},{1,3},{2,0},{3,1},{4,6},{5,7},{6,4},{7,5},{8,10},{9,11},{10,... | collective-permute-start | bytes 1572872 | tf_op jit(solution)/shard_map/ppermute | solution.py:404
  74.9 16.1 %collective-permute-start.16 = (bf16[512,512]{1,0:T(8,128)(2,1)S(1)}, bf16[512,512]{1,0:T(8,128)(2,1)S(1)}, u32[]{:S(2)}, u32[]{:S(2)}) collective-permute-start(bf16[512,512]{1,0:T(8,128)(2,1)S(1)} %collective-permute-done.10.y3), channel_id=1, source_target_pairs={{0,16},{1,17},{2,18},{3,19},{4,20},{5,21},{6,22},{7,23},{8,24},{9,... | collective-permute-start | bytes 1572872 | tf_op jit(solution)/shard_map/ppermute | solution.py:404
  76.4 15.4 %collective-permute-start.17 = (bf16[512,512]{1,0:T(8,128)(2,1)S(1)}, bf16[512,512]{1,0:T(8,128)(2,1)S(1)}, u32[]{:S(2)}, u32[]{:S(2)}) collective-permute-start(bf16[512,512]{1,0:T(8,128)(2,1)S(1)} %get-tuple-element.122), channel_id=1, source_target_pairs={{0,2},{1,3},{2,0},{3,1},{4,6},{5,7},{6,4},{7,5},{8,10},{9,11},{10,... | collective-permute-start | bytes 1572872 | tf_op jit(solution)/shard_map/ppermute | solution.py:404
  77.9 12.8 %collective-permute-start.20 = (bf16[1,576,128]{2,1,0:T(8,128)(2,1)S(1)}, bf16[1,576,128]{2,1,0:T(8,128)(2,1)S(1)}, u32[]{:S(2)}, u32[]{:S(2)}) collective-permute-start(bf16[1,576,128]{2,1,0:T(8,128)(2,1)S(1)} %get-tuple-element.131), channel_id=1, source_target_pairs={{0,8},{1,9},{2,10},{3,11},{4,12},{5,13},{6,14},{7,15},{8,0},{9,1},... | collective-permute-start | bytes 442376 | tf_op jit(solution)/shard_map/ppermute | solution.py:404
  79.7 11.2 %collective-permute-start.21 = (bf16[1,576,128]{2,1,0:T(8,128)(2,1)S(1)}, bf16[1,576,128]{2,1,0:T(8,128)(2,1)S(1)}, u32[]{:S(2)}, u32[]{:S(2)}) collective-permute-start(bf16[1,576,128]{2,1,0:T(8,128)(2,1)S(1)} %get-tuple-element.132), channel_id=1, source_target_pairs={{0,4},{1,5},{2,6},{3,7},{4,0},{5,1},{6,2},{7,3},{8,12},{9,13},{10,... | collective-permute-start | bytes 442376 | tf_op jit(solution)/shard_map/ppermute | solution.py:404
  81.3 9.7 %collective-permute-start.22 = (bf16[1,576,128]{2,1,0:T(8,128)(2,1)S(1)}, bf16[1,576,128]{2,1,0:T(8,128)(2,1)S(1)}, u32[]{:S(2)}, u32[]{:S(2)}) collective-permute-start(bf16[1,576,128]{2,1,0:T(8,128)(2,1)S(1)} %get-tuple-element.133), channel_id=1, source_target_pairs={{0,12},{1,13},{2,14},{3,15},{4,8},{5,9},{6,10},{7,11},{8,4},{9,5},... | collective-permute-start | bytes 442376 | tf_op jit(solution)/shard_map/ppermute | solution.py:404
  91.8 4.6 %collective-permute-start.25 = (f32[512,512]{1,0:T(8,128)S(1)}, f32[512,512]{1,0:T(8,128)S(1)}, u32[]{:S(2)}, u32[]{:S(2)}) collective-permute-start(f32[512,512]{1,0:T(8,128)S(1)} %get-tuple-element.137), channel_id=1, source_target_pairs={{0,1},{1,0},{2,3},{3,2},{4,5},{5,4},{6,7},{7,6},{8,9},{9,8},{10,11... | collective-permute-start | bytes 3145736 | tf_op jit(solution)/shard_map/ppermute | solution.py:404
  91.8 4.6 %collective-permute-start.23 = (bf16[512,512]{1,0:T(8,128)(2,1)S(1)}, bf16[512,512]{1,0:T(8,128)(2,1)S(1)}, u32[]{:S(2)}, u32[]{:S(2)}) collective-permute-start(bf16[512,512]{1,0:T(8,128)(2,1)S(1)} %collective-permute-done.16.e3), channel_id=1, source_target_pairs={{0,1},{1,0},{2,3},{3,2},{4,5},{5,4},{6,7},{7,6},{8,9},{9,8},{10,11... | collective-permute-start | bytes 1572872 | tf_op jit(solution)/shard_map/ppermute | solution.py:404
  92.3 4.1 %collective-permute-start.24 = (bf16[512,512]{1,0:T(8,128)(2,1)S(1)}, bf16[512,512]{1,0:T(8,128)(2,1)S(1)}, u32[]{:S(2)}, u32[]{:S(2)}) collective-permute-start(bf16[512,512]{1,0:T(8,128)(2,1)S(1)} %collective-permute-done.17.e0), channel_id=1, source_target_pairs={{0,1},{1,0},{2,3},{3,2},{4,5},{5,4},{6,7},{7,6},{8,9},{9,8},{10,11... | collective-permute-start | bytes 1572872 | tf_op jit(solution)/shard_map/ppermute | solution.py:404
  92.4 4.0 %collective-permute-start.26 = (f32[1,576,128]{2,1,0:T(8,128)S(1)}, f32[1,576,128]{2,1,0:T(8,128)S(1)}, u32[]{:S(2)}, u32[]{:S(2)}) collective-permute-start(f32[1,576,128]{2,1,0:T(8,128)S(1)} %share.1), channel_id=1, source_target_pairs={{0,1},{1,0},{2,3},{3,2},{4,5},{5,4},{6,7},{7,6},{8,9},{9,8},{10,11... | collective-permute-start | bytes 884744 | tf_op jit(solution)/shard_map/ppermute | solution.py:404

commit v4 on v3

--- a/solution.py
+++ b/solution.py
@@ -251,20 +251,25 @@
     last.wait()
 
 
-def crossed_kernel(sc, tok_ref, sib_ref, total_ref, e1, e2, mine_ref, theirs_ref, tv, wv, vc, sems, out_sems):
+def crossed_kernel(
+    sc, tok_ref, sib_ref, total_ref, e1, e2, mine_ref, theirs_ref, last_ref, last_sib_ref, tv, wv, vc, sems, out_sems,
+):
     deep = e1.shape[0]
     outer, copies = sc[8], []
+    columns = lambda node: pl.ds(pl.multiple_of((2 * sc[node] + outer) * deep, deep), deep)
     for i, (node, piece) in enumerate(((15, e1), (16, e2))):
         part = slice(i * deep, (i + 1) * deep)
-        at = pl.multiple_of((2 * sc[node] + outer) * deep, deep)
         copies.append((piece, wv.at[part, :]))
         for k, tok in enumerate((tok_ref, sib_ref)):
-            copies.append((tok.at[:, pl.ds(at, deep)], tv.at[k, :, part]))
+            copies.append((tok.at[:, columns(node)], tv.at[k, :, part]))
     copies.append((total_ref, vc.at[0]))
+    for i, node in enumerate((17, 14)):
+        copies.append((tok_ref.at[:, columns(node)], last_ref.at[i]))
+        copies.append((sib_ref.at[:, columns(node)], last_sib_ref.at[i]))
     made = [pltpu.make_async_copy(src, dst, sems.at[i]) for i, (src, dst) in enumerate(copies)]
     for c in made:
         c.start()
-    for c in made:
+    for c in made[:7]:
         c.wait()
     saves = []
     for k, dst in enumerate((mine_ref, theirs_ref)):
@@ -272,8 +277,15 @@
         vc[k] = part if k else vc[0] + part
         saves.append(pltpu.make_async_copy(vc.at[k], dst, out_sems.at[k]))
         saves[-1].start()
-    for c in saves:
+    for c in made[7:] + saves:
         c.wait()
+
+
+def last_kernel(total_ref, tok_ref, e3, e0, out_ref):
+    total = total_ref[...]
+    for i, w in enumerate((e3, e0)):
+        total = total + jnp.dot(tok_ref[i], w[...], preferred_element_type=jnp.float32)
+    out_ref[...] = total.astype(out_ref.dtype)
 
 
 def fold_kernel(keep_ref, got_ref, next_ref, *send_refs):
@@ -293,45 +305,31 @@
 
 
 def crossed_keys_kernel(
-    sc, count, pos, tok_ref, total_ref, e3, e0, e3_other, e0_other, given, share, share_other, tab_ref,
-    keys_ref, out_ref, down_ref, up_ref, tv, wv, vc, res, sems,
+    sc, count, pos, total_ref, given, share, share_other, tab_ref, keys_ref, out_ref, down_ref, up_ref, res, sems,
 ):
-    deep, half = e3.shape
+    half = total_ref.shape[1]
     outer = sc[8]
     down_rows = down_ref.shape[0] // 2
     up_rows = up_ref.shape[0] // 2
-    made = load_tokens(sc, tok_ref, (17, 14), (e3, e0), tv, wv, sems)
-    total = pltpu.make_async_copy(total_ref, vc, sems.at[6])
-    total.start()
     saves = []
-    for i, (core, sums) in enumerate(((outer, share), (1 - outer, share_other))):
+
+    def save(src, dst):
+        c = pltpu.make_async_copy(src, dst, sems.at[len(saves)])
+        c.start()
+        saves.append(c)
+
+    for core, sums in ((outer, share), (1 - outer, share_other)):
         down_at = pl.multiple_of(core * down_rows, down_rows)
         up_at = pl.multiple_of(core * up_rows, up_rows)
-        saves += [
-            pltpu.make_async_copy(
-                sums.at[0, 0:down_rows, :], down_ref.at[pl.ds(down_at, down_rows), :], sems.at[7 + 2 * i]
-            ),
-            pltpu.make_async_copy(
-                sums.at[0, down_rows:, :], up_ref.at[pl.ds(up_at, up_rows), :], sems.at[8 + 2 * i]
-            ),
-        ]
-    for c in saves:
-        c.start()
-    for c in made:
-        c.wait()
-    total.wait()
+        save(sums.at[0, 0:down_rows, :], down_ref.at[pl.ds(down_at, down_rows), :])
+        save(sums.at[0, down_rows:, :], up_ref.at[pl.ds(up_at, up_rows), :])
+    columns = pl.ds(pl.multiple_of((1 - sc[9]) * half, half), half)
 
     def write(at, cosine, sine):
-        pre = vc[at, :] + given[at, :] + dots(tv.at[at, :], (0, 2 * deep, 3 * deep), (wv, e3_other, e0_other))
-        rotate_heads(pre, cosine, sine, res, at)
-
-    rope_blocks(pos, count, tab_ref, vc.shape[0], write)
-    saves.append(
-        pltpu.make_async_copy(
-            res, out_ref.at[:, pl.ds(pl.multiple_of((1 - sc[9]) * half, half), half)], sems.at[11]
-        )
-    )
-    saves[-1].start()
+        rotate_heads(total_ref[at, :] + given[at, :].astype(jnp.float32), cosine, sine, res, at)
+        save(res.at[at, :], out_ref.at[at, columns])
+
+    rope_blocks(pos, count, tab_ref, res.shape[0], write)
     for c in saves:
         c.wait()
 
@@ -509,30 +507,34 @@
     e3 = send(y3, to_x)
     e0 = send(c0, to_y)
     e1, e2, total = fence(e1, e2, total)
-    mine, theirs = call(
-        crossed_kernel, "crossed_products", [pltpu.VMEM((rows, half), f32)] * 2,
-        [HBM] * 2 + [ANY] * 3, [ANY, ANY],
+    *sums, last, last_sib = call(
+        crossed_kernel, "crossed_products",
+        [pltpu.VMEM((rows, half), f32)] * 2 + [pltpu.VMEM((2, rows, deep), bf16)] * 2,
+        [HBM] * 2 + [ANY] * 3, [ANY] * 4,
         [
             pltpu.VMEM((2, rows, chunk), bf16), pltpu.VMEM((chunk, half), bf16),
-            pltpu.VMEM((2, rows, half), f32), dma((7,)), dma((2,)),
+            pltpu.VMEM((2, rows, half), f32), dma((11,)), dma((2,)),
         ],
         (sc, tokens, sib_tokens, total, e1, e2),
     )
-    e3, e0, mine, theirs, *got = fence(e3, e0, mine, theirs, *got)
+    e3, e0, mine, theirs, last, last_sib, *got = fence(e3, e0, *sums, last, last_sib, *got)
 
     share = call(
         sum_kernel, "share", pltpu.VMEM(keep.shape, f32), [vm] * 4, vm, [], (keep, *got), prefetch=0,
     )
+    finish = lambda total, toks, dtype: call(
+        last_kernel, "last_product", pltpu.VMEM((rows, half), dtype), [vm] * 4, vm, [], (total, toks, e3, e0), prefetch=0,
+    )
+    given = send(finish(theirs, last_sib, bf16), to_core)
     keys, down, up = call(
         crossed_keys_kernel, "crossed_keys",
         [shape((rows, kv), bf16), shape((chunk, rank), f32), shape((kv // nodes, rank), f32)],
-        [HBM] + [ANY] * 3 + [vm] * 6 + [ANY], [ANY] * 3,
-        own_space + [pltpu.VMEM((rows, half), bf16), dma((12,))],
+        [vm] * 5 + [ANY], [ANY] * 3,
+        [pltpu.VMEM((rows, half), bf16), dma((4 + rows // BLK,))],
         (
-            sc, block_counts, positions, tokens, mine, e3, e0, send(e3, to_core), send(e0, to_core),
-            send(theirs, to_core), share, send(share, to_core), tab, keys,
+            sc, block_counts, positions, finish(mine, last, f32), given, share, send(share, to_core), tab, keys,
         ),
-        prefetch=3, aliases={13: 0},
+        prefetch=3, aliases={8: 0},
     )
     return keys, down, up
 

time: 102 us -> 97.1 us (0.952)
  waiting for transfers between devices: 29.4 us -> 26.9 us
  Pallas kernels: 38.6 us -> 37.1 us
    ppermute x27 -> x25, waiting for transfers between devices: 29.4 us -> 26.9 us  [fast_body(): send = lambda x, f: lax.ppermute(x, ALL, routes.pairs(f))]
    pallas_call x10 -> x12, Pallas kernels: 38.6 us -> 37.1 us  [call(): pl.pallas_call(kernel, out_shape=shapes, grid_spec=pltpu.PrefetchScalarGr...]
    ppermute x27 -> x25, starting transfers between devices: 29.4 us -> 29 us  [fast_body(): send = lambda x, f: lax.ppermute(x, ALL, routes.pairs(f))]
  transfers between devices with their start and end apart: 27 -> 25, of which waited for: 16 -> 16; matrix products, arithmetic and copies ran while one was open for 1% -> 1% of each run, Pallas kernels for 33% -> 36%
where the time goes in v4:
time: 97.1 us; the launch traced here: 96.8 us
  Pallas kernels  37.1 us (38%)
  starting transfers between devices  29 us (30%)
  waiting for transfers between devices  26.9 us (28%)
  local copies, waits for them, and re-layouts  2.3 us (2%)
  between operations  1.57 us (2%)
    pallas_call x12, Pallas kernels, call(): pl.pallas_call(kernel, out_shape=shapes, grid_spec=pltpu.PrefetchScalarGr...  37.1 us
    ppermute x25, starting transfers between devices, fast_body(): send = lambda x, f: lax.ppermute(x, ALL, routes.pairs(f))  29 us
    ppermute x25, waiting for transfers between devices, fast_body(): send = lambda x, f: lax.ppermute(x, ALL, routes.pairs(f))  26.9 us
  transfers between devices with their start and end apart: 25, of which 16 were waited for; matrix products, arithmetic and copies ran while one was open for 1% of the time, Pallas kernels for 36%

profile of v4, /device:TPU:0, one launch (start us, length us, event | category | flops | bytes accessed | tf_op | source)
XLA Modules:
  0.0 96.8 jit_solution(17981893851403115891)
XLA Ops:
  0.6 1.1 %constant_dynamic-slice_fusion = bf16[512,512]{1,0:T(8,128)(2,1)S(1)} fusion(bf16[512,1024]{1,0:T(8,128)(2,1)} %refs_5_.1, s32[]{:T(128)S(6)} %select_n.6), kind=kLoop, calls=%fused_computation.1 | loop fusion | bytes 1048580 | tf_op jit(solution)/shard_map/dynamic_slice | solution.py:443
  2.2 2.6 %collective-permute-start = (bf16[512,512]{1,0:T(8,128)(2,1)S(1)}, bf16[512,512]{1,0:T(8,128)(2,1)S(1)}, u32[]{:S(2)}, u32[]{:S(2)}) collective-permute-start(bf16[512,512]{1,0:T(8,128)(2,1)S(1)} %constant_dynamic-slice_fusion), channel_id=1, source_target_pairs={{0,4},{1,5},{2,6},{3,7},{4,12},{5,13},{6,14},{7,15},{8,0},{9,1},{1... | collective-permute-start | bytes 1572872 | tf_op jit(solution)/shard_map/ppermute | solution.py:402
  4.9 1.5 %collective-permute-start.1 = (bf16[512,512]{1,0:T(8,128)(2,1)S(1)}, bf16[512,512]{1,0:T(8,128)(2,1)S(1)}, u32[]{:S(2)}, u32[]{:S(2)}) collective-permute-start(bf16[512,512]{1,0:T(8,128)(2,1)S(1)} %constant_dynamic-slice_fusion), channel_id=1, source_target_pairs={{0,2},{1,3},{2,0},{3,1},{4,6},{5,7},{6,4},{7,5},{8,10},{9,11},{10,... | collective-permute-start | bytes 1572872 | tf_op jit(solution)/shard_map/ppermute | solution.py:402
  7.1 1.2 %dynamic-slice_bitcast_fusion.sc = s32[18]{0:T(128)} fusion(s32[32,18]{1,0:T(8,128)} %constant.29.clone, s32[]{:T(128)S(6)} %select_n.7), kind=kLoop, calls=%fused_computation | loop fusion | bytes 148 | tf_op jit(solution)/shard_map/squeeze | solution.py:445
  8.3 10.0 %adapter_gradients.1 = (bf16[512,128]{1,0:T(8,128)(2,1)S(1)}, f32[8,576,128]{2,1,0:T(8,128)S(1)}, bf16[8,576,128]{2,1,0:T(8,128)(2,1)S(1)}) custom-call(s32[18]{0:T(128)} %dynamic-slice_bitcast_fusion.sc, s32[4]{0:T(128)} %tids.1, s32[1]{0:T(128)S(6)} %copy.15.count, s32[512]{0:T(512)} %pos.5, bf16[512,8192]{1,0:T(8,128)(2,1)} %tok_ref.5, ...), custom_call_target="tpu_custom_call" | custom-call | flops 1000 | bytes 1024 | tf_op jit(solution)/shard_map/adapter_gradients/pallas_call | solution.py:374
  18.9 2.6 %collective-permute-start.3 = (bf16[512,512]{1,0:T(8,128)(2,1)S(1)}, bf16[512,512]{1,0:T(8,128)(2,1)S(1)}, u32[]{:S(2)}, u32[]{:S(2)}) collective-permute-start(bf16[512,512]{1,0:T(8,128)(2,1)S(1)} %collective-permute-done.refs_4_), channel_id=1, source_target_pairs={{0,4},{1,5},{2,6},{3,7},{4,12},{5,13},{6,14},{7,15},{8,0},{9,1},{1... | collective-permute-start | bytes 1572872 | tf_op jit(solution)/shard_map/ppermute | solution.py:402
  21.5 1.5 %collective-permute-start.4 = (bf16[512,512]{1,0:T(8,128)(2,1)S(1)}, bf16[512,512]{1,0:T(8,128)(2,1)S(1)}, u32[]{:S(2)}, u32[]{:S(2)}) collective-permute-start(bf16[512,512]{1,0:T(8,128)(2,1)S(1)} %collective-permute-done.refs_4_), channel_id=1, source_target_pairs={{0,2},{1,3},{2,0},{3,1},{4,6},{5,7},{6,4},{7,5},{8,10},{9,11},{10,... | collective-permute-start | bytes 1572872 | tf_op jit(solution)/shard_map/ppermute | solution.py:402
  23.0 1.5 %collective-permute-start.5 = (bf16[512,512]{1,0:T(8,128)(2,1)S(1)}, bf16[512,512]{1,0:T(8,128)(2,1)S(1)}, u32[]{:S(2)}, u32[]{:S(2)}) collective-permute-start(bf16[512,512]{1,0:T(8,128)(2,1)S(1)} %collective-permute-done.refs_4_), channel_id=1, source_target_pairs={{0,16},{1,17},{2,18},{3,19},{4,20},{5,21},{6,22},{7,23},{8,24},{9,... | collective-permute-start | bytes 1572872 | tf_op jit(solution)/shard_map/ppermute | solution.py:402
  24.5 5.8 %products.3 = (f32[512,512]{1,0:T(8,128)S(1)}, f32[512,512]{1,0:T(8,128)S(1)}, f32[512,512]{1,0:T(8,128)S(1)}, f32[512,512]{1,0:T(8,128)S(1)}, bf16[512,512]{1,0:T(8,128)(2,1)S(1)}) custom-call(s32[18]{0:T(128)S(1)} %copy-done.2, bf16[512,8192]{1,0:T(8,128)(2,1)} %tok_ref.5, bf16[512,8192]{1,0:T(8,128)(2,1)} %collective-permute-done.2.refs_1_.sib_ref, ...), custom_call_target="tpu_custom_call" | custom-call | flops 1000 | bytes 1024 | tf_op jit(solution)/shard_map/products/pallas_call | solution.py:374
  30.2 3.9 %collective-permute-done.3.refs_3_ = bf16[512,512]{1,0:T(8,128)(2,1)S(1)} collective-permute-done((bf16[512,512]{1,0:T(8,128)(2,1)S(1)}, bf16[512,512]{1,0:T(8,128)(2,1)S(1)}, u32[]{:S(2)}, u32[]{:S(2)}) %collective-permute-start.3) | collective-permute-done | bytes 524320 | tf_op jit(solution)/shard_map/ppermute | solution.py:402
  34.1 1.4 %collective-permute-done.4.refs_2_ = bf16[512,512]{1,0:T(8,128)(2,1)S(1)} collective-permute-done((bf16[512,512]{1,0:T(8,128)(2,1)S(1)}, bf16[512,512]{1,0:T(8,128)(2,1)S(1)}, u32[]{:S(2)}, u32[]{:S(2)}) %collective-permute-start.4) | collective-permute-done | bytes 524320 | tf_op jit(solution)/shard_map/ppermute | solution.py:402
  35.5 1.2 %collective-permute-done.5.refs_4_ = bf16[512,512]{1,0:T(8,128)(2,1)S(1)} collective-permute-done((bf16[512,512]{1,0:T(8,128)(2,1)S(1)}, bf16[512,512]{1,0:T(8,128)(2,1)S(1)}, u32[]{:S(2)}, u32[]{:S(2)}) %collective-permute-start.5) | collective-permute-done | bytes 524320 | tf_op jit(solution)/shard_map/ppermute | solution.py:402
  36.8 1.2 %collective-permute-start.7 = (bf16[512,512]{1,0:T(8,128)(2,1)S(1)}, bf16[512,512]{1,0:T(8,128)(2,1)S(1)}, u32[]{:S(2)}, u32[]{:S(2)}) collective-permute-start(bf16[512,512]{1,0:T(8,128)(2,1)S(1)} %collective-permute-done.3.refs_3_), channel_id=1, source_target_pairs={{0,4},{1,5},{2,6},{3,7},{4,12},{5,13},{6,14},{7,15},{8,0},{9,1},{1... | collective-permute-start | bytes 1572872 | tf_op jit(solution)/shard_map/ppermute | solution.py:402
  38.5 1.5 %collective-permute-start.9 = (bf16[512,512]{1,0:T(8,128)(2,1)S(1)}, bf16[512,512]{1,0:T(8,128)(2,1)S(1)}, u32[]{:S(2)}, u32[]{:S(2)}) collective-permute-start(bf16[512,512]{1,0:T(8,128)(2,1)S(1)} %collective-permute-done.3.refs_3_), channel_id=1, source_target_pairs={{0,16},{1,17},{2,18},{3,19},{4,20},{5,21},{6,22},{7,23},{8,24},{9,... | collective-permute-start | bytes 1572872 | tf_op jit(solution)/shard_map/ppermute | solution.py:402
  40.1 4.6 %products.4 = (f32[512,512]{1,0:T(8,128)S(1)}, f32[512,512]{1,0:T(8,128)S(1)}, f32[512,512]{1,0:T(8,128)S(1)}, f32[512,512]{1,0:T(8,128)S(1)}) custom-call(s32[18]{0:T(128)S(1)} %copy-done.2, bf16[512,8192]{1,0:T(8,128)(2,1)} %tok_ref.5, bf16[512,8192]{1,0:T(8,128)(2,1)} %collective-permute-done.2.refs_1_.sib_ref, ...), custom_call_target="tpu_custom_call" | custom-call | flops 1000 | bytes 1024 | tf_op jit(solution)/shard_map/products/pallas_call | solution.py:374
  44.7 5.9 %collective-permute-done.7.refs_3_ = bf16[512,512]{1,0:T(8,128)(2,1)S(1)} collective-permute-done((bf16[512,512]{1,0:T(8,128)(2,1)S(1)}, bf16[512,512]{1,0:T(8,128)(2,1)S(1)}, u32[]{:S(2)}, u32[]{:S(2)}) %collective-permute-start.7) | collective-permute-done | bytes 524320 | tf_op jit(solution)/shard_map/ppermute | solution.py:402
  50.9 1.4 %collective-permute-start.12 = (bf16[4,576,128]{2,1,0:T(8,128)(2,1)S(1)}, bf16[4,576,128]{2,1,0:T(8,128)(2,1)S(1)}, u32[]{:S(2)}, u32[]{:S(2)}) collective-permute-start(bf16[4,576,128]{2,1,0:T(8,128)(2,1)S(1)} %get-tuple-element.109), channel_id=1, source_target_pairs={{0,2},{1,3},{2,0},{3,1},{4,6},{5,7},{6,4},{7,5},{8,10},{9,11},{10,... | collective-permute-start | bytes 1769480 | tf_op jit(solution)/shard_map/ppermute | solution.py:402
  52.9 1.5 %collective-permute-start.11 = (bf16[512,512]{1,0:T(8,128)(2,1)S(1)}, bf16[512,512]{1,0:T(8,128)(2,1)S(1)}, u32[]{:S(2)}, u32[]{:S(2)}) collective-permute-start(bf16[512,512]{1,0:T(8,128)(2,1)S(1)} %collective-permute-done.7.refs_3_), channel_id=1, source_target_pairs={{0,16},{1,17},{2,18},{3,19},{4,20},{5,21},{6,22},{7,23},{8,24},{9,... | collective-permute-start | bytes 1572872 | tf_op jit(solution)/shard_map/ppermute | solution.py:402
  54.4 4.7 %products.5 = (f32[512,512]{1,0:T(8,128)S(1)}, f32[512,512]{1,0:T(8,128)S(1)}, f32[512,1024]{1,0:T(8,128)S(1)}) custom-call(s32[18]{0:T(128)S(1)} %copy-done.2, bf16[512,8192]{1,0:T(8,128)(2,1)} %tok_ref.5, bf16[512,8192]{1,0:T(8,128)(2,1)} %collective-permute-done.2.refs_1_.sib_ref, bf16[512,512]{1,0:T(8,128)(2,1)S(1)} %collective-permute-done.8.refs_2_, ...), custom_call_target="tpu_custom_call" | custom-call | flops 1000 | bytes 1024 | tf_op jit(solution)/shard_map/products/pallas_call | solution.py:374
  59.1 5.1 %collective-permute-done.10.y3 = bf16[512,512]{1,0:T(8,128)(2,1)S(1)} collective-permute-done((bf16[512,512]{1,0:T(8,128)(2,1)S(1)}, bf16[512,512]{1,0:T(8,128)(2,1)S(1)}, u32[]{:S(2)}, u32[]{:S(2)}) %collective-permute-start.10) | collective-permute-done | bytes 524320 | tf_op jit(solution)/shard_map/ppermute | solution.py:402
  65.0 1.5 %collective-permute-start.18 = (bf16[512,512]{1,0:T(8,128)(2,1)S(1)}, bf16[512,512]{1,0:T(8,128)(2,1)S(1)}, u32[]{:S(2)}, u32[]{:S(2)}) collective-permute-start(bf16[512,512]{1,0:T(8,128)(2,1)S(1)} %collective-permute-done.4.refs_2_), channel_id=1, source_target_pairs={{0,16},{1,17},{2,18},{3,19},{4,20},{5,21},{6,22},{7,23},{8,24},{9,... | collective-permute-start | bytes 1572872 | tf_op jit(solution)/shard_map/ppermute | solution.py:402
  66.5 1.4 %collective-permute-start.19 = (bf16[512,512]{1,0:T(8,128)(2,1)S(1)}, bf16[512,512]{1,0:T(8,128)(2,1)S(1)}, u32[]{:S(2)}, u32[]{:S(2)}) collective-permute-start(bf16[512,512]{1,0:T(8,128)(2,1)S(1)} %collective-permute-done.9.refs_4_), channel_id=1, source_target_pairs={{0,2},{1,3},{2,0},{3,1},{4,6},{5,7},{6,4},{7,5},{8,10},{9,11},{10,... | collective-permute-start | bytes 1572872 | tf_op jit(solution)/shard_map/ppermute | solution.py:402
  67.9 1.5 %collective-permute-done.14.y3_other = bf16[512,512]{1,0:T(8,128)(2,1)S(1)} collective-permute-done((bf16[512,512]{1,0:T(8,128)(2,1)S(1)}, bf16[512,512]{1,0:T(8,128)(2,1)S(1)}, u32[]{:S(2)}, u32[]{:S(2)}) %collective-permute-start.14) | collective-permute-done | bytes 524320 | tf_op jit(solution)/shard_map/ppermute | solution.py:402
  70.2 4.7 %held_keys.1 = (bf16[512,1024]{1,0:T(8,128)(2,1)}, f32[512,512]{1,0:T(8,128)S(1)}) custom-call(s32[18]{0:T(128)S(1)} %copy-done.2, s32[1]{0:T(128)S(6)} %copy.15.count, s32[512]{0:T(512)S(1)} %copy-done.3, bf16[512,8192]{1,0:T(8,128)(2,1)} %tok_ref.5, f32[512,512]{1,0:T(8,128)S(1)} %get-tuple-element.120.mine_h, f32[512,512]{1,0:T(8,128)S(1)} %get-tuple-element.121.mine_c, ...), custom_call_target="tpu_custom_call" | custom-call | flops 1000 | bytes 1024 | tf_op jit(solution)/shard_map/held_keys/pallas_call | solution.py:374
  74.9 1.6 %collective-permute-start.16 = (bf16[512,512]{1,0:T(8,128)(2,1)S(1)}, bf16[512,512]{1,0:T(8,128)(2,1)S(1)}, u32[]{:S(2)}, u32[]{:S(2)}) collective-permute-start(bf16[512,512]{1,0:T(8,128)(2,1)S(1)} %collective-permute-done.10.y3), channel_id=1, source_target_pairs={{0,16},{1,17},{2,18},{3,19},{4,20},{5,21},{6,22},{7,23},{8,24},{9,... | collective-permute-start | bytes 1572872 | tf_op jit(solution)/shard_map/ppermute | solution.py:402
  76.4 1.4 %collective-permute-start.17 = (bf16[512,512]{1,0:T(8,128)(2,1)S(1)}, bf16[512,512]{1,0:T(8,128)(2,1)S(1)}, u32[]{:S(2)}, u32[]{:S(2)}) collective-permute-start(bf16[512,512]{1,0:T(8,128)(2,1)S(1)} %get-tuple-element.126), channel_id=1, source_target_pairs={{0,2},{1,3},{2,0},{3,1},{4,6},{5,7},{6,4},{7,5},{8,10},{9,11},{10,... | collective-permute-start | bytes 1572872 | tf_op jit(solution)/shard_map/ppermute | solution.py:402
  77.9 1.2 %collective-permute-start.20 = (bf16[1,576,128]{2,1,0:T(8,128)(2,1)S(1)}, bf16[1,576,128]{2,1,0:T(8,128)(2,1)S(1)}, u32[]{:S(2)}, u32[]{:S(2)}) collective-permute-start(bf16[1,576,128]{2,1,0:T(8,128)(2,1)S(1)} %get-tuple-element.137), channel_id=1, source_target_pairs={{0,8},{1,9},{2,10},{3,11},{4,12},{5,13},{6,14},{7,15},{8,0},{9,1},... | collective-permute-start | bytes 442376 | tf_op jit(solution)/shard_map/ppermute | solution.py:402
  79.7 1.5 %collective-permute-start.21 = (bf16[1,576,128]{2,1,0:T(8,128)(2,1)S(1)}, bf16[1,576,128]{2,1,0:T(8,128)(2,1)S(1)}, u32[]{:S(2)}, u32[]{:S(2)}) collective-permute-start(bf16[1,576,128]{2,1,0:T(8,128)(2,1)S(1)} %get-tuple-element.138), channel_id=1, source_target_pairs={{0,4},{1,5},{2,6},{3,7},{4,0},{5,1},{6,2},{7,3},{8,12},{9,13},{10,... | collective-permute-start | bytes 442376 | tf_op jit(solution)/shard_map/ppermute | solution.py:402
  81.3 2.2 %collective-permute-start.22 = (bf16[1,576,128]{2,1,0:T(8,128)(2,1)S(1)}, bf16[1,576,128]{2,1,0:T(8,128)(2,1)S(1)}, u32[]{:S(2)}, u32[]{:S(2)}) collective-permute-start(bf16[1,576,128]{2,1,0:T(8,128)(2,1)S(1)} %get-tuple-element.139), channel_id=1, source_target_pairs={{0,12},{1,13},{2,14},{3,15},{4,8},{5,9},{6,10},{7,11},{8,4},{9,5},... | collective-permute-start | bytes 442376 | tf_op jit(solution)/shard_map/ppermute | solution.py:402
  83.5 3.8 %crossed_products.1 = (f32[512,512]{1,0:T(8,128)S(1)}, f32[512,512]{1,0:T(8,128)S(1)}, bf16[2,512,512]{2,1,0:T(8,128)(2,1)S(1)}, bf16[2,512,512]{2,1,0:T(8,128)(2,1)S(1)}) custom-call(s32[18]{0:T(128)S(1)} %copy-done.2, bf16[512,8192]{1,0:T(8,128)(2,1)} %tok_ref.5, bf16[512,8192]{1,0:T(8,128)(2,1)} %collective-permute-done.2.refs_1_.sib_ref, ...), custom_call_target="tpu_custom_call" | custom-call | flops 1000 | bytes 1024 | tf_op jit(solution)/shard_map/crossed_products/pallas_call | solution.py:374
  87.3 3.5 %collective-permute-done.20.refs_0_ = bf16[1,576,128]{2,1,0:T(8,128)(2,1)S(1)} collective-permute-done((bf16[1,576,128]{2,1,0:T(8,128)(2,1)S(1)}, bf16[1,576,128]{2,1,0:T(8,128)(2,1)S(1)}, u32[]{:S(2)}, u32[]{:S(2)}) %collective-permute-start.20) | collective-permute-done | bytes 147488 | tf_op jit(solution)/shard_map/ppermute | solution.py:402
  94.9 1.7 %crossed_keys.1 = (bf16[512,1024]{1,0:T(8,128)(2,1)}, f32[1024,128]{1,0:T(8,128)}, f32[128,128]{1,0:T(8,128)}) custom-call(s32[18]{0:T(128)S(1)} %copy-done.2, s32[1]{0:T(128)S(6)} %copy.15.count, s32[512]{0:T(512)S(1)} %copy-done.3, f32[512,512]{1,0:T(8,128)S(1)} %last_product.2.total_ref, ...), custom_call_target="tpu_custom_call", output_to_operand_aliasing={{0}: (8, {})} | custom-call | flops 1000 | bytes 1024 | tf_op jit(solution)/shard_map/crossed_keys/pallas_call | solution.py:374
  (40 shorter events, 9.0 us)
Async XLA Ops:
  1.7 17.2 %collective-permute-start.2 = (bf16[512,8192]{1,0:T(8,128)(2,1)}, bf16[512,8192]{1,0:T(8,128)(2,1)}, u32[]{:S(2)}, u32[]{:S(2)}) collective-permute-start(bf16[512,8192]{1,0:T(8,128)(2,1)} %tok_ref.5), channel_id=1, source_target_pairs={{0,1},{1,0},{2,3},{3,2},{4,5},{5,4},{6,7},{7,6},{8,9},{9,8},{10,11... | collective-permute-start | bytes 25165832 | tf_op jit(solution)/shard_map/ppermute | solution.py:402
  2.2 16.2 %collective-permute-start = (bf16[512,512]{1,0:T(8,128)(2,1)S(1)}, bf16[512,512]{1,0:T(8,128)(2,1)S(1)}, u32[]{:S(2)}, u32[]{:S(2)}) collective-permute-start(bf16[512,512]{1,0:T(8,128)(2,1)S(1)} %constant_dynamic-slice_fusion), channel_id=1, source_target_pairs={{0,4},{1,5},{2,6},{3,7},{4,12},{5,13},{6,14},{7,15},{8,0},{9,1},{1... | collective-permute-start | bytes 1572872 | tf_op jit(solution)/shard_map/ppermute | solution.py:402
  4.9 14.0 %collective-permute-start.1 = (bf16[512,512]{1,0:T(8,128)(2,1)S(1)}, bf16[512,512]{1,0:T(8,128)(2,1)S(1)}, u32[]{:S(2)}, u32[]{:S(2)}) collective-permute-start(bf16[512,512]{1,0:T(8,128)(2,1)S(1)} %constant_dynamic-slice_fusion), channel_id=1, source_target_pairs={{0,2},{1,3},{2,0},{3,1},{4,6},{5,7},{6,4},{7,5},{8,10},{9,11},{10,... | collective-permute-start | bytes 1572872 | tf_op jit(solution)/shard_map/ppermute | solution.py:402
  8.3 16.2 %copy-start.1 = (bf16[1024,128]{1,0:T(8,128)(2,1)S(1)}, bf16[1024,128]{1,0:T(8,128)(2,1)}, u32[]{:S(2)}) copy-start(bf16[1024,128]{1,0:T(8,128)(2,1)} %refs_7_.1) | copy-start | bytes 786436
  8.3 16.2 %copy-start.2 = (s32[18]{0:T(128)S(1)}, s32[18]{0:T(128)}, u32[]{:S(2)}) copy-start(s32[18]{0:T(128)} %dynamic-slice_bitcast_fusion.sc) | copy-start | bytes 220
  18.9 17.9 %collective-permute-start.6 = (bf16[8,576,128]{2,1,0:T(8,128)(2,1)S(1)}, bf16[8,576,128]{2,1,0:T(8,128)(2,1)S(1)}, u32[]{:S(2)}, u32[]{:S(2)}) collective-permute-start(bf16[8,576,128]{2,1,0:T(8,128)(2,1)S(1)} %get-tuple-element.84), channel_id=1, source_target_pairs={{0,1},{1,0},{2,3},{3,2},{4,5},{5,4},{6,7},{7,6},{8,9},{9,8},{10,11... | collective-permute-start | bytes 3538952 | tf_op jit(solution)/shard_map/ppermute | solution.py:402
  18.9 15.2 %collective-permute-start.3 = (bf16[512,512]{1,0:T(8,128)(2,1)S(1)}, bf16[512,512]{1,0:T(8,128)(2,1)S(1)}, u32[]{:S(2)}, u32[]{:S(2)}) collective-permute-start(bf16[512,512]{1,0:T(8,128)(2,1)S(1)} %collective-permute-done.refs_4_), channel_id=1, source_target_pairs={{0,4},{1,5},{2,6},{3,7},{4,12},{5,13},{6,14},{7,15},{8,0},{9,1},{1... | collective-permute-start | bytes 1572872 | tf_op jit(solution)/shard_map/ppermute | solution.py:402
  21.5 14.1 %collective-permute-start.4 = (bf16[512,512]{1,0:T(8,128)(2,1)S(1)}, bf16[512,512]{1,0:T(8,128)(2,1)S(1)}, u32[]{:S(2)}, u32[]{:S(2)}) collective-permute-start(bf16[512,512]{1,0:T(8,128)(2,1)S(1)} %collective-permute-done.refs_4_), channel_id=1, source_target_pairs={{0,2},{1,3},{2,0},{3,1},{4,6},{5,7},{6,4},{7,5},{8,10},{9,11},{10,... | collective-permute-start | bytes 1572872 | tf_op jit(solution)/shard_map/ppermute | solution.py:402
  23.0 13.8 %collective-permute-start.5 = (bf16[512,512]{1,0:T(8,128)(2,1)S(1)}, bf16[512,512]{1,0:T(8,128)(2,1)S(1)}, u32[]{:S(2)}, u32[]{:S(2)}) collective-permute-start(bf16[512,512]{1,0:T(8,128)(2,1)S(1)} %collective-permute-done.refs_4_), channel_id=1, source_target_pairs={{0,16},{1,17},{2,18},{3,19},{4,20},{5,21},{6,22},{7,23},{8,24},{9,... | collective-permute-start | bytes 1572872 | tf_op jit(solution)/shard_map/ppermute | solution.py:402
  36.8 13.8 %collective-permute-start.7 = (bf16[512,512]{1,0:T(8,128)(2,1)S(1)}, bf16[512,512]{1,0:T(8,128)(2,1)S(1)}, u32[]{:S(2)}, u32[]{:S(2)}) collective-permute-start(bf16[512,512]{1,0:T(8,128)(2,1)S(1)} %collective-permute-done.3.refs_3_), channel_id=1, source_target_pairs={{0,4},{1,5},{2,6},{3,7},{4,12},{5,13},{6,14},{7,15},{8,0},{9,1},{1... | collective-permute-start | bytes 1572872 | tf_op jit(solution)/shard_map/ppermute | solution.py:402
  38.0 12.6 %collective-permute-start.8 = (bf16[512,512]{1,0:T(8,128)(2,1)S(1)}, bf16[512,512]{1,0:T(8,128)(2,1)S(1)}, u32[]{:S(2)}, u32[]{:S(2)}) collective-permute-start(bf16[512,512]{1,0:T(8,128)(2,1)S(1)} %collective-permute-done.3.refs_3_), channel_id=1, source_target_pairs={{0,2},{1,3},{2,0},{3,1},{4,6},{5,7},{6,4},{7,5},{8,10},{9,11},{10,... | collective-permute-start | bytes 1572872 | tf_op jit(solution)/shard_map/ppermute | solution.py:402
  38.5 12.4 %collective-permute-start.9 = (bf16[512,512]{1,0:T(8,128)(2,1)S(1)}, bf16[512,512]{1,0:T(8,128)(2,1)S(1)}, u32[]{:S(2)}, u32[]{:S(2)}) collective-permute-start(bf16[512,512]{1,0:T(8,128)(2,1)S(1)} %collective-permute-done.3.refs_3_), channel_id=1, source_target_pairs={{0,16},{1,17},{2,18},{3,19},{4,20},{5,21},{6,22},{7,23},{8,24},{9,... | collective-permute-start | bytes 1572872 | tf_op jit(solution)/shard_map/ppermute | solution.py:402
  50.9 19.3 %copy-start = (f32[320,128]{1,0:T(8,128)S(1)}, f32[320,128]{1,0:T(8,128)}, u32[]{:S(2)}) copy-start(f32[320,128]{1,0:T(8,128)} %constant.28.clone.tab_ref) | copy-start | bytes 491524
  50.9 19.3 %copy-start.3 = (s32[512]{0:T(512)S(1)}, s32[512]{0:T(512)}, u32[]{:S(2)}) copy-start(s32[512]{0:T(512)} %pos.5) | copy-start | bytes 6148
  50.9 13.6 %collective-permute-start.12 = (bf16[4,576,128]{2,1,0:T(8,128)(2,1)S(1)}, bf16[4,576,128]{2,1,0:T(8,128)(2,1)S(1)}, u32[]{:S(2)}, u32[]{:S(2)}) collective-permute-start(bf16[4,576,128]{2,1,0:T(8,128)(2,1)S(1)} %get-tuple-element.109), channel_id=1, source_target_pairs={{0,2},{1,3},{2,0},{3,1},{4,6},{5,7},{6,4},{7,5},{8,10},{9,11},{10,... | collective-permute-start | bytes 1769480 | tf_op jit(solution)/shard_map/ppermute | solution.py:402
  52.3 12.0 %collective-permute-start.10 = (bf16[512,512]{1,0:T(8,128)(2,1)S(1)}, bf16[512,512]{1,0:T(8,128)(2,1)S(1)}, u32[]{:S(2)}, u32[]{:S(2)}) collective-permute-start(bf16[512,512]{1,0:T(8,128)(2,1)S(1)} %collective-permute-done.8.refs_2_), channel_id=1, source_target_pairs={{0,4},{1,5},{2,6},{3,7},{4,12},{5,13},{6,14},{7,15},{8,0},{9,1},{1... | collective-permute-start | bytes 1572872 | tf_op jit(solution)/shard_map/ppermute | solution.py:402
  52.9 11.6 %collective-permute-start.11 = (bf16[512,512]{1,0:T(8,128)(2,1)S(1)}, bf16[512,512]{1,0:T(8,128)(2,1)S(1)}, u32[]{:S(2)}, u32[]{:S(2)}) collective-permute-start(bf16[512,512]{1,0:T(8,128)(2,1)S(1)} %collective-permute-done.7.refs_3_), channel_id=1, source_target_pairs={{0,16},{1,17},{2,18},{3,19},{4,20},{5,21},{6,22},{7,23},{8,24},{9,... | collective-permute-start | bytes 1572872 | tf_op jit(solution)/shard_map/ppermute | solution.py:402
  64.5 5.7 %collective-permute-start.13 = (f32[512,1024]{1,0:T(8,128)S(1)}, f32[512,1024]{1,0:T(8,128)S(1)}, u32[]{:S(2)}, u32[]{:S(2)}) collective-permute-start(f32[512,1024]{1,0:T(8,128)S(1)} %get-tuple-element.123), channel_id=1, source_target_pairs={{0,1},{1,0},{2,3},{3,2},{4,5},{5,4},{6,7},{7,6},{8,9},{9,8},{10,11... | collective-permute-start | bytes 6291464 | tf_op jit(solution)/shard_map/ppermute | solution.py:402
  64.5 4.9 %collective-permute-start.14 = (bf16[512,512]{1,0:T(8,128)(2,1)S(1)}, bf16[512,512]{1,0:T(8,128)(2,1)S(1)}, u32[]{:S(2)}, u32[]{:S(2)}) collective-permute-start(bf16[512,512]{1,0:T(8,128)(2,1)S(1)} %collective-permute-done.10.y3), channel_id=1, source_target_pairs={{0,1},{1,0},{2,3},{3,2},{4,5},{5,4},{6,7},{7,6},{8,9},{9,8},{10,11... | collective-permute-start | bytes 1572872 | tf_op jit(solution)/shard_map/ppermute | solution.py:402
  65.0 5.1 %collective-permute-start.15 = (bf16[512,512]{1,0:T(8,128)(2,1)S(1)}, bf16[512,512]{1,0:T(8,128)(2,1)S(1)}, u32[]{:S(2)}, u32[]{:S(2)}) collective-permute-start(bf16[512,512]{1,0:T(8,128)(2,1)S(1)} %collective-permute-done.11.a3), channel_id=1, source_target_pairs={{0,1},{1,0},{2,3},{3,2},{4,5},{5,4},{6,7},{7,6},{8,9},{9,8},{10,11... | collective-permute-start | bytes 1572872 | tf_op jit(solution)/shard_map/ppermute | solution.py:402
  65.0 14.7 %collective-permute-start.18 = (bf16[512,512]{1,0:T(8,128)(2,1)S(1)}, bf16[512,512]{1,0:T(8,128)(2,1)S(1)}, u32[]{:S(2)}, u32[]{:S(2)}) collective-permute-start(bf16[512,512]{1,0:T(8,128)(2,1)S(1)} %collective-permute-done.4.refs_2_), channel_id=1, source_target_pairs={{0,16},{1,17},{2,18},{3,19},{4,20},{5,21},{6,22},{7,23},{8,24},{9,... | collective-permute-start | bytes 1572872 | tf_op jit(solution)/shard_map/ppermute | solution.py:402
  66.5 14.8 %collective-permute-start.19 = (bf16[512,512]{1,0:T(8,128)(2,1)S(1)}, bf16[512,512]{1,0:T(8,128)(2,1)S(1)}, u32[]{:S(2)}, u32[]{:S(2)}) collective-permute-start(bf16[512,512]{1,0:T(8,128)(2,1)S(1)} %collective-permute-done.9.refs_4_), channel_id=1, source_target_pairs={{0,2},{1,3},{2,0},{3,1},{4,6},{5,7},{6,4},{7,5},{8,10},{9,11},{10,... | collective-permute-start | bytes 1572872 | tf_op jit(solution)/shard_map/ppermute | solution.py:402
  74.9 16.1 %collective-permute-start.16 = (bf16[512,512]{1,0:T(8,128)(2,1)S(1)}, bf16[512,512]{1,0:T(8,128)(2,1)S(1)}, u32[]{:S(2)}, u32[]{:S(2)}) collective-permute-start(bf16[512,512]{1,0:T(8,128)(2,1)S(1)} %collective-permute-done.10.y3), channel_id=1, source_target_pairs={{0,16},{1,17},{2,18},{3,19},{4,20},{5,21},{6,22},{7,23},{8,24},{9,... | collective-permute-start | bytes 1572872 | tf_op jit(solution)/shard_map/ppermute | solution.py:402
  76.4 15.4 %collective-permute-start.17 = (bf16[512,512]{1,0:T(8,128)(2,1)S(1)}, bf16[512,512]{1,0:T(8,128)(2,1)S(1)}, u32[]{:S(2)}, u32[]{:S(2)}) collective-permute-start(bf16[512,512]{1,0:T(8,128)(2,1)S(1)} %get-tuple-element.126), channel_id=1, source_target_pairs={{0,2},{1,3},{2,0},{3,1},{4,6},{5,7},{6,4},{7,5},{8,10},{9,11},{10,... | collective-permute-start | bytes 1572872 | tf_op jit(solution)/shard_map/ppermute | solution.py:402
  77.9 12.8 %collective-permute-start.20 = (bf16[1,576,128]{2,1,0:T(8,128)(2,1)S(1)}, bf16[1,576,128]{2,1,0:T(8,128)(2,1)S(1)}, u32[]{:S(2)}, u32[]{:S(2)}) collective-permute-start(bf16[1,576,128]{2,1,0:T(8,128)(2,1)S(1)} %get-tuple-element.137), channel_id=1, source_target_pairs={{0,8},{1,9},{2,10},{3,11},{4,12},{5,13},{6,14},{7,15},{8,0},{9,1},... | collective-permute-start | bytes 442376 | tf_op jit(solution)/shard_map/ppermute | solution.py:402
  79.7 11.3 %collective-permute-start.21 = (bf16[1,576,128]{2,1,0:T(8,128)(2,1)S(1)}, bf16[1,576,128]{2,1,0:T(8,128)(2,1)S(1)}, u32[]{:S(2)}, u32[]{:S(2)}) collective-permute-start(bf16[1,576,128]{2,1,0:T(8,128)(2,1)S(1)} %get-tuple-element.138), channel_id=1, source_target_pairs={{0,4},{1,5},{2,6},{3,7},{4,0},{5,1},{6,2},{7,3},{8,12},{9,13},{10,... | collective-permute-start | bytes 442376 | tf_op jit(solution)/shard_map/ppermute | solution.py:402
  81.3 9.7 %collective-permute-start.22 = (bf16[1,576,128]{2,1,0:T(8,128)(2,1)S(1)}, bf16[1,576,128]{2,1,0:T(8,128)(2,1)S(1)}, u32[]{:S(2)}, u32[]{:S(2)}) collective-permute-start(bf16[1,576,128]{2,1,0:T(8,128)(2,1)S(1)} %get-tuple-element.139), channel_id=1, source_target_pairs={{0,12},{1,13},{2,14},{3,15},{4,8},{5,9},{6,10},{7,11},{8,4},{9,5},... | collective-permute-start | bytes 442376 | tf_op jit(solution)/shard_map/ppermute | solution.py:402
  92.5 2.4 %collective-permute-start.23 = (bf16[512,512]{1,0:T(8,128)(2,1)S(1)}, bf16[512,512]{1,0:T(8,128)(2,1)S(1)}, u32[]{:S(2)}, u32[]{:S(2)}) collective-permute-start(bf16[512,512]{1,0:T(8,128)(2,1)S(1)} %last_product.3), channel_id=1, source_target_pairs={{0,1},{1,0},{2,3},{3,2},{4,5},{5,4},{6,7},{7,6},{8,9},{9,8},{10,11... | collective-permute-start | bytes 1572872 | tf_op jit(solution)/shard_map/ppermute | solution.py:402
  92.6 2.2 %collective-permute-start.24 = (f32[1,576,128]{2,1,0:T(8,128)S(1)}, f32[1,576,128]{2,1,0:T(8,128)S(1)}, u32[]{:S(2)}, u32[]{:S(2)}) collective-permute-start(f32[1,576,128]{2,1,0:T(8,128)S(1)} %share.1), channel_id=1, source_target_pairs={{0,1},{1,0},{2,3},{3,2},{4,5},{5,4},{6,7},{7,6},{8,9},{9,8},{10,11... | collective-permute-start | bytes 884744 | tf_op jit(solution)/shard_map/ppermute | solution.py:402

commit v5 on v4

--- a/solution.py
+++ b/solution.py
@@ -118,8 +118,8 @@
     weights = (take(len(held_from)), take(len(crossed_from)))
     given = None if first else (take(2), take(2))
     low_ref, second_ref = take(2) if first else (None, None)
-    outs = (take(2), take(1 if joined else 2))
-    spare = take(1) if first else []
+    sides = 2 if crossed_from else 1
+    outs = (take(sides), take(1 if joined else sides))
     tvs, wvs, tots = (take(2) for _ in range(3))
     sems, out_sems = refs
     deep, half = weights[0][-1].shape
@@ -160,13 +160,9 @@
         )
 
     for k in range(2):
-        for side in range(2):
+        for side in range(sides):
             for c in need[k, side]:
                 c.wait()
-            if first and k == 0 and side:
-                c = pltpu.make_async_copy(wvs[1].at[0:deep, :], spare[0], out_sems.at[4])
-                c.start()
-                saved.append(c)
             tots[side][k] = start(k, side) + jnp.dot(
                 tvs[side][k], wvs[side][...], preferred_element_type=jnp.float32
             )
@@ -179,6 +175,33 @@
             saved.append(c)
     for c in saved:
         c.wait()
+
+
+def own_crossed_kernel(
+    core, passed, sc, tok_ref, sib_ref, w_ref, low_ref, second_ref, *refs
+):
+    mine_ref, theirs_ref, own_ref, tv, sems = refs[passed:]
+
+    @pl.when(sc[8] == core)
+    def _():
+        deep, half = own_ref.shape
+        at = pl.multiple_of((1 - sc[9]) * half, half)
+        columns = pl.ds(pl.multiple_of((2 * sc[10] + sc[8]) * deep, deep), deep)
+        loads = [
+            pltpu.make_async_copy(w_ref.at[:, pl.ds(at, half)], own_ref, sems.at[0]),
+            pltpu.make_async_copy(tok_ref.at[:, columns], tv.at[0], sems.at[1]),
+            pltpu.make_async_copy(sib_ref.at[:, columns], tv.at[1], sems.at[2]),
+        ]
+        for c in loads:
+            c.start()
+        for c in loads:
+            c.wait()
+        adapters = ADAPTER_SCALE * lax.dot_general(
+            low_ref[...], second_ref[pl.ds(at, half), :], (((1,), (1,)), ((), ())),
+            preferred_element_type=jnp.float32,
+        )
+        mine_ref[...] = adapters + jnp.dot(tv[0], own_ref[...], preferred_element_type=jnp.float32)
+        theirs_ref[...] = jnp.dot(tv[1], own_ref[...], preferred_element_type=jnp.float32)
 
 
 def rope_blocks(pos, count, tab_ref, tokens, write):
@@ -420,10 +443,9 @@
         )
 
     def product(held, crossed, given=(), adapters=(), joined=False):
-        kh, kc = len(held) * deep, len(crossed) * deep
-        outs = [pltpu.VMEM((rows, half), f32)] * 2
+        kh, kc = len(held) * deep, max(len(crossed), 1) * deep
+        outs = [pltpu.VMEM((rows, half), f32)] * (2 if crossed else 1)
         outs += [pltpu.VMEM((rows, kv), f32)] if joined else outs
-        outs += [] if given else [shape((deep, half), bf16)]
         return call(
             functools.partial(
                 product_kernel, [i for _, i in held], [i for _, i in crossed], not given, joined
@@ -466,13 +488,26 @@
     )
     z1, y0, low, own, sib, sib_tokens = fence(z1, y0, low, own, sib, sib_tokens)
 
+    def own_crossed(core, *given):
+        return call(
+            functools.partial(own_crossed_kernel, core, len(given)), "own_crossed",
+            [pltpu.VMEM((rows, half), f32)] * 2 + [pltpu.VMEM((deep, half), bf16)],
+            [HBM] * 3 + [vm] * (2 + len(given)), [vm] * 3, [pltpu.VMEM((2, rows, deep), bf16), dma((3,))],
+            (sc, tokens, sib_tokens, frozen_weight, low, second_adapter_weight, *given),
+            aliases={6 + i: i for i in range(len(given))},
+        )
+
+    other = send(sib, to_core)
+    started = own_crossed(0)
+    z1, *started = fence(z1, *started)
     z2 = send(z1, to_z)
     y1 = send(z1, to_y)
     a1 = send(z1, to_x)
-    other = send(sib, to_core)
-    *totals, c0 = product(
-        ((frozen_weight, 10), (y0, 14), (z1, 11)), ((frozen_weight, 10),), adapters=(low, second_adapter_weight)
-    )
+    crossed_sum, crossed_sib, c0 = own_crossed(1, *started)
+    held_sum, held_sib = product(
+        ((frozen_weight, 10), (y0, 14), (z1, 11)), (), adapters=(low, second_adapter_weight)
+    )
+    totals = held_sum, crossed_sum, held_sib, crossed_sib
     z2, y1, a1, other, *totals = fence(z2, y1, a1, other, *totals)
 
     z3 = send(z2, to_z)

time: 97.1 us -> 94.2 us (0.970)
  waiting for transfers between devices: 26.9 us -> 22.7 us
  Pallas kernels: 37.1 us -> 39.1 us
    ppermute x25, waiting for transfers between devices: 26.9 us -> 22.7 us  [fast_body(): send = lambda x, f: lax.ppermute(x, ALL, routes.pairs(f))]
    pallas_call x12 -> x14, Pallas kernels: 37.1 us -> 39.1 us  [call(): pl.pallas_call(kernel, out_shape=shapes, grid_spec=pltpu.PrefetchScalarGr...]
  transfers between devices with their start and end apart: 25 -> 25, of which waited for: 16 -> 17; matrix products, arithmetic and copies ran while one was open for 1% -> 1% of each run, Pallas kernels for 36% -> 39%
where the time goes in v5:
time: 94.2 us; the launch traced here: 93.9 us
  Pallas kernels  39.1 us (42%)
  starting transfers between devices  28.1 us (30%)
  waiting for transfers between devices  22.7 us (24%)
  local copies, waits for them, and re-layouts  2.3 us (2%)
  between operations  1.59 us (2%)
    pallas_call x14, Pallas kernels, call(): pl.pallas_call(kernel, out_shape=shapes, grid_spec=pltpu.PrefetchScalarGr...  39.1 us
    ppermute x25, starting transfers between devices, fast_body(): send = lambda x, f: lax.ppermute(x, ALL, routes.pairs(f))  28.1 us
    ppermute x25, waiting for transfers between devices, fast_body(): send = lambda x, f: lax.ppermute(x, ALL, routes.pairs(f))  22.7 us
  transfers between devices with their start and end apart: 25, of which 17 were waited for; matrix products, arithmetic and copies ran while one was open for 1% of the time, Pallas kernels for 39%

profile of v5, /device:TPU:0, one launch (start us, length us, event | category | flops | bytes accessed | tf_op | source)
XLA Modules:
  0.0 93.9 jit_solution(11324325904127559865)
XLA Ops:
  0.6 1.1 %constant_dynamic-slice_fusion = bf16[512,512]{1,0:T(8,128)(2,1)S(1)} fusion(bf16[512,1024]{1,0:T(8,128)(2,1)} %w_ref.3, s32[]{:T(128)S(6)} %select_n.6), kind=kLoop, calls=%fused_computation.1 | loop fusion | bytes 1048580 | tf_op jit(solution)/shard_map/dynamic_slice | solution.py:465
  2.2 2.6 %collective-permute-start = (bf16[512,512]{1,0:T(8,128)(2,1)S(1)}, bf16[512,512]{1,0:T(8,128)(2,1)S(1)}, u32[]{:S(2)}, u32[]{:S(2)}) collective-permute-start(bf16[512,512]{1,0:T(8,128)(2,1)S(1)} %constant_dynamic-slice_fusion), channel_id=1, source_target_pairs={{0,4},{1,5},{2,6},{3,7},{4,12},{5,13},{6,14},{7,15},{8,0},{9,1},{1... | collective-permute-start | bytes 1572872 | tf_op jit(solution)/shard_map/ppermute | solution.py:425
  4.9 1.5 %collective-permute-start.1 = (bf16[512,512]{1,0:T(8,128)(2,1)S(1)}, bf16[512,512]{1,0:T(8,128)(2,1)S(1)}, u32[]{:S(2)}, u32[]{:S(2)}) collective-permute-start(bf16[512,512]{1,0:T(8,128)(2,1)S(1)} %constant_dynamic-slice_fusion), channel_id=1, source_target_pairs={{0,2},{1,3},{2,0},{3,1},{4,6},{5,7},{6,4},{7,5},{8,10},{9,11},{10,... | collective-permute-start | bytes 1572872 | tf_op jit(solution)/shard_map/ppermute | solution.py:425
  7.1 1.2 %dynamic-slice_bitcast_fusion.sc = s32[18]{0:T(128)} fusion(s32[32,18]{1,0:T(8,128)} %constant.29.clone, s32[]{:T(128)S(6)} %select_n.7), kind=kLoop, calls=%fused_computation | loop fusion | bytes 148 | tf_op jit(solution)/shard_map/squeeze | solution.py:467
  8.3 9.9 %adapter_gradients.1 = (bf16[512,128]{1,0:T(8,128)(2,1)S(1)}, f32[8,576,128]{2,1,0:T(8,128)S(1)}, bf16[8,576,128]{2,1,0:T(8,128)(2,1)S(1)}) custom-call(s32[18]{0:T(128)} %dynamic-slice_bitcast_fusion.sc, s32[4]{0:T(128)} %tids.1, s32[1]{0:T(128)S(6)} %copy.21.count, s32[512]{0:T(512)} %pos.5, bf16[512,8192]{1,0:T(8,128)(2,1)} %tok_ref.9, ...), custom_call_target="tpu_custom_call" | custom-call | flops 1000 | bytes 1024 | tf_op jit(solution)/shard_map/adapter_gradients/pallas_call | solution.py:397
  18.9 2.8 %own_crossed.2 = (f32[512,512]{1,0:T(8,128)S(1)}, f32[512,512]{1,0:T(8,128)S(1)}, bf16[512,512]{1,0:T(8,128)(2,1)S(1)}) custom-call(s32[18]{0:T(128)S(1)} %copy-done.2, bf16[512,8192]{1,0:T(8,128)(2,1)} %tok_ref.9, bf16[512,8192]{1,0:T(8,128)(2,1)} %collective-permute-done.2.sib_ref.refs_1_, bf16[512,1024]{1,0:T(8,128)(2,1)} %w_ref.3, ...), custom_call_target="tpu_custom_call" | custom-call | flops 1000 | bytes 1024 | tf_op jit(solution)/shard_map/own_crossed/pallas_call | solution.py:397
  21.7 2.6 %collective-permute-start.3 = (bf16[512,512]{1,0:T(8,128)(2,1)S(1)}, bf16[512,512]{1,0:T(8,128)(2,1)S(1)}, u32[]{:S(2)}, u32[]{:S(2)}) collective-permute-start(bf16[512,512]{1,0:T(8,128)(2,1)S(1)} %collective-permute-done.refs_4_), channel_id=1, source_target_pairs={{0,4},{1,5},{2,6},{3,7},{4,12},{5,13},{6,14},{7,15},{8,0},{9,1},{1... | collective-permute-start | bytes 1572872 | tf_op jit(solution)/shard_map/ppermute | solution.py:425
  24.3 1.5 %collective-permute-start.4 = (bf16[512,512]{1,0:T(8,128)(2,1)S(1)}, bf16[512,512]{1,0:T(8,128)(2,1)S(1)}, u32[]{:S(2)}, u32[]{:S(2)}) collective-permute-start(bf16[512,512]{1,0:T(8,128)(2,1)S(1)} %collective-permute-done.refs_4_), channel_id=1, source_target_pairs={{0,2},{1,3},{2,0},{3,1},{4,6},{5,7},{6,4},{7,5},{8,10},{9,11},{10,... | collective-permute-start | bytes 1572872 | tf_op jit(solution)/shard_map/ppermute | solution.py:425
  25.9 1.5 %collective-permute-start.5 = (bf16[512,512]{1,0:T(8,128)(2,1)S(1)}, bf16[512,512]{1,0:T(8,128)(2,1)S(1)}, u32[]{:S(2)}, u32[]{:S(2)}) collective-permute-start(bf16[512,512]{1,0:T(8,128)(2,1)S(1)} %collective-permute-done.refs_4_), channel_id=1, source_target_pairs={{0,16},{1,17},{2,18},{3,19},{4,20},{5,21},{6,22},{7,23},{8,24},{9,... | collective-permute-start | bytes 1572872 | tf_op jit(solution)/shard_map/ppermute | solution.py:425
  27.3 4.5 %products.3 = (f32[512,512]{1,0:T(8,128)S(1)}, f32[512,512]{1,0:T(8,128)S(1)}) custom-call(s32[18]{0:T(128)S(1)} %copy-done.2, bf16[512,8192]{1,0:T(8,128)(2,1)} %tok_ref.9, bf16[512,8192]{1,0:T(8,128)(2,1)} %collective-permute-done.2.sib_ref.refs_1_, bf16[512,1024]{1,0:T(8,128)(2,1)} %w_ref.3, bf16[512,512]{1,0:T(8,128)(2,1)S(1)} %collective-permute-done.1.refs_3_, ...), custom_call_target="tpu_custom_call" | custom-call | flops 1000 | bytes 1024 | tf_op jit(solution)/shard_map/products/pallas_call | solution.py:397
  32.4 2.3 %collective-permute-done.3.refs_3_ = bf16[512,512]{1,0:T(8,128)(2,1)S(1)} collective-permute-done((bf16[512,512]{1,0:T(8,128)(2,1)S(1)}, bf16[512,512]{1,0:T(8,128)(2,1)S(1)}, u32[]{:S(2)}, u32[]{:S(2)}) %collective-permute-start.3) | collective-permute-done | bytes 524320 | tf_op jit(solution)/shard_map/ppermute | solution.py:425
  34.8 1.4 %collective-permute-done.4.refs_2_ = bf16[512,512]{1,0:T(8,128)(2,1)S(1)} collective-permute-done((bf16[512,512]{1,0:T(8,128)(2,1)S(1)}, bf16[512,512]{1,0:T(8,128)(2,1)S(1)}, u32[]{:S(2)}, u32[]{:S(2)}) %collective-permute-start.4) | collective-permute-done | bytes 524320 | tf_op jit(solution)/shard_map/ppermute | solution.py:425
  36.2 1.2 %collective-permute-done.5.refs_4_ = bf16[512,512]{1,0:T(8,128)(2,1)S(1)} collective-permute-done((bf16[512,512]{1,0:T(8,128)(2,1)S(1)}, bf16[512,512]{1,0:T(8,128)(2,1)S(1)}, u32[]{:S(2)}, u32[]{:S(2)}) %collective-permute-start.5) | collective-permute-done | bytes 524320 | tf_op jit(solution)/shard_map/ppermute | solution.py:425
  37.4 1.2 %collective-permute-start.7 = (bf16[512,512]{1,0:T(8,128)(2,1)S(1)}, bf16[512,512]{1,0:T(8,128)(2,1)S(1)}, u32[]{:S(2)}, u32[]{:S(2)}) collective-permute-start(bf16[512,512]{1,0:T(8,128)(2,1)S(1)} %collective-permute-done.3.refs_3_), channel_id=1, source_target_pairs={{0,4},{1,5},{2,6},{3,7},{4,12},{5,13},{6,14},{7,15},{8,0},{9,1},{1... | collective-permute-start | bytes 1572872 | tf_op jit(solution)/shard_map/ppermute | solution.py:425
  39.1 1.5 %collective-permute-start.9 = (bf16[512,512]{1,0:T(8,128)(2,1)S(1)}, bf16[512,512]{1,0:T(8,128)(2,1)S(1)}, u32[]{:S(2)}, u32[]{:S(2)}) collective-permute-start(bf16[512,512]{1,0:T(8,128)(2,1)S(1)} %collective-permute-done.3.refs_3_), channel_id=1, source_target_pairs={{0,16},{1,17},{2,18},{3,19},{4,20},{5,21},{6,22},{7,23},{8,24},{9,... | collective-permute-start | bytes 1572872 | tf_op jit(solution)/shard_map/ppermute | solution.py:425
  40.8 4.6 %products.4 = (f32[512,512]{1,0:T(8,128)S(1)}, f32[512,512]{1,0:T(8,128)S(1)}, f32[512,512]{1,0:T(8,128)S(1)}, f32[512,512]{1,0:T(8,128)S(1)}) custom-call(s32[18]{0:T(128)S(1)} %copy-done.2, bf16[512,8192]{1,0:T(8,128)(2,1)} %tok_ref.9, bf16[512,8192]{1,0:T(8,128)(2,1)} %collective-permute-done.2.sib_ref.refs_1_, ...), custom_call_target="tpu_custom_call" | custom-call | flops 1000 | bytes 1024 | tf_op jit(solution)/shard_map/products/pallas_call | solution.py:397
  45.4 3.6 %collective-permute-done.7.refs_3_ = bf16[512,512]{1,0:T(8,128)(2,1)S(1)} collective-permute-done((bf16[512,512]{1,0:T(8,128)(2,1)S(1)}, bf16[512,512]{1,0:T(8,128)(2,1)S(1)}, u32[]{:S(2)}, u32[]{:S(2)}) %collective-permute-start.7) | collective-permute-done | bytes 524320 | tf_op jit(solution)/shard_map/ppermute | solution.py:425
  48.9 1.4 %collective-permute-done.8.refs_2_ = bf16[512,512]{1,0:T(8,128)(2,1)S(1)} collective-permute-done((bf16[512,512]{1,0:T(8,128)(2,1)S(1)}, bf16[512,512]{1,0:T(8,128)(2,1)S(1)}, u32[]{:S(2)}, u32[]{:S(2)}) %collective-permute-start.8) | collective-permute-done | bytes 524320 | tf_op jit(solution)/shard_map/ppermute | solution.py:425
  50.7 1.5 %collective-permute-start.10 = (bf16[512,512]{1,0:T(8,128)(2,1)S(1)}, bf16[512,512]{1,0:T(8,128)(2,1)S(1)}, u32[]{:S(2)}, u32[]{:S(2)}) collective-permute-start(bf16[512,512]{1,0:T(8,128)(2,1)S(1)} %collective-permute-done.8.refs_2_), channel_id=1, source_target_pairs={{0,4},{1,5},{2,6},{3,7},{4,12},{5,13},{6,14},{7,15},{8,0},{9,1},{1... | collective-permute-start | bytes 1572872 | tf_op jit(solution)/shard_map/ppermute | solution.py:425
  52.2 1.5 %collective-permute-start.11 = (bf16[512,512]{1,0:T(8,128)(2,1)S(1)}, bf16[512,512]{1,0:T(8,128)(2,1)S(1)}, u32[]{:S(2)}, u32[]{:S(2)}) collective-permute-start(bf16[512,512]{1,0:T(8,128)(2,1)S(1)} %collective-permute-done.7.refs_3_), channel_id=1, source_target_pairs={{0,16},{1,17},{2,18},{3,19},{4,20},{5,21},{6,22},{7,23},{8,24},{9,... | collective-permute-start | bytes 1572872 | tf_op jit(solution)/shard_map/ppermute | solution.py:425
  53.7 4.7 %products.5 = (f32[512,512]{1,0:T(8,128)S(1)}, f32[512,512]{1,0:T(8,128)S(1)}, f32[512,1024]{1,0:T(8,128)S(1)}) custom-call(s32[18]{0:T(128)S(1)} %copy-done.2, bf16[512,8192]{1,0:T(8,128)(2,1)} %tok_ref.9, bf16[512,8192]{1,0:T(8,128)(2,1)} %collective-permute-done.2.sib_ref.refs_1_, bf16[512,512]{1,0:T(8,128)(2,1)S(1)} %collective-permute-done.8.refs_2_, ...), custom_call_target="tpu_custom_call" | custom-call | flops 1000 | bytes 1024 | tf_op jit(solution)/shard_map/products/pallas_call | solution.py:397
  58.4 2.4 %collective-permute-done.10.y3 = bf16[512,512]{1,0:T(8,128)(2,1)S(1)} collective-permute-done((bf16[512,512]{1,0:T(8,128)(2,1)S(1)}, bf16[512,512]{1,0:T(8,128)(2,1)S(1)}, u32[]{:S(2)}, u32[]{:S(2)}) %collective-permute-start.10) | collective-permute-done | bytes 524320 | tf_op jit(solution)/shard_map/ppermute | solution.py:425
  62.1 1.5 %collective-permute-start.18 = (bf16[512,512]{1,0:T(8,128)(2,1)S(1)}, bf16[512,512]{1,0:T(8,128)(2,1)S(1)}, u32[]{:S(2)}, u32[]{:S(2)}) collective-permute-start(bf16[512,512]{1,0:T(8,128)(2,1)S(1)} %collective-permute-done.4.refs_2_), channel_id=1, source_target_pairs={{0,16},{1,17},{2,18},{3,19},{4,20},{5,21},{6,22},{7,23},{8,24},{9,... | collective-permute-start | bytes 1572872 | tf_op jit(solution)/shard_map/ppermute | solution.py:425
  64.6 1.9 %collective-permute-done.14.y3_other = bf16[512,512]{1,0:T(8,128)(2,1)S(1)} collective-permute-done((bf16[512,512]{1,0:T(8,128)(2,1)S(1)}, bf16[512,512]{1,0:T(8,128)(2,1)S(1)}, u32[]{:S(2)}, u32[]{:S(2)}) %collective-permute-start.14) | collective-permute-done | bytes 524320 | tf_op jit(solution)/shard_map/ppermute | solution.py:425
  67.2 4.8 %held_keys.1 = (bf16[512,1024]{1,0:T(8,128)(2,1)}, f32[512,512]{1,0:T(8,128)S(1)}) custom-call(s32[18]{0:T(128)S(1)} %copy-done.2, s32[1]{0:T(128)S(6)} %copy.21.count, s32[512]{0:T(512)S(1)} %copy-done.3, bf16[512,8192]{1,0:T(8,128)(2,1)} %tok_ref.9, f32[512,512]{1,0:T(8,128)S(1)} %get-tuple-element.134.mine_h, f32[512,512]{1,0:T(8,128)S(1)} %get-tuple-element.135.mine_c, ...), custom_call_target="tpu_custom_call" | custom-call | flops 1000 | bytes 1024 | tf_op jit(solution)/shard_map/held_keys/pallas_call | solution.py:397
  72.0 1.6 %collective-permute-start.16 = (bf16[512,512]{1,0:T(8,128)(2,1)S(1)}, bf16[512,512]{1,0:T(8,128)(2,1)S(1)}, u32[]{:S(2)}, u32[]{:S(2)}) collective-permute-start(bf16[512,512]{1,0:T(8,128)(2,1)S(1)} %collective-permute-done.10.y3), channel_id=1, source_target_pairs={{0,16},{1,17},{2,18},{3,19},{4,20},{5,21},{6,22},{7,23},{8,24},{9,... | collective-permute-start | bytes 1572872 | tf_op jit(solution)/shard_map/ppermute | solution.py:425
  74.6 2.1 %collective-permute-start.20 = (bf16[1,576,128]{2,1,0:T(8,128)(2,1)S(1)}, bf16[1,576,128]{2,1,0:T(8,128)(2,1)S(1)}, u32[]{:S(2)}, u32[]{:S(2)}) collective-permute-start(bf16[1,576,128]{2,1,0:T(8,128)(2,1)S(1)} %get-tuple-element.151), channel_id=1, source_target_pairs={{0,8},{1,9},{2,10},{3,11},{4,12},{5,13},{6,14},{7,15},{8,0},{9,1},... | collective-permute-start | bytes 442376 | tf_op jit(solution)/shard_map/ppermute | solution.py:425
  76.8 1.0 %collective-permute-start.21 = (bf16[1,576,128]{2,1,0:T(8,128)(2,1)S(1)}, bf16[1,576,128]{2,1,0:T(8,128)(2,1)S(1)}, u32[]{:S(2)}, u32[]{:S(2)}) collective-permute-start(bf16[1,576,128]{2,1,0:T(8,128)(2,1)S(1)} %get-tuple-element.152), channel_id=1, source_target_pairs={{0,4},{1,5},{2,6},{3,7},{4,0},{5,1},{6,2},{7,3},{8,12},{9,13},{10,... | collective-permute-start | bytes 442376 | tf_op jit(solution)/shard_map/ppermute | solution.py:425
  78.3 2.0 %collective-permute-start.22 = (bf16[1,576,128]{2,1,0:T(8,128)(2,1)S(1)}, bf16[1,576,128]{2,1,0:T(8,128)(2,1)S(1)}, u32[]{:S(2)}, u32[]{:S(2)}) collective-permute-start(bf16[1,576,128]{2,1,0:T(8,128)(2,1)S(1)} %get-tuple-element.153), channel_id=1, source_target_pairs={{0,12},{1,13},{2,14},{3,15},{4,8},{5,9},{6,10},{7,11},{8,4},{9,5},... | collective-permute-start | bytes 442376 | tf_op jit(solution)/shard_map/ppermute | solution.py:425
  80.3 3.8 %crossed_products.1 = (f32[512,512]{1,0:T(8,128)S(1)}, f32[512,512]{1,0:T(8,128)S(1)}, bf16[2,512,512]{2,1,0:T(8,128)(2,1)S(1)}, bf16[2,512,512]{2,1,0:T(8,128)(2,1)S(1)}) custom-call(s32[18]{0:T(128)S(1)} %copy-done.2, bf16[512,8192]{1,0:T(8,128)(2,1)} %tok_ref.9, bf16[512,8192]{1,0:T(8,128)(2,1)} %collective-permute-done.2.sib_ref.refs_1_, ...), custom_call_target="tpu_custom_call" | custom-call | flops 1000 | bytes 1024 | tf_op jit(solution)/shard_map/crossed_products/pallas_call | solution.py:397
  84.1 3.8 %collective-permute-done.20.refs_0_ = bf16[1,576,128]{2,1,0:T(8,128)(2,1)S(1)} collective-permute-done((bf16[1,576,128]{2,1,0:T(8,128)(2,1)S(1)}, bf16[1,576,128]{2,1,0:T(8,128)(2,1)S(1)}, u32[]{:S(2)}, u32[]{:S(2)}) %collective-permute-start.20) | collective-permute-done | bytes 147488 | tf_op jit(solution)/shard_map/ppermute | solution.py:425
  92.0 1.7 %crossed_keys.1 = (bf16[512,1024]{1,0:T(8,128)(2,1)}, f32[1024,128]{1,0:T(8,128)}, f32[128,128]{1,0:T(8,128)}) custom-call(s32[18]{0:T(128)S(1)} %copy-done.2, s32[1]{0:T(128)S(6)} %copy.21.count, s32[512]{0:T(512)S(1)} %copy-done.3, f32[512,512]{1,0:T(8,128)S(1)} %last_product.2.total_ref, ...), custom_call_target="tpu_custom_call", output_to_operand_aliasing={{0}: (8, {})} | custom-call | flops 1000 | bytes 1024 | tf_op jit(solution)/shard_map/crossed_keys/pallas_call | solution.py:397
  (42 shorter events, 11.6 us)
Async XLA Ops:
  1.7 17.2 %collective-permute-start.2 = (bf16[512,8192]{1,0:T(8,128)(2,1)}, bf16[512,8192]{1,0:T(8,128)(2,1)}, u32[]{:S(2)}, u32[]{:S(2)}) collective-permute-start(bf16[512,8192]{1,0:T(8,128)(2,1)} %tok_ref.9), channel_id=1, source_target_pairs={{0,1},{1,0},{2,3},{3,2},{4,5},{5,4},{6,7},{7,6},{8,9},{9,8},{10,11... | collective-permute-start | bytes 25165832 | tf_op jit(solution)/shard_map/ppermute | solution.py:425
  2.2 16.2 %collective-permute-start = (bf16[512,512]{1,0:T(8,128)(2,1)S(1)}, bf16[512,512]{1,0:T(8,128)(2,1)S(1)}, u32[]{:S(2)}, u32[]{:S(2)}) collective-permute-start(bf16[512,512]{1,0:T(8,128)(2,1)S(1)} %constant_dynamic-slice_fusion), channel_id=1, source_target_pairs={{0,4},{1,5},{2,6},{3,7},{4,12},{5,13},{6,14},{7,15},{8,0},{9,1},{1... | collective-permute-start | bytes 1572872 | tf_op jit(solution)/shard_map/ppermute | solution.py:425
  4.9 14.0 %collective-permute-start.1 = (bf16[512,512]{1,0:T(8,128)(2,1)S(1)}, bf16[512,512]{1,0:T(8,128)(2,1)S(1)}, u32[]{:S(2)}, u32[]{:S(2)}) collective-permute-start(bf16[512,512]{1,0:T(8,128)(2,1)S(1)} %constant_dynamic-slice_fusion), channel_id=1, source_target_pairs={{0,2},{1,3},{2,0},{3,1},{4,6},{5,7},{6,4},{7,5},{8,10},{9,11},{10,... | collective-permute-start | bytes 1572872 | tf_op jit(solution)/shard_map/ppermute | solution.py:425
  8.3 10.6 %copy-start = (bf16[1024,128]{1,0:T(8,128)(2,1)S(1)}, bf16[1024,128]{1,0:T(8,128)(2,1)}, u32[]{:S(2)}) copy-start(bf16[1024,128]{1,0:T(8,128)(2,1)} %second_ref.3) | copy-start | bytes 786436
  8.3 10.6 %copy-start.2 = (s32[18]{0:T(128)S(1)}, s32[18]{0:T(128)}, u32[]{:S(2)}) copy-start(s32[18]{0:T(128)} %dynamic-slice_bitcast_fusion.sc) | copy-start | bytes 220
  18.9 18.5 %collective-permute-start.6 = (bf16[8,576,128]{2,1,0:T(8,128)(2,1)S(1)}, bf16[8,576,128]{2,1,0:T(8,128)(2,1)S(1)}, u32[]{:S(2)}, u32[]{:S(2)}) collective-permute-start(bf16[8,576,128]{2,1,0:T(8,128)(2,1)S(1)} %get-tuple-element.97), channel_id=1, source_target_pairs={{0,1},{1,0},{2,3},{3,2},{4,5},{5,4},{6,7},{7,6},{8,9},{9,8},{10,11... | collective-permute-start | bytes 3538952 | tf_op jit(solution)/shard_map/ppermute | solution.py:425
  21.7 13.1 %collective-permute-start.3 = (bf16[512,512]{1,0:T(8,128)(2,1)S(1)}, bf16[512,512]{1,0:T(8,128)(2,1)S(1)}, u32[]{:S(2)}, u32[]{:S(2)}) collective-permute-start(bf16[512,512]{1,0:T(8,128)(2,1)S(1)} %collective-permute-done.refs_4_), channel_id=1, source_target_pairs={{0,4},{1,5},{2,6},{3,7},{4,12},{5,13},{6,14},{7,15},{8,0},{9,1},{1... | collective-permute-start | bytes 1572872 | tf_op jit(solution)/shard_map/ppermute | solution.py:425
  24.3 11.8 %collective-permute-start.4 = (bf16[512,512]{1,0:T(8,128)(2,1)S(1)}, bf16[512,512]{1,0:T(8,128)(2,1)S(1)}, u32[]{:S(2)}, u32[]{:S(2)}) collective-permute-start(bf16[512,512]{1,0:T(8,128)(2,1)S(1)} %collective-permute-done.refs_4_), channel_id=1, source_target_pairs={{0,2},{1,3},{2,0},{3,1},{4,6},{5,7},{6,4},{7,5},{8,10},{9,11},{10,... | collective-permute-start | bytes 1572872 | tf_op jit(solution)/shard_map/ppermute | solution.py:425
  25.9 11.5 %collective-permute-start.5 = (bf16[512,512]{1,0:T(8,128)(2,1)S(1)}, bf16[512,512]{1,0:T(8,128)(2,1)S(1)}, u32[]{:S(2)}, u32[]{:S(2)}) collective-permute-start(bf16[512,512]{1,0:T(8,128)(2,1)S(1)} %collective-permute-done.refs_4_), channel_id=1, source_target_pairs={{0,16},{1,17},{2,18},{3,19},{4,20},{5,21},{6,22},{7,23},{8,24},{9,... | collective-permute-start | bytes 1572872 | tf_op jit(solution)/shard_map/ppermute | solution.py:425
  37.4 11.5 %collective-permute-start.7 = (bf16[512,512]{1,0:T(8,128)(2,1)S(1)}, bf16[512,512]{1,0:T(8,128)(2,1)S(1)}, u32[]{:S(2)}, u32[]{:S(2)}) collective-permute-start(bf16[512,512]{1,0:T(8,128)(2,1)S(1)} %collective-permute-done.3.refs_3_), channel_id=1, source_target_pairs={{0,4},{1,5},{2,6},{3,7},{4,12},{5,13},{6,14},{7,15},{8,0},{9,1},{1... | collective-permute-start | bytes 1572872 | tf_op jit(solution)/shard_map/ppermute | solution.py:425
  38.6 11.7 %collective-permute-start.8 = (bf16[512,512]{1,0:T(8,128)(2,1)S(1)}, bf16[512,512]{1,0:T(8,128)(2,1)S(1)}, u32[]{:S(2)}, u32[]{:S(2)}) collective-permute-start(bf16[512,512]{1,0:T(8,128)(2,1)S(1)} %collective-permute-done.3.refs_3_), channel_id=1, source_target_pairs={{0,2},{1,3},{2,0},{3,1},{4,6},{5,7},{6,4},{7,5},{8,10},{9,11},{10,... | collective-permute-start | bytes 1572872 | tf_op jit(solution)/shard_map/ppermute | solution.py:425
  39.1 11.2 %collective-permute-start.9 = (bf16[512,512]{1,0:T(8,128)(2,1)S(1)}, bf16[512,512]{1,0:T(8,128)(2,1)S(1)}, u32[]{:S(2)}, u32[]{:S(2)}) collective-permute-start(bf16[512,512]{1,0:T(8,128)(2,1)S(1)} %collective-permute-done.3.refs_3_), channel_id=1, source_target_pairs={{0,16},{1,17},{2,18},{3,19},{4,20},{5,21},{6,22},{7,23},{8,24},{9,... | collective-permute-start | bytes 1572872 | tf_op jit(solution)/shard_map/ppermute | solution.py:425
  50.3 16.9 %copy-start.1 = (f32[320,128]{1,0:T(8,128)S(1)}, f32[320,128]{1,0:T(8,128)}, u32[]{:S(2)}) copy-start(f32[320,128]{1,0:T(8,128)} %constant.28.clone.tab_ref) | copy-start | bytes 491524
  50.3 16.9 %copy-start.3 = (s32[512]{0:T(512)S(1)}, s32[512]{0:T(512)}, u32[]{:S(2)}) copy-start(s32[512]{0:T(512)} %pos.5) | copy-start | bytes 6148
  50.3 11.3 %collective-permute-start.12 = (bf16[4,576,128]{2,1,0:T(8,128)(2,1)S(1)}, bf16[4,576,128]{2,1,0:T(8,128)(2,1)S(1)}, u32[]{:S(2)}, u32[]{:S(2)}) collective-permute-start(bf16[4,576,128]{2,1,0:T(8,128)(2,1)S(1)} %get-tuple-element.123), channel_id=1, source_target_pairs={{0,2},{1,3},{2,0},{3,1},{4,6},{5,7},{6,4},{7,5},{8,10},{9,11},{10,... | collective-permute-start | bytes 1769480 | tf_op jit(solution)/shard_map/ppermute | solution.py:425
  50.7 10.1 %collective-permute-start.10 = (bf16[512,512]{1,0:T(8,128)(2,1)S(1)}, bf16[512,512]{1,0:T(8,128)(2,1)S(1)}, u32[]{:S(2)}, u32[]{:S(2)}) collective-permute-start(bf16[512,512]{1,0:T(8,128)(2,1)S(1)} %collective-permute-done.8.refs_2_), channel_id=1, source_target_pairs={{0,4},{1,5},{2,6},{3,7},{4,12},{5,13},{6,14},{7,15},{8,0},{9,1},{1... | collective-permute-start | bytes 1572872 | tf_op jit(solution)/shard_map/ppermute | solution.py:425
  52.2 9.2 %collective-permute-start.11 = (bf16[512,512]{1,0:T(8,128)(2,1)S(1)}, bf16[512,512]{1,0:T(8,128)(2,1)S(1)}, u32[]{:S(2)}, u32[]{:S(2)}) collective-permute-start(bf16[512,512]{1,0:T(8,128)(2,1)S(1)} %collective-permute-done.7.refs_3_), channel_id=1, source_target_pairs={{0,16},{1,17},{2,18},{3,19},{4,20},{5,21},{6,22},{7,23},{8,24},{9,... | collective-permute-start | bytes 1572872 | tf_op jit(solution)/shard_map/ppermute | solution.py:425
  61.6 5.7 %collective-permute-start.13 = (f32[512,1024]{1,0:T(8,128)S(1)}, f32[512,1024]{1,0:T(8,128)S(1)}, u32[]{:S(2)}, u32[]{:S(2)}) collective-permute-start(f32[512,1024]{1,0:T(8,128)S(1)} %get-tuple-element.137), channel_id=1, source_target_pairs={{0,1},{1,0},{2,3},{3,2},{4,5},{5,4},{6,7},{7,6},{8,9},{9,8},{10,11... | collective-permute-start | bytes 6291464 | tf_op jit(solution)/shard_map/ppermute | solution.py:425
  61.6 4.9 %collective-permute-start.14 = (bf16[512,512]{1,0:T(8,128)(2,1)S(1)}, bf16[512,512]{1,0:T(8,128)(2,1)S(1)}, u32[]{:S(2)}, u32[]{:S(2)}) collective-permute-start(bf16[512,512]{1,0:T(8,128)(2,1)S(1)} %collective-permute-done.10.y3), channel_id=1, source_target_pairs={{0,1},{1,0},{2,3},{3,2},{4,5},{5,4},{6,7},{7,6},{8,9},{9,8},{10,11... | collective-permute-start | bytes 1572872 | tf_op jit(solution)/shard_map/ppermute | solution.py:425
  62.1 5.1 %collective-permute-start.15 = (bf16[512,512]{1,0:T(8,128)(2,1)S(1)}, bf16[512,512]{1,0:T(8,128)(2,1)S(1)}, u32[]{:S(2)}, u32[]{:S(2)}) collective-permute-start(bf16[512,512]{1,0:T(8,128)(2,1)S(1)} %collective-permute-done.11.a3), channel_id=1, source_target_pairs={{0,1},{1,0},{2,3},{3,2},{4,5},{5,4},{6,7},{7,6},{8,9},{9,8},{10,11... | collective-permute-start | bytes 1572872 | tf_op jit(solution)/shard_map/ppermute | solution.py:425
  62.1 14.7 %collective-permute-start.18 = (bf16[512,512]{1,0:T(8,128)(2,1)S(1)}, bf16[512,512]{1,0:T(8,128)(2,1)S(1)}, u32[]{:S(2)}, u32[]{:S(2)}) collective-permute-start(bf16[512,512]{1,0:T(8,128)(2,1)S(1)} %collective-permute-done.4.refs_2_), channel_id=1, source_target_pairs={{0,16},{1,17},{2,18},{3,19},{4,20},{5,21},{6,22},{7,23},{8,24},{9,... | collective-permute-start | bytes 1572872 | tf_op jit(solution)/shard_map/ppermute | solution.py:425
  63.6 14.8 %collective-permute-start.19 = (bf16[512,512]{1,0:T(8,128)(2,1)S(1)}, bf16[512,512]{1,0:T(8,128)(2,1)S(1)}, u32[]{:S(2)}, u32[]{:S(2)}) collective-permute-start(bf16[512,512]{1,0:T(8,128)(2,1)S(1)} %collective-permute-done.9.refs_4_), channel_id=1, source_target_pairs={{0,2},{1,3},{2,0},{3,1},{4,6},{5,7},{6,4},{7,5},{8,10},{9,11},{10,... | collective-permute-start | bytes 1572872 | tf_op jit(solution)/shard_map/ppermute | solution.py:425
  72.0 15.9 %collective-permute-start.16 = (bf16[512,512]{1,0:T(8,128)(2,1)S(1)}, bf16[512,512]{1,0:T(8,128)(2,1)S(1)}, u32[]{:S(2)}, u32[]{:S(2)}) collective-permute-start(bf16[512,512]{1,0:T(8,128)(2,1)S(1)} %collective-permute-done.10.y3), channel_id=1, source_target_pairs={{0,16},{1,17},{2,18},{3,19},{4,20},{5,21},{6,22},{7,23},{8,24},{9,... | collective-permute-start | bytes 1572872 | tf_op jit(solution)/shard_map/ppermute | solution.py:425
  73.6 15.3 %collective-permute-start.17 = (bf16[512,512]{1,0:T(8,128)(2,1)S(1)}, bf16[512,512]{1,0:T(8,128)(2,1)S(1)}, u32[]{:S(2)}, u32[]{:S(2)}) collective-permute-start(bf16[512,512]{1,0:T(8,128)(2,1)S(1)} %get-tuple-element.140), channel_id=1, source_target_pairs={{0,2},{1,3},{2,0},{3,1},{4,6},{5,7},{6,4},{7,5},{8,10},{9,11},{10,... | collective-permute-start | bytes 1572872 | tf_op jit(solution)/shard_map/ppermute | solution.py:425
  74.6 13.4 %collective-permute-start.20 = (bf16[1,576,128]{2,1,0:T(8,128)(2,1)S(1)}, bf16[1,576,128]{2,1,0:T(8,128)(2,1)S(1)}, u32[]{:S(2)}, u32[]{:S(2)}) collective-permute-start(bf16[1,576,128]{2,1,0:T(8,128)(2,1)S(1)} %get-tuple-element.151), channel_id=1, source_target_pairs={{0,8},{1,9},{2,10},{3,11},{4,12},{5,13},{6,14},{7,15},{8,0},{9,1},... | collective-permute-start | bytes 442376 | tf_op jit(solution)/shard_map/ppermute | solution.py:425
  76.8 11.1 %collective-permute-start.21 = (bf16[1,576,128]{2,1,0:T(8,128)(2,1)S(1)}, bf16[1,576,128]{2,1,0:T(8,128)(2,1)S(1)}, u32[]{:S(2)}, u32[]{:S(2)}) collective-permute-start(bf16[1,576,128]{2,1,0:T(8,128)(2,1)S(1)} %get-tuple-element.152), channel_id=1, source_target_pairs={{0,4},{1,5},{2,6},{3,7},{4,0},{5,1},{6,2},{7,3},{8,12},{9,13},{10,... | collective-permute-start | bytes 442376 | tf_op jit(solution)/shard_map/ppermute | solution.py:425
  78.3 9.6 %collective-permute-start.22 = (bf16[1,576,128]{2,1,0:T(8,128)(2,1)S(1)}, bf16[1,576,128]{2,1,0:T(8,128)(2,1)S(1)}, u32[]{:S(2)}, u32[]{:S(2)}) collective-permute-start(bf16[1,576,128]{2,1,0:T(8,128)(2,1)S(1)} %get-tuple-element.153), channel_id=1, source_target_pairs={{0,12},{1,13},{2,14},{3,15},{4,8},{5,9},{6,10},{7,11},{8,4},{9,5},... | collective-permute-start | bytes 442376 | tf_op jit(solution)/shard_map/ppermute | solution.py:425
  89.6 2.4 %collective-permute-start.23 = (bf16[512,512]{1,0:T(8,128)(2,1)S(1)}, bf16[512,512]{1,0:T(8,128)(2,1)S(1)}, u32[]{:S(2)}, u32[]{:S(2)}) collective-permute-start(bf16[512,512]{1,0:T(8,128)(2,1)S(1)} %last_product.3), channel_id=1, source_target_pairs={{0,1},{1,0},{2,3},{3,2},{4,5},{5,4},{6,7},{7,6},{8,9},{9,8},{10,11... | collective-permute-start | bytes 1572872 | tf_op jit(solution)/shard_map/ppermute | solution.py:425
  89.7 2.2 %collective-permute-start.24 = (f32[1,576,128]{2,1,0:T(8,128)S(1)}, f32[1,576,128]{2,1,0:T(8,128)S(1)}, u32[]{:S(2)}, u32[]{:S(2)}) collective-permute-start(f32[1,576,128]{2,1,0:T(8,128)S(1)} %share.1), channel_id=1, source_target_pairs={{0,1},{1,0},{2,3},{3,2},{4,5},{5,4},{6,7},{7,6},{8,9},{9,8},{10,11... | collective-permute-start | bytes 884744 | tf_op jit(solution)/shard_map/ppermute | solution.py:425

commit v6 on v5

--- a/solution.py
+++ b/solution.py
@@ -508,7 +508,7 @@
         ((frozen_weight, 10), (y0, 14), (z1, 11)), (), adapters=(low, second_adapter_weight)
     )
     totals = held_sum, crossed_sum, held_sib, crossed_sib
-    z2, y1, a1, other, *totals = fence(z2, y1, a1, other, *totals)
+    z2, other, *totals = fence(z2, other, *totals)
 
     z3 = send(z2, to_z)
     y2 = send(z2, to_y)

time: 94.2 us -> 94 us (level)
  transfers between devices with their start and end apart: 25 -> 25, of which waited for: 17 -> 15; matrix products, arithmetic and copies ran while one was open for 1% -> 1% of each run, Pallas kernels for 39% -> 39%
where the time goes in v6:
time: 94 us; the launch traced here: 93.6 us
  Pallas kernels  39.2 us (42%)
  starting transfers between devices  28.3 us (30%)
  waiting for transfers between devices  22.2 us (24%)
  local copies, waits for them, and re-layouts  2.3 us (2%)
  between operations  1.61 us (2%)
    pallas_call x14, Pallas kernels, call(): pl.pallas_call(kernel, out_shape=shapes, grid_spec=pltpu.PrefetchScalarGr...  39.2 us
    ppermute x25, starting transfers between devices, fast_body(): send = lambda x, f: lax.ppermute(x, ALL, routes.pairs(f))  28.3 us
    ppermute x25, waiting for transfers between devices, fast_body(): send = lambda x, f: lax.ppermute(x, ALL, routes.pairs(f))  22.2 us
  transfers between devices with their start and end apart: 25, of which 15 were waited for; matrix products, arithmetic and copies ran while one was open for 1% of the time, Pallas kernels for 39%

profile of v6, /device:TPU:0, one launch (start us, length us, event | category | flops | bytes accessed | tf_op | source)
XLA Modules:
  0.0 93.6 jit_solution(455258319240719932)
XLA Ops:
  0.6 1.1 %constant_dynamic-slice_fusion = bf16[512,512]{1,0:T(8,128)(2,1)S(1)} fusion(bf16[512,1024]{1,0:T(8,128)(2,1)} %w_ref.3, s32[]{:T(128)S(6)} %select_n.6), kind=kLoop, calls=%fused_computation.1 | loop fusion | bytes 1048580 | tf_op jit(solution)/shard_map/dynamic_slice | solution.py:465
  2.2 2.6 %collective-permute-start = (bf16[512,512]{1,0:T(8,128)(2,1)S(1)}, bf16[512,512]{1,0:T(8,128)(2,1)S(1)}, u32[]{:S(2)}, u32[]{:S(2)}) collective-permute-start(bf16[512,512]{1,0:T(8,128)(2,1)S(1)} %constant_dynamic-slice_fusion), channel_id=1, source_target_pairs={{0,4},{1,5},{2,6},{3,7},{4,12},{5,13},{6,14},{7,15},{8,0},{9,1},{1... | collective-permute-start | bytes 1572872 | tf_op jit(solution)/shard_map/ppermute | solution.py:425
  4.9 1.5 %collective-permute-start.1 = (bf16[512,512]{1,0:T(8,128)(2,1)S(1)}, bf16[512,512]{1,0:T(8,128)(2,1)S(1)}, u32[]{:S(2)}, u32[]{:S(2)}) collective-permute-start(bf16[512,512]{1,0:T(8,128)(2,1)S(1)} %constant_dynamic-slice_fusion), channel_id=1, source_target_pairs={{0,2},{1,3},{2,0},{3,1},{4,6},{5,7},{6,4},{7,5},{8,10},{9,11},{10,... | collective-permute-start | bytes 1572872 | tf_op jit(solution)/shard_map/ppermute | solution.py:425
  7.1 1.2 %dynamic-slice_bitcast_fusion.sc = s32[18]{0:T(128)} fusion(s32[32,18]{1,0:T(8,128)} %constant.29.clone, s32[]{:T(128)S(6)} %select_n.7), kind=kLoop, calls=%fused_computation | loop fusion | bytes 148 | tf_op jit(solution)/shard_map/squeeze | solution.py:467
  8.3 10.0 %adapter_gradients.1 = (bf16[512,128]{1,0:T(8,128)(2,1)S(1)}, f32[8,576,128]{2,1,0:T(8,128)S(1)}, bf16[8,576,128]{2,1,0:T(8,128)(2,1)S(1)}) custom-call(s32[18]{0:T(128)} %dynamic-slice_bitcast_fusion.sc, s32[4]{0:T(128)} %tids.1, s32[1]{0:T(128)S(6)} %copy.21.count, s32[512]{0:T(512)} %pos.5, bf16[512,8192]{1,0:T(8,128)(2,1)} %tok_ref.9, ...), custom_call_target="tpu_custom_call" | custom-call | flops 1000 | bytes 1024 | tf_op jit(solution)/shard_map/adapter_gradients/pallas_call | solution.py:397
  18.9 2.8 %own_crossed.2 = (f32[512,512]{1,0:T(8,128)S(1)}, f32[512,512]{1,0:T(8,128)S(1)}, bf16[512,512]{1,0:T(8,128)(2,1)S(1)}) custom-call(s32[18]{0:T(128)S(1)} %copy-done.2, bf16[512,8192]{1,0:T(8,128)(2,1)} %tok_ref.9, bf16[512,8192]{1,0:T(8,128)(2,1)} %collective-permute-done.2.sib_ref.refs_1_, bf16[512,1024]{1,0:T(8,128)(2,1)} %w_ref.3, ...), custom_call_target="tpu_custom_call" | custom-call | flops 1000 | bytes 1024 | tf_op jit(solution)/shard_map/own_crossed/pallas_call | solution.py:397
  21.7 2.6 %collective-permute-start.3 = (bf16[512,512]{1,0:T(8,128)(2,1)S(1)}, bf16[512,512]{1,0:T(8,128)(2,1)S(1)}, u32[]{:S(2)}, u32[]{:S(2)}) collective-permute-start(bf16[512,512]{1,0:T(8,128)(2,1)S(1)} %collective-permute-done.refs_4_), channel_id=1, source_target_pairs={{0,4},{1,5},{2,6},{3,7},{4,12},{5,13},{6,14},{7,15},{8,0},{9,1},{1... | collective-permute-start | bytes 1572872 | tf_op jit(solution)/shard_map/ppermute | solution.py:425
  24.3 1.5 %collective-permute-start.8 = (bf16[512,512]{1,0:T(8,128)(2,1)S(1)}, bf16[512,512]{1,0:T(8,128)(2,1)S(1)}, u32[]{:S(2)}, u32[]{:S(2)}) collective-permute-start(bf16[512,512]{1,0:T(8,128)(2,1)S(1)} %collective-permute-done.refs_4_), channel_id=1, source_target_pairs={{0,2},{1,3},{2,0},{3,1},{4,6},{5,7},{6,4},{7,5},{8,10},{9,11},{10,... | collective-permute-start | bytes 1572872 | tf_op jit(solution)/shard_map/ppermute | solution.py:425
  25.9 1.5 %collective-permute-start.9 = (bf16[512,512]{1,0:T(8,128)(2,1)S(1)}, bf16[512,512]{1,0:T(8,128)(2,1)S(1)}, u32[]{:S(2)}, u32[]{:S(2)}) collective-permute-start(bf16[512,512]{1,0:T(8,128)(2,1)S(1)} %collective-permute-done.refs_4_), channel_id=1, source_target_pairs={{0,16},{1,17},{2,18},{3,19},{4,20},{5,21},{6,22},{7,23},{8,24},{9,... | collective-permute-start | bytes 1572872 | tf_op jit(solution)/shard_map/ppermute | solution.py:425
  27.4 4.5 %products.3 = (f32[512,512]{1,0:T(8,128)S(1)}, f32[512,512]{1,0:T(8,128)S(1)}) custom-call(s32[18]{0:T(128)S(1)} %copy-done.2, bf16[512,8192]{1,0:T(8,128)(2,1)} %tok_ref.9, bf16[512,8192]{1,0:T(8,128)(2,1)} %collective-permute-done.2.sib_ref.refs_1_, bf16[512,1024]{1,0:T(8,128)(2,1)} %w_ref.3, bf16[512,512]{1,0:T(8,128)(2,1)S(1)} %collective-permute-done.1.refs_3_, ...), custom_call_target="tpu_custom_call" | custom-call | flops 1000 | bytes 1024 | tf_op jit(solution)/shard_map/products/pallas_call | solution.py:397
  32.4 2.3 %collective-permute-done.3.refs_3_ = bf16[512,512]{1,0:T(8,128)(2,1)S(1)} collective-permute-done((bf16[512,512]{1,0:T(8,128)(2,1)S(1)}, bf16[512,512]{1,0:T(8,128)(2,1)S(1)}, u32[]{:S(2)}, u32[]{:S(2)}) %collective-permute-start.3) | collective-permute-done | bytes 524320 | tf_op jit(solution)/shard_map/ppermute | solution.py:425
  34.8 1.7 %collective-permute-start.5 = (bf16[512,512]{1,0:T(8,128)(2,1)S(1)}, bf16[512,512]{1,0:T(8,128)(2,1)S(1)}, u32[]{:S(2)}, u32[]{:S(2)}) collective-permute-start(bf16[512,512]{1,0:T(8,128)(2,1)S(1)} %collective-permute-done.3.refs_3_), channel_id=1, source_target_pairs={{0,4},{1,5},{2,6},{3,7},{4,12},{5,13},{6,14},{7,15},{8,0},{9,1},{1... | collective-permute-start | bytes 1572872 | tf_op jit(solution)/shard_map/ppermute | solution.py:425
  36.4 1.5 %collective-permute-start.6 = (bf16[512,512]{1,0:T(8,128)(2,1)S(1)}, bf16[512,512]{1,0:T(8,128)(2,1)S(1)}, u32[]{:S(2)}, u32[]{:S(2)}) collective-permute-start(bf16[512,512]{1,0:T(8,128)(2,1)S(1)} %collective-permute-done.3.refs_3_), channel_id=1, source_target_pairs={{0,2},{1,3},{2,0},{3,1},{4,6},{5,7},{6,4},{7,5},{8,10},{9,11},{10,... | collective-permute-start | bytes 1572872 | tf_op jit(solution)/shard_map/ppermute | solution.py:425
  38.0 1.5 %collective-permute-start.7 = (bf16[512,512]{1,0:T(8,128)(2,1)S(1)}, bf16[512,512]{1,0:T(8,128)(2,1)S(1)}, u32[]{:S(2)}, u32[]{:S(2)}) collective-permute-start(bf16[512,512]{1,0:T(8,128)(2,1)S(1)} %collective-permute-done.3.refs_3_), channel_id=1, source_target_pairs={{0,16},{1,17},{2,18},{3,19},{4,20},{5,21},{6,22},{7,23},{8,24},{9,... | collective-permute-start | bytes 1572872 | tf_op jit(solution)/shard_map/ppermute | solution.py:425
  39.7 4.6 %products.4 = (f32[512,512]{1,0:T(8,128)S(1)}, f32[512,512]{1,0:T(8,128)S(1)}, f32[512,512]{1,0:T(8,128)S(1)}, f32[512,512]{1,0:T(8,128)S(1)}) custom-call(s32[18]{0:T(128)S(1)} %copy-done.2, bf16[512,8192]{1,0:T(8,128)(2,1)} %tok_ref.9, bf16[512,8192]{1,0:T(8,128)(2,1)} %collective-permute-done.2.sib_ref.refs_1_, ...), custom_call_target="tpu_custom_call" | custom-call | flops 1000 | bytes 1024 | tf_op jit(solution)/shard_map/products/pallas_call | solution.py:397
  44.3 2.6 %collective-permute-done.5.refs_3_ = bf16[512,512]{1,0:T(8,128)(2,1)S(1)} collective-permute-done((bf16[512,512]{1,0:T(8,128)(2,1)S(1)}, bf16[512,512]{1,0:T(8,128)(2,1)S(1)}, u32[]{:S(2)}, u32[]{:S(2)}) %collective-permute-start.5) | collective-permute-done | bytes 524320 | tf_op jit(solution)/shard_map/ppermute | solution.py:425
  47.6 1.1 %collective-permute-done.7.refs_4_ = bf16[512,512]{1,0:T(8,128)(2,1)S(1)} collective-permute-done((bf16[512,512]{1,0:T(8,128)(2,1)S(1)}, bf16[512,512]{1,0:T(8,128)(2,1)S(1)}, u32[]{:S(2)}, u32[]{:S(2)}) %collective-permute-start.7) | collective-permute-done | bytes 524320 | tf_op jit(solution)/shard_map/ppermute | solution.py:425
  48.6 1.4 %collective-permute-start.12 = (bf16[4,576,128]{2,1,0:T(8,128)(2,1)S(1)}, bf16[4,576,128]{2,1,0:T(8,128)(2,1)S(1)}, u32[]{:S(2)}, u32[]{:S(2)}) collective-permute-start(bf16[4,576,128]{2,1,0:T(8,128)(2,1)S(1)} %get-tuple-element.119), channel_id=1, source_target_pairs={{0,2},{1,3},{2,0},{3,1},{4,6},{5,7},{6,4},{7,5},{8,10},{9,11},{10,... | collective-permute-start | bytes 1769480 | tf_op jit(solution)/shard_map/ppermute | solution.py:425
  50.1 2.1 %collective-permute-start.10 = (bf16[512,512]{1,0:T(8,128)(2,1)S(1)}, bf16[512,512]{1,0:T(8,128)(2,1)S(1)}, u32[]{:S(2)}, u32[]{:S(2)}) collective-permute-start(bf16[512,512]{1,0:T(8,128)(2,1)S(1)} %collective-permute-done.6.refs_2_), channel_id=1, source_target_pairs={{0,4},{1,5},{2,6},{3,7},{4,12},{5,13},{6,14},{7,15},{8,0},{9,1},{1... | collective-permute-start | bytes 1572872 | tf_op jit(solution)/shard_map/ppermute | solution.py:425
  52.1 1.5 %collective-permute-start.11 = (bf16[512,512]{1,0:T(8,128)(2,1)S(1)}, bf16[512,512]{1,0:T(8,128)(2,1)S(1)}, u32[]{:S(2)}, u32[]{:S(2)}) collective-permute-start(bf16[512,512]{1,0:T(8,128)(2,1)S(1)} %collective-permute-done.5.refs_3_), channel_id=1, source_target_pairs={{0,16},{1,17},{2,18},{3,19},{4,20},{5,21},{6,22},{7,23},{8,24},{9,... | collective-permute-start | bytes 1572872 | tf_op jit(solution)/shard_map/ppermute | solution.py:425
  53.6 4.7 %products.5 = (f32[512,512]{1,0:T(8,128)S(1)}, f32[512,512]{1,0:T(8,128)S(1)}, f32[512,1024]{1,0:T(8,128)S(1)}) custom-call(s32[18]{0:T(128)S(1)} %copy-done.2, bf16[512,8192]{1,0:T(8,128)(2,1)} %tok_ref.9, bf16[512,8192]{1,0:T(8,128)(2,1)} %collective-permute-done.2.sib_ref.refs_1_, bf16[512,512]{1,0:T(8,128)(2,1)S(1)} %collective-permute-done.6.refs_2_, ...), custom_call_target="tpu_custom_call" | custom-call | flops 1000 | bytes 1024 | tf_op jit(solution)/shard_map/products/pallas_call | solution.py:397
  58.3 1.8 %collective-permute-done.10.y3 = bf16[512,512]{1,0:T(8,128)(2,1)S(1)} collective-permute-done((bf16[512,512]{1,0:T(8,128)(2,1)S(1)}, bf16[512,512]{1,0:T(8,128)(2,1)S(1)}, u32[]{:S(2)}, u32[]{:S(2)}) %collective-permute-start.10) | collective-permute-done | bytes 524320 | tf_op jit(solution)/shard_map/ppermute | solution.py:425
  60.1 1.2 %collective-permute-done.11.a3 = bf16[512,512]{1,0:T(8,128)(2,1)S(1)} collective-permute-done((bf16[512,512]{1,0:T(8,128)(2,1)S(1)}, bf16[512,512]{1,0:T(8,128)(2,1)S(1)}, u32[]{:S(2)}, u32[]{:S(2)}) %collective-permute-start.11) | collective-permute-done | bytes 524320 | tf_op jit(solution)/shard_map/ppermute | solution.py:425
  61.8 1.5 %collective-permute-start.18 = (bf16[512,512]{1,0:T(8,128)(2,1)S(1)}, bf16[512,512]{1,0:T(8,128)(2,1)S(1)}, u32[]{:S(2)}, u32[]{:S(2)}) collective-permute-start(bf16[512,512]{1,0:T(8,128)(2,1)S(1)} %collective-permute-done.8.refs_2_), channel_id=1, source_target_pairs={{0,16},{1,17},{2,18},{3,19},{4,20},{5,21},{6,22},{7,23},{8,24},{9,... | collective-permute-start | bytes 1572872 | tf_op jit(solution)/shard_map/ppermute | solution.py:425
  63.9 2.4 %collective-permute-done.14.y3_other = bf16[512,512]{1,0:T(8,128)(2,1)S(1)} collective-permute-done((bf16[512,512]{1,0:T(8,128)(2,1)S(1)}, bf16[512,512]{1,0:T(8,128)(2,1)S(1)}, u32[]{:S(2)}, u32[]{:S(2)}) %collective-permute-start.14) | collective-permute-done | bytes 524320 | tf_op jit(solution)/shard_map/ppermute | solution.py:425
  67.0 4.7 %held_keys.1 = (bf16[512,1024]{1,0:T(8,128)(2,1)}, f32[512,512]{1,0:T(8,128)S(1)}) custom-call(s32[18]{0:T(128)S(1)} %copy-done.2, s32[1]{0:T(128)S(6)} %copy.21.count, s32[512]{0:T(512)S(1)} %copy-done.3, bf16[512,8192]{1,0:T(8,128)(2,1)} %tok_ref.9, f32[512,512]{1,0:T(8,128)S(1)} %get-tuple-element.130.mine_h, f32[512,512]{1,0:T(8,128)S(1)} %get-tuple-element.131.mine_c, ...), custom_call_target="tpu_custom_call" | custom-call | flops 1000 | bytes 1024 | tf_op jit(solution)/shard_map/held_keys/pallas_call | solution.py:397
  71.7 1.6 %collective-permute-start.16 = (bf16[512,512]{1,0:T(8,128)(2,1)S(1)}, bf16[512,512]{1,0:T(8,128)(2,1)S(1)}, u32[]{:S(2)}, u32[]{:S(2)}) collective-permute-start(bf16[512,512]{1,0:T(8,128)(2,1)S(1)} %collective-permute-done.10.y3), channel_id=1, source_target_pairs={{0,16},{1,17},{2,18},{3,19},{4,20},{5,21},{6,22},{7,23},{8,24},{9,... | collective-permute-start | bytes 1572872 | tf_op jit(solution)/shard_map/ppermute | solution.py:425
  74.9 1.7 %collective-permute-done.18.e1 = bf16[512,512]{1,0:T(8,128)(2,1)S(1)} collective-permute-done((bf16[512,512]{1,0:T(8,128)(2,1)S(1)}, bf16[512,512]{1,0:T(8,128)(2,1)S(1)}, u32[]{:S(2)}, u32[]{:S(2)}) %collective-permute-start.18) | collective-permute-done | bytes 524320 | tf_op jit(solution)/shard_map/ppermute | solution.py:425
  78.1 1.3 %collective-permute-start.22 = (bf16[1,576,128]{2,1,0:T(8,128)(2,1)S(1)}, bf16[1,576,128]{2,1,0:T(8,128)(2,1)S(1)}, u32[]{:S(2)}, u32[]{:S(2)}) collective-permute-start(bf16[1,576,128]{2,1,0:T(8,128)(2,1)S(1)} %get-tuple-element.149), channel_id=1, source_target_pairs={{0,12},{1,13},{2,14},{3,15},{4,8},{5,9},{6,10},{7,11},{8,4},{9,5},... | collective-permute-start | bytes 442376 | tf_op jit(solution)/shard_map/ppermute | solution.py:425
  79.4 3.8 %crossed_products.1 = (f32[512,512]{1,0:T(8,128)S(1)}, f32[512,512]{1,0:T(8,128)S(1)}, bf16[2,512,512]{2,1,0:T(8,128)(2,1)S(1)}, bf16[2,512,512]{2,1,0:T(8,128)(2,1)S(1)}) custom-call(s32[18]{0:T(128)S(1)} %copy-done.2, bf16[512,8192]{1,0:T(8,128)(2,1)} %tok_ref.9, bf16[512,8192]{1,0:T(8,128)(2,1)} %collective-permute-done.2.sib_ref.refs_1_, ...), custom_call_target="tpu_custom_call" | custom-call | flops 1000 | bytes 1024 | tf_op jit(solution)/shard_map/crossed_products/pallas_call | solution.py:397
  83.2 4.6 %collective-permute-done.20.refs_0_ = bf16[1,576,128]{2,1,0:T(8,128)(2,1)S(1)} collective-permute-done((bf16[1,576,128]{2,1,0:T(8,128)(2,1)S(1)}, bf16[1,576,128]{2,1,0:T(8,128)(2,1)S(1)}, u32[]{:S(2)}, u32[]{:S(2)}) %collective-permute-start.20) | collective-permute-done | bytes 147488 | tf_op jit(solution)/shard_map/ppermute | solution.py:425
  91.7 1.7 %crossed_keys.1 = (bf16[512,1024]{1,0:T(8,128)(2,1)}, f32[1024,128]{1,0:T(8,128)}, f32[128,128]{1,0:T(8,128)}) custom-call(s32[18]{0:T(128)S(1)} %copy-done.2, s32[1]{0:T(128)S(6)} %copy.21.count, s32[512]{0:T(512)S(1)} %copy-done.3, f32[512,512]{1,0:T(8,128)S(1)} %last_product.2.total_ref, ...), custom_call_target="tpu_custom_call", output_to_operand_aliasing={{0}: (8, {})} | custom-call | flops 1000 | bytes 1024 | tf_op jit(solution)/shard_map/crossed_keys/pallas_call | solution.py:397
  (42 shorter events, 11.4 us)
Async XLA Ops:
  1.7 17.2 %collective-permute-start.2 = (bf16[512,8192]{1,0:T(8,128)(2,1)}, bf16[512,8192]{1,0:T(8,128)(2,1)}, u32[]{:S(2)}, u32[]{:S(2)}) collective-permute-start(bf16[512,8192]{1,0:T(8,128)(2,1)} %tok_ref.9), channel_id=1, source_target_pairs={{0,1},{1,0},{2,3},{3,2},{4,5},{5,4},{6,7},{7,6},{8,9},{9,8},{10,11... | collective-permute-start | bytes 25165832 | tf_op jit(solution)/shard_map/ppermute | solution.py:425
  2.2 16.2 %collective-permute-start = (bf16[512,512]{1,0:T(8,128)(2,1)S(1)}, bf16[512,512]{1,0:T(8,128)(2,1)S(1)}, u32[]{:S(2)}, u32[]{:S(2)}) collective-permute-start(bf16[512,512]{1,0:T(8,128)(2,1)S(1)} %constant_dynamic-slice_fusion), channel_id=1, source_target_pairs={{0,4},{1,5},{2,6},{3,7},{4,12},{5,13},{6,14},{7,15},{8,0},{9,1},{1... | collective-permute-start | bytes 1572872 | tf_op jit(solution)/shard_map/ppermute | solution.py:425
  4.9 14.0 %collective-permute-start.1 = (bf16[512,512]{1,0:T(8,128)(2,1)S(1)}, bf16[512,512]{1,0:T(8,128)(2,1)S(1)}, u32[]{:S(2)}, u32[]{:S(2)}) collective-permute-start(bf16[512,512]{1,0:T(8,128)(2,1)S(1)} %constant_dynamic-slice_fusion), channel_id=1, source_target_pairs={{0,2},{1,3},{2,0},{3,1},{4,6},{5,7},{6,4},{7,5},{8,10},{9,11},{10,... | collective-permute-start | bytes 1572872 | tf_op jit(solution)/shard_map/ppermute | solution.py:425
  8.3 10.6 %copy-start = (bf16[1024,128]{1,0:T(8,128)(2,1)S(1)}, bf16[1024,128]{1,0:T(8,128)(2,1)}, u32[]{:S(2)}) copy-start(bf16[1024,128]{1,0:T(8,128)(2,1)} %second_ref.3) | copy-start | bytes 786436
  8.3 10.6 %copy-start.2 = (s32[18]{0:T(128)S(1)}, s32[18]{0:T(128)}, u32[]{:S(2)}) copy-start(s32[18]{0:T(128)} %dynamic-slice_bitcast_fusion.sc) | copy-start | bytes 220
  18.9 15.9 %collective-permute-start.4 = (bf16[8,576,128]{2,1,0:T(8,128)(2,1)S(1)}, bf16[8,576,128]{2,1,0:T(8,128)(2,1)S(1)}, u32[]{:S(2)}, u32[]{:S(2)}) collective-permute-start(bf16[8,576,128]{2,1,0:T(8,128)(2,1)S(1)} %get-tuple-element.95), channel_id=1, source_target_pairs={{0,1},{1,0},{2,3},{3,2},{4,5},{5,4},{6,7},{7,6},{8,9},{9,8},{10,11... | collective-permute-start | bytes 3538952 | tf_op jit(solution)/shard_map/ppermute | solution.py:425
  21.7 13.1 %collective-permute-start.3 = (bf16[512,512]{1,0:T(8,128)(2,1)S(1)}, bf16[512,512]{1,0:T(8,128)(2,1)S(1)}, u32[]{:S(2)}, u32[]{:S(2)}) collective-permute-start(bf16[512,512]{1,0:T(8,128)(2,1)S(1)} %collective-permute-done.refs_4_), channel_id=1, source_target_pairs={{0,4},{1,5},{2,6},{3,7},{4,12},{5,13},{6,14},{7,15},{8,0},{9,1},{1... | collective-permute-start | bytes 1572872 | tf_op jit(solution)/shard_map/ppermute | solution.py:425
  24.3 15.3 %collective-permute-start.8 = (bf16[512,512]{1,0:T(8,128)(2,1)S(1)}, bf16[512,512]{1,0:T(8,128)(2,1)S(1)}, u32[]{:S(2)}, u32[]{:S(2)}) collective-permute-start(bf16[512,512]{1,0:T(8,128)(2,1)S(1)} %collective-permute-done.refs_4_), channel_id=1, source_target_pairs={{0,2},{1,3},{2,0},{3,1},{4,6},{5,7},{6,4},{7,5},{8,10},{9,11},{10,... | collective-permute-start | bytes 1572872 | tf_op jit(solution)/shard_map/ppermute | solution.py:425
  25.9 13.8 %collective-permute-start.9 = (bf16[512,512]{1,0:T(8,128)(2,1)S(1)}, bf16[512,512]{1,0:T(8,128)(2,1)S(1)}, u32[]{:S(2)}, u32[]{:S(2)}) collective-permute-start(bf16[512,512]{1,0:T(8,128)(2,1)S(1)} %collective-permute-done.refs_4_), channel_id=1, source_target_pairs={{0,16},{1,17},{2,18},{3,19},{4,20},{5,21},{6,22},{7,23},{8,24},{9,... | collective-permute-start | bytes 1572872 | tf_op jit(solution)/shard_map/ppermute | solution.py:425
  34.8 12.2 %collective-permute-start.5 = (bf16[512,512]{1,0:T(8,128)(2,1)S(1)}, bf16[512,512]{1,0:T(8,128)(2,1)S(1)}, u32[]{:S(2)}, u32[]{:S(2)}) collective-permute-start(bf16[512,512]{1,0:T(8,128)(2,1)S(1)} %collective-permute-done.3.refs_3_), channel_id=1, source_target_pairs={{0,4},{1,5},{2,6},{3,7},{4,12},{5,13},{6,14},{7,15},{8,0},{9,1},{1... | collective-permute-start | bytes 1572872 | tf_op jit(solution)/shard_map/ppermute | solution.py:425
  36.4 11.1 %collective-permute-start.6 = (bf16[512,512]{1,0:T(8,128)(2,1)S(1)}, bf16[512,512]{1,0:T(8,128)(2,1)S(1)}, u32[]{:S(2)}, u32[]{:S(2)}) collective-permute-start(bf16[512,512]{1,0:T(8,128)(2,1)S(1)} %collective-permute-done.3.refs_3_), channel_id=1, source_target_pairs={{0,2},{1,3},{2,0},{3,1},{4,6},{5,7},{6,4},{7,5},{8,10},{9,11},{10,... | collective-permute-start | bytes 1572872 | tf_op jit(solution)/shard_map/ppermute | solution.py:425
  38.0 10.7 %collective-permute-start.7 = (bf16[512,512]{1,0:T(8,128)(2,1)S(1)}, bf16[512,512]{1,0:T(8,128)(2,1)S(1)}, u32[]{:S(2)}, u32[]{:S(2)}) collective-permute-start(bf16[512,512]{1,0:T(8,128)(2,1)S(1)} %collective-permute-done.3.refs_3_), channel_id=1, source_target_pairs={{0,16},{1,17},{2,18},{3,19},{4,20},{5,21},{6,22},{7,23},{8,24},{9,... | collective-permute-start | bytes 1572872 | tf_op jit(solution)/shard_map/ppermute | solution.py:425
  48.6 18.3 %copy-start.1 = (f32[320,128]{1,0:T(8,128)S(1)}, f32[320,128]{1,0:T(8,128)}, u32[]{:S(2)}) copy-start(f32[320,128]{1,0:T(8,128)} %constant.28.clone.tab_ref) | copy-start | bytes 491524
  48.6 18.4 %copy-start.3 = (s32[512]{0:T(512)S(1)}, s32[512]{0:T(512)}, u32[]{:S(2)}) copy-start(s32[512]{0:T(512)} %pos.5) | copy-start | bytes 6148
  48.6 12.7 %collective-permute-start.12 = (bf16[4,576,128]{2,1,0:T(8,128)(2,1)S(1)}, bf16[4,576,128]{2,1,0:T(8,128)(2,1)S(1)}, u32[]{:S(2)}, u32[]{:S(2)}) collective-permute-start(bf16[4,576,128]{2,1,0:T(8,128)(2,1)S(1)} %get-tuple-element.119), channel_id=1, source_target_pairs={{0,2},{1,3},{2,0},{3,1},{4,6},{5,7},{6,4},{7,5},{8,10},{9,11},{10,... | collective-permute-start | bytes 1769480 | tf_op jit(solution)/shard_map/ppermute | solution.py:425
  50.1 10.1 %collective-permute-start.10 = (bf16[512,512]{1,0:T(8,128)(2,1)S(1)}, bf16[512,512]{1,0:T(8,128)(2,1)S(1)}, u32[]{:S(2)}, u32[]{:S(2)}) collective-permute-start(bf16[512,512]{1,0:T(8,128)(2,1)S(1)} %collective-permute-done.6.refs_2_), channel_id=1, source_target_pairs={{0,4},{1,5},{2,6},{3,7},{4,12},{5,13},{6,14},{7,15},{8,0},{9,1},{1... | collective-permute-start | bytes 1572872 | tf_op jit(solution)/shard_map/ppermute | solution.py:425
  52.1 9.2 %collective-permute-start.11 = (bf16[512,512]{1,0:T(8,128)(2,1)S(1)}, bf16[512,512]{1,0:T(8,128)(2,1)S(1)}, u32[]{:S(2)}, u32[]{:S(2)}) collective-permute-start(bf16[512,512]{1,0:T(8,128)(2,1)S(1)} %collective-permute-done.5.refs_3_), channel_id=1, source_target_pairs={{0,16},{1,17},{2,18},{3,19},{4,20},{5,21},{6,22},{7,23},{8,24},{9,... | collective-permute-start | bytes 1572872 | tf_op jit(solution)/shard_map/ppermute | solution.py:425
  61.3 5.7 %collective-permute-start.13 = (f32[512,1024]{1,0:T(8,128)S(1)}, f32[512,1024]{1,0:T(8,128)S(1)}, u32[]{:S(2)}, u32[]{:S(2)}) collective-permute-start(f32[512,1024]{1,0:T(8,128)S(1)} %get-tuple-element.133), channel_id=1, source_target_pairs={{0,1},{1,0},{2,3},{3,2},{4,5},{5,4},{6,7},{7,6},{8,9},{9,8},{10,11... | collective-permute-start | bytes 6291464 | tf_op jit(solution)/shard_map/ppermute | solution.py:425
  61.3 4.9 %collective-permute-start.14 = (bf16[512,512]{1,0:T(8,128)(2,1)S(1)}, bf16[512,512]{1,0:T(8,128)(2,1)S(1)}, u32[]{:S(2)}, u32[]{:S(2)}) collective-permute-start(bf16[512,512]{1,0:T(8,128)(2,1)S(1)} %collective-permute-done.10.y3), channel_id=1, source_target_pairs={{0,1},{1,0},{2,3},{3,2},{4,5},{5,4},{6,7},{7,6},{8,9},{9,8},{10,11... | collective-permute-start | bytes 1572872 | tf_op jit(solution)/shard_map/ppermute | solution.py:425
  61.8 5.1 %collective-permute-start.15 = (bf16[512,512]{1,0:T(8,128)(2,1)S(1)}, bf16[512,512]{1,0:T(8,128)(2,1)S(1)}, u32[]{:S(2)}, u32[]{:S(2)}) collective-permute-start(bf16[512,512]{1,0:T(8,128)(2,1)S(1)} %collective-permute-done.11.a3), channel_id=1, source_target_pairs={{0,1},{1,0},{2,3},{3,2},{4,5},{5,4},{6,7},{7,6},{8,9},{9,8},{10,11... | collective-permute-start | bytes 1572872 | tf_op jit(solution)/shard_map/ppermute | solution.py:425
  61.8 14.7 %collective-permute-start.18 = (bf16[512,512]{1,0:T(8,128)(2,1)S(1)}, bf16[512,512]{1,0:T(8,128)(2,1)S(1)}, u32[]{:S(2)}, u32[]{:S(2)}) collective-permute-start(bf16[512,512]{1,0:T(8,128)(2,1)S(1)} %collective-permute-done.8.refs_2_), channel_id=1, source_target_pairs={{0,16},{1,17},{2,18},{3,19},{4,20},{5,21},{6,22},{7,23},{8,24},{9,... | collective-permute-start | bytes 1572872 | tf_op jit(solution)/shard_map/ppermute | solution.py:425
  63.3 14.8 %collective-permute-start.19 = (bf16[512,512]{1,0:T(8,128)(2,1)S(1)}, bf16[512,512]{1,0:T(8,128)(2,1)S(1)}, u32[]{:S(2)}, u32[]{:S(2)}) collective-permute-start(bf16[512,512]{1,0:T(8,128)(2,1)S(1)} %collective-permute-done.7.refs_4_), channel_id=1, source_target_pairs={{0,2},{1,3},{2,0},{3,1},{4,6},{5,7},{6,4},{7,5},{8,10},{9,11},{10,... | collective-permute-start | bytes 1572872 | tf_op jit(solution)/shard_map/ppermute | solution.py:425
  71.7 16.1 %collective-permute-start.16 = (bf16[512,512]{1,0:T(8,128)(2,1)S(1)}, bf16[512,512]{1,0:T(8,128)(2,1)S(1)}, u32[]{:S(2)}, u32[]{:S(2)}) collective-permute-start(bf16[512,512]{1,0:T(8,128)(2,1)S(1)} %collective-permute-done.10.y3), channel_id=1, source_target_pairs={{0,16},{1,17},{2,18},{3,19},{4,20},{5,21},{6,22},{7,23},{8,24},{9,... | collective-permute-start | bytes 1572872 | tf_op jit(solution)/shard_map/ppermute | solution.py:425
  73.3 15.4 %collective-permute-start.17 = (bf16[512,512]{1,0:T(8,128)(2,1)S(1)}, bf16[512,512]{1,0:T(8,128)(2,1)S(1)}, u32[]{:S(2)}, u32[]{:S(2)}) collective-permute-start(bf16[512,512]{1,0:T(8,128)(2,1)S(1)} %get-tuple-element.136), channel_id=1, source_target_pairs={{0,2},{1,3},{2,0},{3,1},{4,6},{5,7},{6,4},{7,5},{8,10},{9,11},{10,... | collective-permute-start | bytes 1572872 | tf_op jit(solution)/shard_map/ppermute | solution.py:425
  73.9 13.9 %collective-permute-start.20 = (bf16[1,576,128]{2,1,0:T(8,128)(2,1)S(1)}, bf16[1,576,128]{2,1,0:T(8,128)(2,1)S(1)}, u32[]{:S(2)}, u32[]{:S(2)}) collective-permute-start(bf16[1,576,128]{2,1,0:T(8,128)(2,1)S(1)} %get-tuple-element.147), channel_id=1, source_target_pairs={{0,8},{1,9},{2,10},{3,11},{4,12},{5,13},{6,14},{7,15},{8,0},{9,1},... | collective-permute-start | bytes 442376 | tf_op jit(solution)/shard_map/ppermute | solution.py:425
  76.6 11.2 %collective-permute-start.21 = (bf16[1,576,128]{2,1,0:T(8,128)(2,1)S(1)}, bf16[1,576,128]{2,1,0:T(8,128)(2,1)S(1)}, u32[]{:S(2)}, u32[]{:S(2)}) collective-permute-start(bf16[1,576,128]{2,1,0:T(8,128)(2,1)S(1)} %get-tuple-element.148), channel_id=1, source_target_pairs={{0,4},{1,5},{2,6},{3,7},{4,0},{5,1},{6,2},{7,3},{8,12},{9,13},{10,... | collective-permute-start | bytes 442376 | tf_op jit(solution)/shard_map/ppermute | solution.py:425
  78.1 9.7 %collective-permute-start.22 = (bf16[1,576,128]{2,1,0:T(8,128)(2,1)S(1)}, bf16[1,576,128]{2,1,0:T(8,128)(2,1)S(1)}, u32[]{:S(2)}, u32[]{:S(2)}) collective-permute-start(bf16[1,576,128]{2,1,0:T(8,128)(2,1)S(1)} %get-tuple-element.149), channel_id=1, source_target_pairs={{0,12},{1,13},{2,14},{3,15},{4,8},{5,9},{6,10},{7,11},{8,4},{9,5},... | collective-permute-start | bytes 442376 | tf_op jit(solution)/shard_map/ppermute | solution.py:425
  89.3 2.4 %collective-permute-start.23 = (bf16[512,512]{1,0:T(8,128)(2,1)S(1)}, bf16[512,512]{1,0:T(8,128)(2,1)S(1)}, u32[]{:S(2)}, u32[]{:S(2)}) collective-permute-start(bf16[512,512]{1,0:T(8,128)(2,1)S(1)} %last_product.3), channel_id=1, source_target_pairs={{0,1},{1,0},{2,3},{3,2},{4,5},{5,4},{6,7},{7,6},{8,9},{9,8},{10,11... | collective-permute-start | bytes 1572872 | tf_op jit(solution)/shard_map/ppermute | solution.py:425
  89.5 2.2 %collective-permute-start.24 = (f32[1,576,128]{2,1,0:T(8,128)S(1)}, f32[1,576,128]{2,1,0:T(8,128)S(1)}, u32[]{:S(2)}, u32[]{:S(2)}) collective-permute-start(f32[1,576,128]{2,1,0:T(8,128)S(1)} %share.1), channel_id=1, source_target_pairs={{0,1},{1,0},{2,3},{3,2},{4,5},{5,4},{6,7},{7,6},{8,9},{9,8},{10,11... | collective-permute-start | bytes 884744 | tf_op jit(solution)/shard_map/ppermute | solution.py:425
